TPU v7x, 512 devices: a whole 4x4x16 slice. The times are simulated.
512 devices in a mesh: context: 64 (over x, z), head: 8 (over y, core).
Axes of the slice: x: 4, y: 4, z: 16, core: 2. Of those that a mesh axis runs over, the one named last changes fastest.
Arguments:
- query: bfloat16 [32768, 2048], P(('context', 'head')), may hold values from -96 to 96
- key: bfloat16 [32768, 2048], P(('context', 'head')), may hold values from -12 to 12
- value: bfloat16 [32768, 2048], P(('context', 'head')), may hold values from -12 to 12
- cotangent: bfloat16 [32768, 2048], P(('context', 'head')), may hold values from -6 to 6
Outputs:
- attended: bfloat16 [32768, 2048], P('context', 'head')
- query_gradient: bfloat16 [32768, 2048], P('context', 'head')
- grad_key: bfloat16 [32768, 2048], P('context', 'head')
- grad_value: bfloat16 [32768, 2048], P('context', 'head')
All inputs are finite; a program needn't handle non-finite values.
Results may differ from a plain program's by a relative error of at most 0.019.
Values may be sent and summed in bfloat16 or wider, within the bound.
No kernel may reach another device: no remote copies, remote signals or barrier semaphores. Data moves between devices by JAX's collectives and lax.ppermute only.
A program may use at most 64 MiB of HBM per device.

v0:
```python
import math

import jax
import jax.numpy as jnp
from jax import lax
from jax.sharding import PartitionSpec as P

HEAD_DIM = 128
LEAF = 256
RATIO = 16


def padded(block, sides, width):
    for axis, dim in sides:
        count = lax.axis_size(axis)
        forward = [(i, i + 1) for i in range(count - 1)]
        backward = [(target, source) for source, target in forward]
        low = lax.ppermute(
            lax.slice_in_dim(block, block.shape[dim] - width, None, axis=dim), axis, forward
        )
        high = lax.ppermute(lax.slice_in_dim(block, 0, width, axis=dim), axis, backward)
        block = jnp.concatenate([low, block, high], axis=dim)
    return block


def partner(value, axis, bit):
    mask = 2**bit
    pairs = [(source, source ^ mask) for source in range(lax.axis_size(axis))]
    return lax.ppermute(value, axis, pairs)


def product(form, left, right):
    return jnp.einsum(form, left, right, preferred_element_type=jnp.float32)


def windows(framed):
    return jnp.concatenate([framed[:-2], framed[1:-1], framed[2:]], axis=1)


def unfold(window_grad):
    blocks = window_grad.shape[0]
    parts = window_grad.reshape(blocks, 3, LEAF, -1)
    spread = jnp.pad(parts[:, 0], ((0, 2), (0, 0), (0, 0)))
    spread = spread + jnp.pad(parts[:, 1], ((1, 1), (0, 0), (0, 0)))
    spread = spread + jnp.pad(parts[:, 2], ((2, 0), (0, 0), (0, 0)))
    return spread.reshape((blocks + 2) * LEAF, -1)


def attend(queries, key_ext, value_ext, grad_out, coarse_keys, coarse_values, valid):
    tokens, span_width = queries.shape
    heads = span_width // HEAD_DIM
    blocks = tokens // LEAF
    factor = HEAD_DIM ** (-0.5)
    query_four = queries.reshape(blocks, LEAF, heads, HEAD_DIM)
    grad_four = grad_out.reshape(blocks, LEAF, heads, HEAD_DIM)
    key_win = windows(key_ext.reshape(blocks + 2, LEAF, heads, HEAD_DIM))
    value_win = windows(value_ext.reshape(blocks + 2, LEAF, heads, HEAD_DIM))
    allowed = windows(valid.reshape(blocks + 2, LEAF))
    coarse_k = coarse_keys.reshape(-1, heads, HEAD_DIM)
    coarse_v = coarse_values.reshape(-1, heads, HEAD_DIM)
    near = product("bqhd,bkhd->bhqk", query_four, key_win) * factor
    near = jnp.where(allowed[:, None, None, :], near, -1e30)
    far = product("bqhd,khd->bhqk", query_four, coarse_k) * factor + math.log(RATIO)
    top = jnp.maximum(jnp.max(near, axis=-1), jnp.max(far, axis=-1))
    near_exp = jnp.exp(near - top[..., None])
    far_exp = jnp.exp(far - top[..., None])
    total = jnp.sum(near_exp, axis=-1) + jnp.sum(far_exp, axis=-1)
    near_prob = near_exp / total[..., None]
    far_prob = far_exp / total[..., None]
    near_low = near_prob.astype(jnp.bfloat16)
    far_low = far_prob.astype(jnp.bfloat16)
    mixed_output = product("bhqk,bkhd->bqhd", near_low, value_win) + product(
        "bhqk,khd->bqhd", far_low, coarse_v
    )
    delta = jnp.transpose(jnp.sum(grad_four.astype(jnp.float32) * mixed_output, axis=-1), (0, 2, 1))
    near_dprob = product("bqhd,bkhd->bhqk", grad_four, value_win)
    far_dprob = product("bqhd,khd->bhqk", grad_four, coarse_v)
    near_dscore = (near_prob * (near_dprob - delta[..., None])).astype(jnp.bfloat16)
    far_dscore = (far_prob * (far_dprob - delta[..., None])).astype(jnp.bfloat16)
    query_gradient = (
        product("bhqk,bkhd->bqhd", near_dscore, key_win)
        + product("bhqk,khd->bqhd", far_dscore, coarse_k)
    ) * factor
    key_grad_win = product("bhqk,bqhd->bkhd", near_dscore, query_four) * factor
    value_grad_win = product("bhqk,bqhd->bkhd", near_low, grad_four)
    coarse_kgrad = product("bhqk,bqhd->khd", far_dscore, query_four) * factor
    coarse_vgrad = product("bhqk,bqhd->khd", far_low, grad_four)
    return (
        mixed_output.astype(jnp.bfloat16).reshape(tokens, span_width),
        query_gradient.reshape(tokens, span_width),
        unfold(key_grad_win),
        unfold(value_grad_win),
        coarse_kgrad.reshape(-1, span_width),
        coarse_vgrad.reshape(-1, span_width),
        (top, total, delta),
    )


def body(query, key, value, cotangent):
    packed = jnp.stack([query, key, value, cotangent])
    local = lax.all_to_all(packed, "head", split_axis=2, concat_axis=1, tiled=True)
    queries = local[0]
    keys_local = local[1]
    values_local = local[2]
    grad_out = local[3]
    tokens, span_width = queries.shape
    group_summary = tokens // RATIO
    position = lax.axis_index("context")
    devices = lax.axis_size("context")
    levels = devices.bit_length() - 1
    spots = position * tokens - LEAF + jnp.arange(tokens + 2 * LEAF, dtype=jnp.int32)
    valid = (spots >= 0) & (spots < devices * tokens)
    edges = local[1:3]
    edge_rows = jnp.concatenate([edges[:, :LEAF], edges[:, tokens - LEAF :]], axis=1)
    kv_rim = padded(edge_rows, (("context", 1),), LEAF)
    key_ext = jnp.concatenate([kv_rim[0, :LEAF], keys_local, kv_rim[0, 3 * LEAF :]], axis=0)
    value_ext = jnp.concatenate([kv_rim[1, :LEAF], values_local, kv_rim[1, 3 * LEAF :]], axis=0)
    pair = jnp.stack([keys_local, values_local])
    own_summary = (
        jnp.sum(pair.reshape(2, group_summary, RATIO, span_width), axis=2, dtype=jnp.float32)
        / RATIO
    )
    sibling_list = []
    for tree_level_index in range(levels):
        other = partner(own_summary, "context", tree_level_index)
        sibling_list.append(other)
        if tree_level_index + 1 < levels:
            upper = position // (1 << tree_level_index) % 2 == 1
            first_half = jnp.where(upper, other, own_summary)
            second_half = jnp.where(upper, own_summary, other)
            joined = jnp.concatenate([first_half, second_half], axis=1)
            own_summary = jnp.sum(joined.reshape(2, group_summary, 2, span_width), axis=2) * 0.5
    coarse = jnp.concatenate(sibling_list, axis=1).astype(jnp.bfloat16)
    result = attend(queries, key_ext, value_ext, grad_out, coarse[0], coarse[1], valid)
    (
        mixed_output,
        query_gradient,
        key_ext_grad,
        value_ext_grad,
        coarse_kgrad,
        coarse_vgrad,
        row_stats,
    ) = result
    ext_grads = jnp.stack([key_ext_grad, value_ext_grad])
    grads = ext_grads[:, LEAF : LEAF + tokens]
    edge_grads = jnp.concatenate([ext_grads[:, :LEAF], ext_grads[:, tokens + LEAF :]], axis=1)
    back = padded(edge_grads, (("context", 1),), LEAF)
    from_prev = back[:, :LEAF]
    from_next = back[:, 3 * LEAF :]
    grads = grads + jnp.pad(from_prev, ((0, 0), (0, tokens - LEAF), (0, 0)))
    grads = grads + jnp.pad(from_next, ((0, 0), (tokens - LEAF, 0), (0, 0)))
    coarse_grads = jnp.stack([coarse_kgrad, coarse_vgrad]).reshape(
        2, levels, group_summary, span_width
    )
    returned = [
        partner(coarse_grads[:, tree_level_index], "context", tree_level_index)
        for tree_level_index in range(levels)
    ]
    group_totals = []
    for tree_level_index in range(levels):
        running = returned[tree_level_index]
        for bit_index in range(tree_level_index):
            running = running + partner(running.astype(jnp.bfloat16), "context", bit_index).astype(
                running.dtype
            )
        group_totals.append(running)
    spread = jnp.zeros((2, group_summary, span_width), jnp.float32)
    for tree_level_index in range(levels):
        span = 1 << tree_level_index
        row_count = group_summary // span
        offset = position % span * row_count
        piece = lax.dynamic_slice_in_dim(group_totals[tree_level_index], offset, row_count, 1)
        spread = spread + jnp.repeat(piece, span, axis=1) / span
    grads = (
        grads.reshape(2, group_summary, RATIO, span_width) + spread[:, :, None, :] / RATIO
    ).reshape(2, tokens, span_width)
    return (
        mixed_output,
        query_gradient.astype(jnp.bfloat16),
        grads[0].astype(jnp.bfloat16),
        grads[1].astype(jnp.bfloat16),
    )


def solution(mesh):
    in_specs = (
        P(("context", "head"), None),
        P(("context", "head"), None),
        P(("context", "head"), None),
        P(("context", "head"), None),
    )
    out_specs = (
        P("context", "head"),
        P("context", "head"),
        P("context", "head"),
        P("context", "head"),
    )
    return jax.shard_map(body, mesh=mesh, in_specs=in_specs, out_specs=out_specs, check_vma=False)
```

profile of v0, /device:TPU:2, one launch (start us, length us, event | category | flops | bytes accessed | tf_op | source)
XLA Modules:
  0.0 261.1 jit_solution(11258896146131328894)
XLA Ops:
  3.4 2.7 %reshape.132 = bf16[8,2,32768]{2,1,0:T(2,128)(2,1)} reshape(bf16[2048,4,64]{2,1,0:T(4,128)(2,1)S(1)} %bitcast.156) | data formatting | bytes 2097152
  6.0 4.5 %all-to-all-start = ((bf16[8,2,32768]{2,1,0:T(2,128)(2,1)}), bf16[8,2,32768]{2,1,0:T(2,128)(2,1)S(1)}, u32[]{:S(2)}, u32[]{:S(2)}) async-start(bf16[8,2,32768]{2,1,0:T(2,128)(2,1)} %reshape.132), calls=%async_computation | async-start | bytes 2097152 | tf_op jit(solution)/shard_map/all_to_all | solution.py:101
  10.5 15.9 %all-to-all-done = bf16[8,2,32768]{2,1,0:T(2,128)(2,1)S(1)} async-done(((bf16[8,2,32768]{2,1,0:T(2,128)(2,1)}), bf16[8,2,32768]{2,1,0:T(2,128)(2,1)S(1)}, u32[]{:S(2)}, u32[]{:S(2)}) %all-to-all-start) | async-done | bytes 1048608 | tf_op jit(solution)/shard_map/all_to_all | solution.py:101
  29.9 3.8 %collective-permute-start.2 = (f32[2,32,256]{2,1,0:T(8,128)S(1)}, f32[2,32,256]{2,1,0:T(8,128)S(1)}, u32[]{:S(2)}, u32[]{:S(2)}) collective-permute-start(f32[2,32,256]{2,1,0:T(8,128)S(1)} %broadcast_multiply_fusion.5), channel_id=1, source_target_pairs={{0,8},{8,0},{16,24},{24,16},{32,40},{40,32},{48,56},{56,48},{64,72... | collective-permute-start | bytes 196616 | tf_op jit(solution)/shard_map/ppermute | solution.py:29
  36.7 10.5 %collective-permute-start.1 = (bf16[2,256,256]{2,1,0:T(8,128)(2,1)S(1)}, bf16[2,256,256]{2,1,0:T(8,128)(2,1)S(1)}, u32[]{:S(2)}, u32[]{:S(2)}) collective-permute-start(bf16[2,256,256]{2,1,0:T(8,128)(2,1)S(1)} %get-tuple-element.28), channel_id=1, source_target_pairs={{8,0},{16,8},{24,16},{32,24},{40,32},{48,40},{56,48},{64,56},{72,6... | collective-permute-start | bytes 786440 | tf_op jit(solution)/shard_map/ppermute | solution.py:21
  47.2 1.9 collective-permute-start
  49.4 1.9 collective-permute-start.3
  51.3 5.1 %collective-permute-done.3 = f32[2,32,256]{2,1,0:T(8,128)S(1)} collective-permute-done((f32[2,32,256]{2,1,0:T(8,128)S(1)}, f32[2,32,256]{2,1,0:T(8,128)S(1)}, u32[]{:S(2)}, u32[]{:S(2)}) %collective-permute-start.3) | collective-permute-done | bytes 65568 | tf_op jit(solution)/shard_map/ppermute | solution.py:29
  56.8 3.6 %collective-permute-start.4 = (f32[2,32,256]{2,1,0:T(8,128)S(1)}, f32[2,32,256]{2,1,0:T(8,128)S(1)}, u32[]{:S(2)}, u32[]{:S(2)}) collective-permute-start(f32[2,32,256]{2,1,0:T(8,128)S(1)} %broadcast_multiply_fusion.3), channel_id=1, source_target_pairs={{0,32},{8,40},{16,48},{24,56},{32,0},{40,8},{48,16},{56,24},{64,96... | collective-permute-start | bytes 196616 | tf_op jit(solution)/shard_map/ppermute | solution.py:29
  60.4 7.0 %collective-permute-done.4 = f32[2,32,256]{2,1,0:T(8,128)S(1)} collective-permute-done((f32[2,32,256]{2,1,0:T(8,128)S(1)}, f32[2,32,256]{2,1,0:T(8,128)S(1)}, u32[]{:S(2)}, u32[]{:S(2)}) %collective-permute-start.4) | collective-permute-done | bytes 65568 | tf_op jit(solution)/shard_map/ppermute | solution.py:29
  68.2 10.3 %collective-permute-start.5 = (f32[2,32,256]{2,1,0:T(8,128)}, f32[2,32,256]{2,1,0:T(8,128)S(1)}, u32[]{:S(2)}, u32[]{:S(2)}) collective-permute-start(f32[2,32,256]{2,1,0:T(8,128)} %broadcast_multiply_fusion.2), channel_id=1, source_target_pairs={{0,64},{8,72},{16,80},{24,88},{32,96},{40,104},{48,112},{56,120},{... | collective-permute-start | bytes 196616 | tf_op jit(solution)/shard_map/ppermute | solution.py:29
  84.9 1.8 copy.210
  88.4 1.8 copy.208
  92.6 2.4 collective-permute-start.6
  96.5 2.3 collective-permute-done.6
  101.2 4.2 %collective-permute-start.7 = (bf16[2,32,256]{2,1,0:T(8,128)(2,1)S(1)}, bf16[2,32,256]{2,1,0:T(8,128)(2,1)S(1)}, u32[]{:S(2)}, u32[]{:S(2)}) collective-permute-start(bf16[2,32,256]{2,1,0:T(8,128)(2,1)S(1)} %broadcast_multiply_fusion), channel_id=1, source_target_pairs={{0,256},{8,264},{16,272},{24,280},{32,288},{40,296},{48,304},{56,3... | collective-permute-start | bytes 98312 | tf_op jit(solution)/shard_map/ppermute | solution.py:29
  114.4 2.0 multiply_reduce_fusion
  118.8 2.2 multiply_convert_fusion
  121.0 2.2 convolution_bitcast_fusion
  127.3 4.2 %collective-permute-start.16 = (f32[2,32,256]{2,1,0:T(8,128)}, f32[2,32,256]{2,1,0:T(8,128)}, u32[]{:S(2)}, u32[]{:S(2)}) collective-permute-start(f32[2,32,256]{2,1,0:T(8,128)} %get-tuple-element.30), channel_id=1, source_target_pairs={{0,64},{8,72},{16,80},{24,88},{32,96},{40,104},{48,112},{56,120},{... | collective-permute-start | bytes 196616 | tf_op jit(solution)/shard_map/ppermute | solution.py:29
  131.6 4.2 %collective-permute-start.25 = (f32[2,32,256]{2,1,0:T(8,128)}, f32[2,32,256]{2,1,0:T(8,128)S(1)}, u32[]{:S(2)}, u32[]{:S(2)}) collective-permute-start(f32[2,32,256]{2,1,0:T(8,128)} %get-tuple-element.31), channel_id=1, source_target_pairs={{0,256},{8,264},{16,272},{24,280},{32,288},{40,296},{48,304},{56,3... | collective-permute-start | bytes 196616 | tf_op jit(solution)/shard_map/ppermute | solution.py:29
  135.8 3.1 %collective-permute-start.20 = (f32[2,32,256]{2,1,0:T(8,128)}, f32[2,32,256]{2,1,0:T(8,128)S(1)}, u32[]{:S(2)}, u32[]{:S(2)}) collective-permute-start(f32[2,32,256]{2,1,0:T(8,128)} %get-tuple-element.32), channel_id=1, source_target_pairs={{0,128},{8,136},{16,144},{24,152},{32,160},{40,168},{48,176},{56,1... | collective-permute-start | bytes 196616 | tf_op jit(solution)/shard_map/ppermute | solution.py:29
  138.9 3.4 %collective-permute-start.13 = (f32[2,32,256]{2,1,0:T(8,128)}, f32[2,32,256]{2,1,0:T(8,128)}, u32[]{:S(2)}, u32[]{:S(2)}) collective-permute-start(f32[2,32,256]{2,1,0:T(8,128)} %get-tuple-element.33), channel_id=1, source_target_pairs={{0,32},{8,40},{16,48},{24,56},{32,0},{40,8},{48,16},{56,24},{64,96... | collective-permute-start | bytes 196616 | tf_op jit(solution)/shard_map/ppermute | solution.py:29
  142.3 5.5 %collective-permute-start.11 = (f32[2,32,256]{2,1,0:T(8,128)}, f32[2,32,256]{2,1,0:T(8,128)}, u32[]{:S(2)}, u32[]{:S(2)}) collective-permute-start(f32[2,32,256]{2,1,0:T(8,128)} %get-tuple-element.34), channel_id=1, source_target_pairs={{0,16},{8,24},{16,0},{24,8},{32,48},{40,56},{48,32},{56,40},{64,80... | collective-permute-start | bytes 196616 | tf_op jit(solution)/shard_map/ppermute | solution.py:29
  150.0 2.6 copy.241
  153.9 3.6 %copy.245 = f32[2,768,2,128]{3,2,1,0:T(2,128)} copy(f32[2,768,2,128]{1,3,2,0:T(8,128)} %convolution_bitcast_fusion) | data formatting | bytes 3145728 | tf_op jit(solution)/shard_map/bhqk,bqhd->bkhd/transpose | solution.py:33
  157.5 2.5 reshape.122
  162.0 4.1 %collective-permute-start.14 = (bf16[2,32,256]{2,1,0:T(8,128)(2,1)}, bf16[2,32,256]{2,1,0:T(8,128)(2,1)}, u32[]{:S(2)}, u32[]{:S(2)}) collective-permute-start(bf16[2,32,256]{2,1,0:T(8,128)(2,1)} %convert_element_type.150), channel_id=1, source_target_pairs={{0,8},{8,0},{16,24},{24,16},{32,40},{40,32},{48,56},{56,48},{64,72... | collective-permute-start | bytes 98312 | tf_op jit(solution)/shard_map/ppermute | solution.py:29
  168.8 1.9 collective-permute-start.10
  171.5 3.9 %collective-permute-start.8 = (f32[2,256,256]{2,1,0:T(8,128)}, f32[2,256,256]{2,1,0:T(8,128)}, u32[]{:S(2)}, u32[]{:S(2)}) collective-permute-start(f32[2,256,256]{2,1,0:T(8,128)} %get-tuple-element.12), channel_id=1, source_target_pairs={{0,8},{8,16},{16,24},{24,32},{32,40},{40,48},{48,56},{56,64},{64,7... | collective-permute-start | bytes 1572872 | tf_op jit(solution)/shard_map/ppermute | solution.py:18
  175.5 4.0 %collective-permute-start.9 = (f32[2,256,256]{2,1,0:T(8,128)S(1)}, f32[2,256,256]{2,1,0:T(8,128)}, u32[]{:S(2)}, u32[]{:S(2)}) collective-permute-start(f32[2,256,256]{2,1,0:T(8,128)S(1)} %get-tuple-element.13), channel_id=1, source_target_pairs={{8,0},{16,8},{24,16},{32,24},{40,32},{48,40},{56,48},{64,56},{72,6... | collective-permute-start | bytes 1572872 | tf_op jit(solution)/shard_map/ppermute | solution.py:21
  179.6 1.9 collective-permute-start.17
  182.3 3.9 %collective-permute-start.26 = (bf16[2,32,256]{2,1,0:T(8,128)(2,1)S(1)}, bf16[2,32,256]{2,1,0:T(8,128)(2,1)S(1)}, u32[]{:S(2)}, u32[]{:S(2)}) collective-permute-start(bf16[2,32,256]{2,1,0:T(8,128)(2,1)S(1)} %convert_element_type.168), channel_id=1, source_target_pairs={{0,8},{8,0},{16,24},{24,16},{32,40},{40,32},{48,56},{56,48},{64,72... | collective-permute-start | bytes 98312 | tf_op jit(solution)/shard_map/ppermute | solution.py:29
  187.6 1.9 collective-permute-start.21
  190.4 3.9 %collective-permute-start.12 = (bf16[2,32,256]{2,1,0:T(8,128)(2,1)S(1)}, bf16[2,32,256]{2,1,0:T(8,128)(2,1)S(1)}, u32[]{:S(2)}, u32[]{:S(2)}) collective-permute-start(bf16[2,32,256]{2,1,0:T(8,128)(2,1)S(1)} %convert_element_type.148), channel_id=1, source_target_pairs={{0,8},{8,0},{16,24},{24,16},{32,40},{40,32},{48,56},{56,48},{64,72... | collective-permute-start | bytes 98312 | tf_op jit(solution)/shard_map/ppermute | solution.py:29
  194.4 2.1 collective-permute-start.18
  196.5 4.7 %collective-permute-start.27 = (bf16[2,32,256]{2,1,0:T(8,128)(2,1)S(1)}, bf16[2,32,256]{2,1,0:T(8,128)(2,1)S(1)}, u32[]{:S(2)}, u32[]{:S(2)}) collective-permute-start(bf16[2,32,256]{2,1,0:T(8,128)(2,1)S(1)} %fusion.39), channel_id=1, source_target_pairs={{0,16},{8,24},{16,0},{24,8},{32,48},{40,56},{48,32},{56,40},{64,80... | collective-permute-start | bytes 98312 | tf_op jit(solution)/shard_map/ppermute | solution.py:29
  202.0 2.1 collective-permute-start.22
  205.0 4.7 %collective-permute-start.15 = (bf16[2,32,256]{2,1,0:T(8,128)(2,1)S(1)}, bf16[2,32,256]{2,1,0:T(8,128)(2,1)S(1)}, u32[]{:S(2)}, u32[]{:S(2)}) collective-permute-start(bf16[2,32,256]{2,1,0:T(8,128)(2,1)S(1)} %get-tuple-element.10), channel_id=1, source_target_pairs={{0,16},{8,24},{16,0},{24,8},{32,48},{40,56},{48,32},{56,40},{64,80... | collective-permute-start | bytes 98312 | tf_op jit(solution)/shard_map/ppermute | solution.py:29
  209.7 3.9 %collective-permute-start.19 = (bf16[2,32,256]{2,1,0:T(8,128)(2,1)S(1)}, bf16[2,32,256]{2,1,0:T(8,128)(2,1)S(1)}, u32[]{:S(2)}, u32[]{:S(2)}) collective-permute-start(bf16[2,32,256]{2,1,0:T(8,128)(2,1)S(1)} %get-tuple-element.4), channel_id=1, source_target_pairs={{0,32},{8,40},{16,48},{24,56},{32,0},{40,8},{48,16},{56,24},{64,96... | collective-permute-start | bytes 98312 | tf_op jit(solution)/shard_map/ppermute | solution.py:29
  213.6 5.9 %collective-permute-start.28 = (bf16[2,32,256]{2,1,0:T(8,128)(2,1)S(1)}, bf16[2,32,256]{2,1,0:T(8,128)(2,1)S(1)}, u32[]{:S(2)}, u32[]{:S(2)}) collective-permute-start(bf16[2,32,256]{2,1,0:T(8,128)(2,1)S(1)} %fusion.54), channel_id=1, source_target_pairs={{0,32},{8,40},{16,48},{24,56},{32,0},{40,8},{48,16},{56,24},{64,96... | collective-permute-start | bytes 98312 | tf_op jit(solution)/shard_map/ppermute | solution.py:29
  219.5 3.9 %collective-permute-done.28 = bf16[2,32,256]{2,1,0:T(8,128)(2,1)S(1)} collective-permute-done((bf16[2,32,256]{2,1,0:T(8,128)(2,1)S(1)}, bf16[2,32,256]{2,1,0:T(8,128)(2,1)S(1)}, u32[]{:S(2)}, u32[]{:S(2)}) %collective-permute-start.28) | collective-permute-done | bytes 32800 | tf_op jit(solution)/shard_map/ppermute | solution.py:29
  223.5 5.7 %collective-permute-start.23 = (bf16[2,32,256]{2,1,0:T(8,128)(2,1)S(1)}, bf16[2,32,256]{2,1,0:T(8,128)(2,1)S(1)}, u32[]{:S(2)}, u32[]{:S(2)}) collective-permute-start(bf16[2,32,256]{2,1,0:T(8,128)(2,1)S(1)} %fusion.42), channel_id=1, source_target_pairs={{0,32},{8,40},{16,48},{24,56},{32,0},{40,8},{48,16},{56,24},{64,96... | collective-permute-start | bytes 98312 | tf_op jit(solution)/shard_map/ppermute | solution.py:29
  229.2 4.1 %collective-permute-done.23 = bf16[2,32,256]{2,1,0:T(8,128)(2,1)S(1)} collective-permute-done((bf16[2,32,256]{2,1,0:T(8,128)(2,1)S(1)}, bf16[2,32,256]{2,1,0:T(8,128)(2,1)S(1)}, u32[]{:S(2)}, u32[]{:S(2)}) %collective-permute-start.23) | collective-permute-done | bytes 32800 | tf_op jit(solution)/shard_map/ppermute | solution.py:29
  233.3 10.4 %collective-permute-start.29 = (bf16[2,32,256]{2,1,0:T(8,128)(2,1)S(1)}, bf16[2,32,256]{2,1,0:T(8,128)(2,1)S(1)}, u32[]{:S(2)}, u32[]{:S(2)}) collective-permute-start(bf16[2,32,256]{2,1,0:T(8,128)(2,1)S(1)} %fusion.40), channel_id=1, source_target_pairs={{0,64},{8,72},{16,80},{24,88},{32,96},{40,104},{48,112},{56,120},{... | collective-permute-start | bytes 98312 | tf_op jit(solution)/shard_map/ppermute | solution.py:29
  243.7 4.1 %collective-permute-start.24 = (bf16[2,32,256]{2,1,0:T(8,128)(2,1)S(1)}, bf16[2,32,256]{2,1,0:T(8,128)(2,1)S(1)}, u32[]{:S(2)}, u32[]{:S(2)}) collective-permute-start(bf16[2,32,256]{2,1,0:T(8,128)(2,1)S(1)} %get-tuple-element.6), channel_id=1, source_target_pairs={{0,64},{8,72},{16,80},{24,88},{32,96},{40,104},{48,112},{56,120},{... | collective-permute-start | bytes 98312 | tf_op jit(solution)/shard_map/ppermute | solution.py:29
  247.9 2.2 collective-permute-start.30
  250.1 8.5 %collective-permute-done.24 = bf16[2,32,256]{2,1,0:T(8,128)(2,1)S(1)} collective-permute-done((bf16[2,32,256]{2,1,0:T(8,128)(2,1)S(1)}, bf16[2,32,256]{2,1,0:T(8,128)(2,1)S(1)}, u32[]{:S(2)}, u32[]{:S(2)}) %collective-permute-start.24) | collective-permute-done | bytes 32800 | tf_op jit(solution)/shard_map/ppermute | solution.py:29
  (188 shorter events, 56.2 us)
Async XLA Ops:
  6.0 20.4 %all-to-all-start = ((bf16[8,2,32768]{2,1,0:T(2,128)(2,1)}), bf16[8,2,32768]{2,1,0:T(2,128)(2,1)S(1)}, u32[]{:S(2)}, u32[]{:S(2)}) async-start(bf16[8,2,32768]{2,1,0:T(2,128)(2,1)} %reshape.132), calls=%async_computation | async-start | bytes 2097152 | tf_op jit(solution)/shard_map/all_to_all | solution.py:101
  29.9 19.2 %collective-permute-start.2 = (f32[2,32,256]{2,1,0:T(8,128)S(1)}, f32[2,32,256]{2,1,0:T(8,128)S(1)}, u32[]{:S(2)}, u32[]{:S(2)}) collective-permute-start(f32[2,32,256]{2,1,0:T(8,128)S(1)} %broadcast_multiply_fusion.5), channel_id=1, source_target_pairs={{0,8},{8,0},{16,24},{24,16},{32,40},{40,32},{48,56},{56,48},{64,72... | collective-permute-start | bytes 196616 | tf_op jit(solution)/shard_map/ppermute | solution.py:29
  34.0 45.3 %copy-start.3 = (bf16[2,256,2,128]{3,2,1,0:T(2,128)(2,1)}, bf16[2,256,2,128]{3,2,1,0:T(2,128)(2,1)S(1)}, u32[]{:S(2)}) copy-start(bf16[2,256,2,128]{3,2,1,0:T(2,128)(2,1)S(1)} %reshape_squeeze.15) | copy-start | bytes 786436
  36.7 42.6 %collective-permute-start.1 = (bf16[2,256,256]{2,1,0:T(8,128)(2,1)S(1)}, bf16[2,256,256]{2,1,0:T(8,128)(2,1)S(1)}, u32[]{:S(2)}, u32[]{:S(2)}) collective-permute-start(bf16[2,256,256]{2,1,0:T(8,128)(2,1)S(1)} %get-tuple-element.28), channel_id=1, source_target_pairs={{8,0},{16,8},{24,16},{32,24},{40,32},{48,40},{56,48},{64,56},{72,6... | collective-permute-start | bytes 786440 | tf_op jit(solution)/shard_map/ppermute | solution.py:21
  47.2 32.1 %collective-permute-start = (bf16[2,256,256]{2,1,0:T(8,128)(2,1)S(1)}, bf16[2,256,256]{2,1,0:T(8,128)(2,1)S(1)}, u32[]{:S(2)}, u32[]{:S(2)}) collective-permute-start(bf16[2,256,256]{2,1,0:T(8,128)(2,1)S(1)} %get-tuple-element.29), channel_id=1, source_target_pairs={{0,8},{8,16},{16,24},{24,32},{32,40},{40,48},{48,56},{56,64},{64,7... | collective-permute-start | bytes 786440 | tf_op jit(solution)/shard_map/ppermute | solution.py:18
  49.4 7.1 %collective-permute-start.3 = (f32[2,32,256]{2,1,0:T(8,128)S(1)}, f32[2,32,256]{2,1,0:T(8,128)S(1)}, u32[]{:S(2)}, u32[]{:S(2)}) collective-permute-start(f32[2,32,256]{2,1,0:T(8,128)S(1)} %broadcast_multiply_fusion.4), channel_id=1, source_target_pairs={{0,16},{8,24},{16,0},{24,8},{32,48},{40,56},{48,32},{56,40},{64,80... | collective-permute-start | bytes 196616 | tf_op jit(solution)/shard_map/ppermute | solution.py:29
  56.8 10.6 %collective-permute-start.4 = (f32[2,32,256]{2,1,0:T(8,128)S(1)}, f32[2,32,256]{2,1,0:T(8,128)S(1)}, u32[]{:S(2)}, u32[]{:S(2)}) collective-permute-start(f32[2,32,256]{2,1,0:T(8,128)S(1)} %broadcast_multiply_fusion.3), channel_id=1, source_target_pairs={{0,32},{8,40},{16,48},{24,56},{32,0},{40,8},{48,16},{56,24},{64,96... | collective-permute-start | bytes 196616 | tf_op jit(solution)/shard_map/ppermute | solution.py:29
  68.2 22.0 %collective-permute-start.5 = (f32[2,32,256]{2,1,0:T(8,128)}, f32[2,32,256]{2,1,0:T(8,128)S(1)}, u32[]{:S(2)}, u32[]{:S(2)}) collective-permute-start(f32[2,32,256]{2,1,0:T(8,128)} %broadcast_multiply_fusion.2), channel_id=1, source_target_pairs={{0,64},{8,72},{16,80},{24,88},{32,96},{40,104},{48,112},{56,120},{... | collective-permute-start | bytes 196616 | tf_op jit(solution)/shard_map/ppermute | solution.py:29
  78.6 0.7 copy-start.8
  80.5 0.9 copy-start.1
  90.2 0.6 copy-start.14
  92.6 6.2 %collective-permute-start.6 = (f32[2,32,256]{2,1,0:T(8,128)S(1)}, f32[2,32,256]{2,1,0:T(8,128)S(1)}, u32[]{:S(2)}, u32[]{:S(2)}) collective-permute-start(f32[2,32,256]{2,1,0:T(8,128)S(1)} %broadcast_multiply_fusion.1), channel_id=1, source_target_pairs={{0,128},{8,136},{16,144},{24,152},{32,160},{40,168},{48,176},{56,1... | collective-permute-start | bytes 196616 | tf_op jit(solution)/shard_map/ppermute | solution.py:29
  98.8 0.6 copy-start.15
  101.2 7.3 %collective-permute-start.7 = (bf16[2,32,256]{2,1,0:T(8,128)(2,1)S(1)}, bf16[2,32,256]{2,1,0:T(8,128)(2,1)S(1)}, u32[]{:S(2)}, u32[]{:S(2)}) collective-permute-start(bf16[2,32,256]{2,1,0:T(8,128)(2,1)S(1)} %broadcast_multiply_fusion), channel_id=1, source_target_pairs={{0,256},{8,264},{16,272},{24,280},{32,288},{40,296},{48,304},{56,3... | collective-permute-start | bytes 98312 | tf_op jit(solution)/shard_map/ppermute | solution.py:29
  112.3 1.5 copy-start.4
  112.6 1.5 copy-start.7
  112.7 1.7 copy-start.9
  112.7 1.7 copy-start.10
  112.7 1.7 copy-start.12
  112.7 1.7 copy-start.13
  123.2 24.6 %copy-start = (bf16[2,2,256,768]{3,2,1,0:T(8,128)(2,1)S(1)}, bf16[2,2,256,768]{3,2,1,0:T(8,128)(2,1)}, u32[]{:S(2)}) copy-start(bf16[2,2,256,768]{3,2,1,0:T(8,128)(2,1)} %multiply_convert_fusion) | copy-start | bytes 4718596
  123.2 24.6 %copy-start.5 = (bf16[2,256,2,128]{1,3,2,0:T(8,128)(2,1)S(1)}, bf16[2,256,2,128]{1,3,2,0:T(8,128)(2,1)}, u32[]{:S(2)}) copy-start(bf16[2,256,2,128]{1,3,2,0:T(8,128)(2,1)} %copy.240) | copy-start | bytes 786436
  123.3 26.0 %copy-start.2 = (bf16[2,768,2,128]{3,1,2,0:T(8,128)(2,1)S(1)}, bf16[2,768,2,128]{3,1,2,0:T(8,128)(2,1)}, u32[]{:S(2)}) copy-start(bf16[2,768,2,128]{3,1,2,0:T(8,128)(2,1)} %copy-done.1) | copy-start | bytes 2359300
  123.4 26.0 %copy-start.6 = (f32[2,256,2,128]{1,3,2,0:T(8,128)S(1)}, f32[2,256,2,128]{1,3,2,0:T(8,128)}, u32[]{:S(2)}) copy-start(f32[2,256,2,128]{1,3,2,0:T(8,128)} %convolution_bitcast_fusion.2) | copy-start | bytes 1572868
  127.3 41.4 %collective-permute-start.16 = (f32[2,32,256]{2,1,0:T(8,128)}, f32[2,32,256]{2,1,0:T(8,128)}, u32[]{:S(2)}, u32[]{:S(2)}) collective-permute-start(f32[2,32,256]{2,1,0:T(8,128)} %get-tuple-element.30), channel_id=1, source_target_pairs={{0,64},{8,72},{16,80},{24,88},{32,96},{40,104},{48,112},{56,120},{... | collective-permute-start | bytes 196616 | tf_op jit(solution)/shard_map/ppermute | solution.py:29
  131.6 40.0 %collective-permute-start.25 = (f32[2,32,256]{2,1,0:T(8,128)}, f32[2,32,256]{2,1,0:T(8,128)S(1)}, u32[]{:S(2)}, u32[]{:S(2)}) collective-permute-start(f32[2,32,256]{2,1,0:T(8,128)} %get-tuple-element.31), channel_id=1, source_target_pairs={{0,256},{8,264},{16,272},{24,280},{32,288},{40,296},{48,304},{56,3... | collective-permute-start | bytes 196616 | tf_op jit(solution)/shard_map/ppermute | solution.py:29
  135.8 39.7 %collective-permute-start.20 = (f32[2,32,256]{2,1,0:T(8,128)}, f32[2,32,256]{2,1,0:T(8,128)S(1)}, u32[]{:S(2)}, u32[]{:S(2)}) collective-permute-start(f32[2,32,256]{2,1,0:T(8,128)} %get-tuple-element.32), channel_id=1, source_target_pairs={{0,128},{8,136},{16,144},{24,152},{32,160},{40,168},{48,176},{56,1... | collective-permute-start | bytes 196616 | tf_op jit(solution)/shard_map/ppermute | solution.py:29
  138.9 21.6 %collective-permute-start.13 = (f32[2,32,256]{2,1,0:T(8,128)}, f32[2,32,256]{2,1,0:T(8,128)}, u32[]{:S(2)}, u32[]{:S(2)}) collective-permute-start(f32[2,32,256]{2,1,0:T(8,128)} %get-tuple-element.33), channel_id=1, source_target_pairs={{0,32},{8,40},{16,48},{24,56},{32,0},{40,8},{48,16},{56,24},{64,96... | collective-permute-start | bytes 196616 | tf_op jit(solution)/shard_map/ppermute | solution.py:29
  142.3 37.3 %collective-permute-start.11 = (f32[2,32,256]{2,1,0:T(8,128)}, f32[2,32,256]{2,1,0:T(8,128)}, u32[]{:S(2)}, u32[]{:S(2)}) collective-permute-start(f32[2,32,256]{2,1,0:T(8,128)} %get-tuple-element.34), channel_id=1, source_target_pairs={{0,16},{8,24},{16,0},{24,8},{32,48},{40,56},{48,32},{56,40},{64,80... | collective-permute-start | bytes 196616 | tf_op jit(solution)/shard_map/ppermute | solution.py:29
  160.4 6.5 %copy-start.11 = (bf16[2,256,2,128]{1,3,2,0:T(8,128)(2,1)S(1)}, bf16[2,256,2,128]{1,3,2,0:T(8,128)(2,1)}, u32[]{:S(2)}) copy-start(bf16[2,256,2,128]{1,3,2,0:T(8,128)(2,1)} %get-tuple-element.27) | copy-start | bytes 786436
  162.0 20.3 %collective-permute-start.14 = (bf16[2,32,256]{2,1,0:T(8,128)(2,1)}, bf16[2,32,256]{2,1,0:T(8,128)(2,1)}, u32[]{:S(2)}, u32[]{:S(2)}) collective-permute-start(bf16[2,32,256]{2,1,0:T(8,128)(2,1)} %convert_element_type.150), channel_id=1, source_target_pairs={{0,8},{8,0},{16,24},{24,16},{32,40},{40,32},{48,56},{56,48},{64,72... | collective-permute-start | bytes 98312 | tf_op jit(solution)/shard_map/ppermute | solution.py:29
  168.8 89.9 %collective-permute-start.10 = (f32[2,32,256]{2,1,0:T(8,128)}, f32[2,32,256]{2,1,0:T(8,128)S(1)}, u32[]{:S(2)}, u32[]{:S(2)}) collective-permute-start(f32[2,32,256]{2,1,0:T(8,128)} %get-tuple-element.35), channel_id=1, source_target_pairs={{0,8},{8,0},{16,24},{24,16},{32,40},{40,32},{48,56},{56,48},{64,72... | collective-permute-start | bytes 196616 | tf_op jit(solution)/shard_map/ppermute | solution.py:29
  171.5 87.2 %collective-permute-start.8 = (f32[2,256,256]{2,1,0:T(8,128)}, f32[2,256,256]{2,1,0:T(8,128)}, u32[]{:S(2)}, u32[]{:S(2)}) collective-permute-start(f32[2,256,256]{2,1,0:T(8,128)} %get-tuple-element.12), channel_id=1, source_target_pairs={{0,8},{8,16},{16,24},{24,32},{32,40},{40,48},{48,56},{56,64},{64,7... | collective-permute-start | bytes 1572872 | tf_op jit(solution)/shard_map/ppermute | solution.py:18
  175.5 83.2 %collective-permute-start.9 = (f32[2,256,256]{2,1,0:T(8,128)S(1)}, f32[2,256,256]{2,1,0:T(8,128)}, u32[]{:S(2)}, u32[]{:S(2)}) collective-permute-start(f32[2,256,256]{2,1,0:T(8,128)S(1)} %get-tuple-element.13), channel_id=1, source_target_pairs={{8,0},{16,8},{24,16},{32,24},{40,32},{48,40},{56,48},{64,56},{72,6... | collective-permute-start | bytes 1572872 | tf_op jit(solution)/shard_map/ppermute | solution.py:21
  179.6 8.1 %collective-permute-start.17 = (bf16[2,32,256]{2,1,0:T(8,128)(2,1)S(1)}, bf16[2,32,256]{2,1,0:T(8,128)(2,1)S(1)}, u32[]{:S(2)}, u32[]{:S(2)}) collective-permute-start(bf16[2,32,256]{2,1,0:T(8,128)(2,1)S(1)} %convert_element_type.154), channel_id=1, source_target_pairs={{0,8},{8,0},{16,24},{24,16},{32,40},{40,32},{48,56},{56,48},{64,72... | collective-permute-start | bytes 98312 | tf_op jit(solution)/shard_map/ppermute | solution.py:29
  182.3 8.1 %collective-permute-start.26 = (bf16[2,32,256]{2,1,0:T(8,128)(2,1)S(1)}, bf16[2,32,256]{2,1,0:T(8,128)(2,1)S(1)}, u32[]{:S(2)}, u32[]{:S(2)}) collective-permute-start(bf16[2,32,256]{2,1,0:T(8,128)(2,1)S(1)} %convert_element_type.168), channel_id=1, source_target_pairs={{0,8},{8,0},{16,24},{24,16},{32,40},{40,32},{48,56},{56,48},{64,72... | collective-permute-start | bytes 98312 | tf_op jit(solution)/shard_map/ppermute | solution.py:29
  187.6 6.7 %collective-permute-start.21 = (bf16[2,32,256]{2,1,0:T(8,128)(2,1)S(1)}, bf16[2,32,256]{2,1,0:T(8,128)(2,1)S(1)}, u32[]{:S(2)}, u32[]{:S(2)}) collective-permute-start(bf16[2,32,256]{2,1,0:T(8,128)(2,1)S(1)} %convert_element_type.160), channel_id=1, source_target_pairs={{0,8},{8,0},{16,24},{24,16},{32,40},{40,32},{48,56},{56,48},{64,72... | collective-permute-start | bytes 98312 | tf_op jit(solution)/shard_map/ppermute | solution.py:29
  190.4 6.1 %collective-permute-start.12 = (bf16[2,32,256]{2,1,0:T(8,128)(2,1)S(1)}, bf16[2,32,256]{2,1,0:T(8,128)(2,1)S(1)}, u32[]{:S(2)}, u32[]{:S(2)}) collective-permute-start(bf16[2,32,256]{2,1,0:T(8,128)(2,1)S(1)} %convert_element_type.148), channel_id=1, source_target_pairs={{0,8},{8,0},{16,24},{24,16},{32,40},{40,32},{48,56},{56,48},{64,72... | collective-permute-start | bytes 98312 | tf_op jit(solution)/shard_map/ppermute | solution.py:29
  194.4 7.6 %collective-permute-start.18 = (bf16[2,32,256]{2,1,0:T(8,128)(2,1)S(1)}, bf16[2,32,256]{2,1,0:T(8,128)(2,1)S(1)}, u32[]{:S(2)}, u32[]{:S(2)}) collective-permute-start(bf16[2,32,256]{2,1,0:T(8,128)(2,1)S(1)} %fusion.37), channel_id=1, source_target_pairs={{0,16},{8,24},{16,0},{24,8},{32,48},{40,56},{48,32},{56,40},{64,80... | collective-permute-start | bytes 98312 | tf_op jit(solution)/shard_map/ppermute | solution.py:29
  196.5 8.5 %collective-permute-start.27 = (bf16[2,32,256]{2,1,0:T(8,128)(2,1)S(1)}, bf16[2,32,256]{2,1,0:T(8,128)(2,1)S(1)}, u32[]{:S(2)}, u32[]{:S(2)}) collective-permute-start(bf16[2,32,256]{2,1,0:T(8,128)(2,1)S(1)} %fusion.39), channel_id=1, source_target_pairs={{0,16},{8,24},{16,0},{24,8},{32,48},{40,56},{48,32},{56,40},{64,80... | collective-permute-start | bytes 98312 | tf_op jit(solution)/shard_map/ppermute | solution.py:29
  202.0 7.7 %collective-permute-start.22 = (bf16[2,32,256]{2,1,0:T(8,128)(2,1)S(1)}, bf16[2,32,256]{2,1,0:T(8,128)(2,1)S(1)}, u32[]{:S(2)}, u32[]{:S(2)}) collective-permute-start(bf16[2,32,256]{2,1,0:T(8,128)(2,1)S(1)} %fusion.38), channel_id=1, source_target_pairs={{0,16},{8,24},{16,0},{24,8},{32,48},{40,56},{48,32},{56,40},{64,80... | collective-permute-start | bytes 98312 | tf_op jit(solution)/shard_map/ppermute | solution.py:29
  205.0 8.6 %collective-permute-start.15 = (bf16[2,32,256]{2,1,0:T(8,128)(2,1)S(1)}, bf16[2,32,256]{2,1,0:T(8,128)(2,1)S(1)}, u32[]{:S(2)}, u32[]{:S(2)}) collective-permute-start(bf16[2,32,256]{2,1,0:T(8,128)(2,1)S(1)} %get-tuple-element.10), channel_id=1, source_target_pairs={{0,16},{8,24},{16,0},{24,8},{32,48},{40,56},{48,32},{56,40},{64,80... | collective-permute-start | bytes 98312 | tf_op jit(solution)/shard_map/ppermute | solution.py:29
  209.7 34.1 %collective-permute-start.19 = (bf16[2,32,256]{2,1,0:T(8,128)(2,1)S(1)}, bf16[2,32,256]{2,1,0:T(8,128)(2,1)S(1)}, u32[]{:S(2)}, u32[]{:S(2)}) collective-permute-start(bf16[2,32,256]{2,1,0:T(8,128)(2,1)S(1)} %get-tuple-element.4), channel_id=1, source_target_pairs={{0,32},{8,40},{16,48},{24,56},{32,0},{40,8},{48,16},{56,24},{64,96... | collective-permute-start | bytes 98312 | tf_op jit(solution)/shard_map/ppermute | solution.py:29
  213.6 9.8 %collective-permute-start.28 = (bf16[2,32,256]{2,1,0:T(8,128)(2,1)S(1)}, bf16[2,32,256]{2,1,0:T(8,128)(2,1)S(1)}, u32[]{:S(2)}, u32[]{:S(2)}) collective-permute-start(bf16[2,32,256]{2,1,0:T(8,128)(2,1)S(1)} %fusion.54), channel_id=1, source_target_pairs={{0,32},{8,40},{16,48},{24,56},{32,0},{40,8},{48,16},{56,24},{64,96... | collective-permute-start | bytes 98312 | tf_op jit(solution)/shard_map/ppermute | solution.py:29
  223.5 9.8 %collective-permute-start.23 = (bf16[2,32,256]{2,1,0:T(8,128)(2,1)S(1)}, bf16[2,32,256]{2,1,0:T(8,128)(2,1)S(1)}, u32[]{:S(2)}, u32[]{:S(2)}) collective-permute-start(bf16[2,32,256]{2,1,0:T(8,128)(2,1)S(1)} %fusion.42), channel_id=1, source_target_pairs={{0,32},{8,40},{16,48},{24,56},{32,0},{40,8},{48,16},{56,24},{64,96... | collective-permute-start | bytes 98312 | tf_op jit(solution)/shard_map/ppermute | solution.py:29
  233.3 14.6 %collective-permute-start.29 = (bf16[2,32,256]{2,1,0:T(8,128)(2,1)S(1)}, bf16[2,32,256]{2,1,0:T(8,128)(2,1)S(1)}, u32[]{:S(2)}, u32[]{:S(2)}) collective-permute-start(bf16[2,32,256]{2,1,0:T(8,128)(2,1)S(1)} %fusion.40), channel_id=1, source_target_pairs={{0,64},{8,72},{16,80},{24,88},{32,96},{40,104},{48,112},{56,120},{... | collective-permute-start | bytes 98312 | tf_op jit(solution)/shard_map/ppermute | solution.py:29
  243.7 14.9 %collective-permute-start.24 = (bf16[2,32,256]{2,1,0:T(8,128)(2,1)S(1)}, bf16[2,32,256]{2,1,0:T(8,128)(2,1)S(1)}, u32[]{:S(2)}, u32[]{:S(2)}) collective-permute-start(bf16[2,32,256]{2,1,0:T(8,128)(2,1)S(1)} %get-tuple-element.6), channel_id=1, source_target_pairs={{0,64},{8,72},{16,80},{24,88},{32,96},{40,104},{48,112},{56,120},{... | collective-permute-start | bytes 98312 | tf_op jit(solution)/shard_map/ppermute | solution.py:29
  247.9 10.7 %collective-permute-start.30 = (bf16[2,32,256]{2,1,0:T(8,128)(2,1)S(1)}, bf16[2,32,256]{2,1,0:T(8,128)(2,1)S(1)}, u32[]{:S(2)}, u32[]{:S(2)}) collective-permute-start(bf16[2,32,256]{2,1,0:T(8,128)(2,1)S(1)} %get-tuple-element.8), channel_id=1, source_target_pairs={{0,128},{8,136},{16,144},{24,152},{32,160},{40,168},{48,176},{56,1... | collective-permute-start | bytes 98312 | tf_op jit(solution)/shard_map/ppermute | solution.py:29
where the time goes:
time: 263 us; the launch traced here: 261 us
  starting transfers between devices  135 us (51%)
  waiting for transfers between devices  48.9 us (19%)
  local copies, waits for them, and re-layouts  42.9 us (16%)
  other arithmetic  19.1 us (7%)
  matrix products  13.5 us (5%)
    ppermute x27, starting transfers between devices, partner(): return lax.ppermute(value, axis, pairs)  110 us
    ppermute x27, waiting for transfers between devices, partner(): return lax.ppermute(value, axis, pairs)  33 us
    all_to_all x1, waiting for transfers between devices, body(): lax.all_to_all(packed, 'head', split_axis=2, concat_axis=1, tiled=True)  15.9 us
    ppermute x2, starting transfers between devices, padded(): lax.ppermute(lax.slice_in_dim(block, 0, width, axis=dim), axis, backward)  14.5 us
    dot_general x12, matrix products, product(): return jnp.einsum(form, left, right, preferred_element_type=jnp.float32)  13.5 us
    unnamed x40, local copies, waits for them, and re-layouts  9.43 us
    slice x10, local copies, waits for them, and re-layouts, windows(): return jnp.concatenate([framed[:-2], framed[1:-1], framed[2:]], axis=1)  8.19 us
    ppermute x2, starting transfers between devices, padded(): lax.ppermute(lax.slice_in_dim(block, block.shape[dim] - width, None, axis...  5.84 us
  transfers between devices with their start and end apart: 32, of which 9 were waited for; matrix products, arithmetic and copies ran while one was open for 15% of the time, Pallas kernels for 0%

commit v1 on v0

v1 whole, which is shorter than its diff:
```python
import math

import jax
import jax.numpy as jnp
from jax import lax
from jax.experimental import pallas as pl
from jax.experimental.pallas import tpu as pltpu
from jax.sharding import PartitionSpec as P

HEAD_DIM = 128
LEAF = 256
RATIO = 16
TOKENS = 512
SPAN = 256
SHARES = 8
SHARE = 64
LEVELS = 6
OWN = 64
COUNT = [32 >> level for level in range(LEVELS)]
START = [64 - (64 >> level) for level in range(LEVELS)]
MESSAGE = [(16 >> b) * (7 - b) if b < 5 else 1 for b in range(LEVELS)]
HELD = [sum(MESSAGE[b + 1 :]) for b in range(LEVELS)]
COARSE = sum(MESSAGE)
F32 = jnp.float32
BF16 = jnp.bfloat16
VMEM = pl.BlockSpec(memory_space=pltpu.VMEM)
SMEM = pl.BlockSpec(memory_space=pltpu.SMEM)
LIMIT = pltpu.CompilerParams(vmem_limit_bytes=48 * 1024 * 1024)


def dot(left, right, over):
    return lax.dot_general(left, right, (over, ((), ())), preferred_element_type=F32)


NN = ((1,), (0,))
NT = ((1,), (1,))


def call(kernel, out_shape, scratch=(), specs=None, count=1):
    return pl.pallas_call(
        kernel,
        out_shape=out_shape,
        in_specs=specs or [VMEM] * count,
        out_specs=jax.tree.map(lambda _: VMEM, out_shape),
        scratch_shapes=scratch,
        compiler_params=LIMIT,
    )


def shape(rows, columns, kind=BF16):
    return jax.ShapeDtypeStruct((rows, columns), kind)


def pack_kernel(first, second, packed):
    for share in range(SHARES):
        columns = slice(share * SPAN, (share + 1) * SPAN)
        packed[share, :SHARE, :] = first[:, columns]
        packed[share, SHARE:, :] = second[:, columns]


def pack(first, second):
    out = jax.ShapeDtypeStruct((SHARES, 2 * SHARE, SPAN), BF16)
    return call(pack_kernel, out, count=2)(first, second)


def member(rows, columns, row_axis):
    row = lax.broadcasted_iota(jnp.int32, (rows, columns), row_axis)
    token = lax.broadcasted_iota(jnp.int32, (rows, columns), 1 - row_axis)
    weight = jnp.zeros((rows, columns), F32)
    for level in range(LEVELS):
        shift = 4 + level
        hit = row == START[level] + lax.shift_right_logical(token, shift)
        weight = jnp.where(hit, 1.0 / (1 << shift), weight)
    return weight.astype(BF16)


def pool_kernel(kv, pooled):
    weight = member(OWN, TOKENS, 0)
    for part in range(2):
        rows = kv[:, part * SHARE : (part + 1) * SHARE, :].reshape(TOKENS, SPAN)
        pooled[:, part * SPAN : (part + 1) * SPAN] = dot(weight, rows, NN).astype(BF16)


def attend_kernel(
    spot, kv, low, high, qg, coarse,
    attended, query_grad, centre, to_prev, to_next, coarse_grad,
    keys, values, key_grad, value_grad,
):
    factor = HEAD_DIM ** (-0.5)
    binary = factor * math.log2(math.e)
    position = spot[0]
    bias_low = jnp.where(position == 0, -1e30, 0.0).astype(F32)
    bias_high = jnp.where(position == spot[1] - 1, -1e30, 0.0).astype(F32)
    for head in range(2):
        columns = slice(head * HEAD_DIM, (head + 1) * HEAD_DIM)
        for part, store in ((0, keys), (1, values)):
            rows = slice(part * SHARE, (part + 1) * SHARE)
            store[:LEAF, :] = low[:, rows, columns].reshape(LEAF, HEAD_DIM)
            store[LEAF : LEAF + TOKENS, :] = kv[:, rows, columns].reshape(TOKENS, HEAD_DIM)
            store[LEAF + TOKENS :, :] = high[:, rows, columns].reshape(LEAF, HEAD_DIM)
        far_key = coarse[:, head * HEAD_DIM : (head + 1) * HEAD_DIM]
        far_value = coarse[:, SPAN + head * HEAD_DIM : SPAN + (head + 1) * HEAD_DIM]
        key_t = jnp.transpose(keys[...])
        value_t = jnp.transpose(values[...])
        far_key_t = jnp.transpose(far_key)
        far_value_t = jnp.transpose(far_value)
        far_key_grad = jnp.zeros((COARSE, HEAD_DIM), F32)
        far_value_grad = jnp.zeros((COARSE, HEAD_DIM), F32)
        for block in range(2):
            query = qg[4 * block : 4 * block + 4, :SHARE, columns].reshape(LEAF, HEAD_DIM)
            grad = qg[4 * block : 4 * block + 4, SHARE:, columns].reshape(LEAF, HEAD_DIM)
            window = slice(block * LEAF, block * LEAF + 3 * LEAF)
            near = dot(keys[window, :], query, NT) * binary
            if block == 0:
                near = jnp.concatenate([near[:LEAF] + bias_low, near[LEAF:]], axis=0)
            else:
                near = jnp.concatenate([near[: 2 * LEAF], near[2 * LEAF :] + bias_high], axis=0)
            far = dot(far_key, query, NT) * binary + math.log2(RATIO)
            top = jnp.maximum(
                jnp.max(near, axis=0, keepdims=True), jnp.max(far, axis=0, keepdims=True)
            )
            near = jnp.exp2(near - top)
            far = jnp.exp2(far - top)
            total = jnp.sum(near, axis=0, keepdims=True) + jnp.sum(far, axis=0, keepdims=True)
            inverse = 1.0 / total
            near = near * inverse
            far = far * inverse
            near_low = near.astype(BF16)
            far_low = far.astype(BF16)
            mixed_t = dot(value_t[:, window], near_low, NN) + dot(far_value_t, far_low, NN)
            grad_t = jnp.transpose(grad.astype(F32))
            delta = jnp.sum(grad_t * mixed_t, axis=0, keepdims=True)
            near_score = (near * (dot(values[window, :], grad, NT) - delta)).astype(BF16)
            far_score = (far * (dot(far_value, grad, NT) - delta)).astype(BF16)
            query_t = dot(key_t[:, window], near_score, NN) + dot(far_key_t, far_score, NN)
            out = slice(block * LEAF, (block + 1) * LEAF)
            attended[out, columns] = jnp.transpose(mixed_t).astype(BF16)
            query_grad[out, columns] = jnp.transpose(query_t * factor).astype(BF16)
            near_key_grad = dot(near_score, query, NN) * factor
            near_value_grad = dot(near_low, grad, NN)
            far_key_grad = far_key_grad + dot(far_score, query, NN) * factor
            far_value_grad = far_value_grad + dot(far_low, grad, NN)
            if block == 0:
                key_grad[: 3 * LEAF, :] = near_key_grad
                value_grad[: 3 * LEAF, :] = near_value_grad
            else:
                key_grad[LEAF : 3 * LEAF, :] += near_key_grad[: 2 * LEAF]
                value_grad[LEAF : 3 * LEAF, :] += near_value_grad[: 2 * LEAF]
                key_grad[3 * LEAF :, :] = near_key_grad[2 * LEAF :]
                value_grad[3 * LEAF :, :] = near_value_grad[2 * LEAF :]
        for part, store, far_grad in ((0, key_grad, far_key_grad), (1, value_grad, far_value_grad)):
            place = slice(part * SPAN + head * HEAD_DIM, part * SPAN + (head + 1) * HEAD_DIM)
            to_prev[:, place] = store[:LEAF, :].astype(BF16)
            centre[:, place] = store[LEAF : LEAF + TOKENS, :]
            to_next[:, place] = store[LEAF + TOKENS :, :].astype(BF16)
            coarse_grad[:, place] = far_grad


def finish_kernel(centre, from_prev, from_next, pooled, key_grad, value_grad):
    weight = member(TOKENS, OWN, 1)
    spread = dot(weight, pooled[...], NN) + centre[...]
    low = spread[:LEAF] + from_prev[...].astype(F32)
    high = spread[LEAF:] + from_next[...].astype(F32)
    key_grad[:LEAF, :] = low[:, :SPAN].astype(BF16)
    key_grad[LEAF:, :] = high[:, :SPAN].astype(BF16)
    value_grad[:LEAF, :] = low[:, SPAN:].astype(BF16)
    value_grad[LEAF:, :] = high[:, SPAN:].astype(BF16)


def body(query, key, value, cotangent):
    devices = lax.axis_size("context")
    position = lax.axis_index("context")

    def ring(block, step):
        pairs = [(source, (source + step) % devices) for source in range(devices)]
        return lax.ppermute(block, "context", pairs)

    def partner(block, bit):
        pairs = [(source, source ^ (1 << bit)) for source in range(devices)]
        return lax.ppermute(block, "context", pairs)

    kv = lax.all_to_all(pack(key, value), "head", 0, 0)
    qg = lax.all_to_all(pack(query, cotangent), "head", 0, 0)
    low = ring(kv[4:], 1)
    high = ring(kv[:4], -1)
    pooled = call(pool_kernel, shape(OWN, 2 * SPAN))(kv)
    held = jnp.zeros((0, 2 * SPAN), BF16)
    for bit in reversed(range(LEVELS)):
        own = pooled[START[bit] : START[bit] + COUNT[bit]]
        held = jnp.concatenate([held, partner(jnp.concatenate([own, held]), bit)])
    attended, query_grad, centre, to_prev, to_next, coarse_grad = call(
        attend_kernel,
        (
            shape(TOKENS, SPAN),
            shape(TOKENS, SPAN),
            shape(TOKENS, 2 * SPAN, F32),
            shape(LEAF, 2 * SPAN),
            shape(LEAF, 2 * SPAN),
            shape(COARSE, 2 * SPAN, F32),
        ),
        [
            pltpu.VMEM((2 * LEAF + TOKENS, HEAD_DIM), BF16),
            pltpu.VMEM((2 * LEAF + TOKENS, HEAD_DIM), BF16),
            pltpu.VMEM((2 * LEAF + TOKENS, HEAD_DIM), F32),
            pltpu.VMEM((2 * LEAF + TOKENS, HEAD_DIM), F32),
        ],
        [SMEM] + [VMEM] * 5,
    )(jnp.stack([position, jnp.int32(devices)]), kv, low, high, qg, held)
    from_next = ring(to_prev, -1)
    from_prev = ring(to_next, 1)
    rest = coarse_grad
    own_grads = []
    for bit in range(LEVELS):
        back = partner(rest[HELD[bit] :].astype(BF16), bit)
        own_grads.append(back[: COUNT[bit]])
        rest = rest[: HELD[bit]] + back[COUNT[bit] :].astype(F32)
    own_grads.append(jnp.zeros((1, 2 * SPAN), BF16))
    key_grad, value_grad = call(
        finish_kernel, (shape(TOKENS, SPAN), shape(TOKENS, SPAN)), count=4
    )(centre, from_prev, from_next, jnp.concatenate(own_grads))
    return attended, query_grad, key_grad, value_grad


def solution(mesh):
    spec = P(("context", "head"), None)
    out = P("context", "head")
    return jax.shard_map(
        body, mesh=mesh, in_specs=(spec,) * 4, out_specs=(out,) * 4, check_vma=False
    )
```

time: 263 us -> 141 us (0.54)
  starting transfers between devices: 135 us -> 72.1 us
  local copies, waits for them, and re-layouts: 42.9 us -> 2.93 us
  other arithmetic: 19.1 us -> 0.16 us
  blocking collectives: 0 us -> 14.7 us
  matrix products: 13.5 us -> 0 us
  waiting for transfers between devices: 48.9 us -> 40 us
  Pallas kernels: 0 us -> 8.81 us
    ppermute x31 -> x16, starting transfers between devices: 130 us -> 68.6 us  [the longest x12 52.7 us: partner(): return lax.ppermute(block, 'context', pairs)]
    all_to_all x1, waiting for transfers between devices: 15.9 us -> 0.01 us  [body(): qg = lax.all_to_all(pack(query, cotangent), 'head', 0, 0)]
    all_to_all x0 -> x1, blocking collectives: none -> 14.7 us  [body(): kv = lax.all_to_all(pack(key, value), 'head', 0, 0)]
    dot_general x12 -> x0, matrix products: 13.5 us -> none  [product(): return jnp.einsum(form, left, right, preferred_element_type=jnp.float32)]
    slice x20 -> x22, local copies, waits for them, and re-layouts: 11.1 us -> 0.14 us  [the longest x5 0.05 us: body(): back = partner(rest[HELD[bit]:].astype(BF16), bit)]
    pallas_call x0 -> x5, Pallas kernels: none -> 8.81 us  [the longest x1 6.59 us: body(): call(attend_kernel, (shape(TOKENS, SPAN), shape(TOKENS, SPAN), shape(TOKE...]
    unnamed x40 -> x18, local copies, waits for them, and re-layouts: 9.43 us -> 1.92 us
    ppermute x31 -> x16, waiting for transfers between devices: 33 us -> 40 us  [the longest x12 40 us: partner(): return lax.ppermute(block, 'context', pairs)]
  transfers between devices with their start and end apart: 32 -> 17, of which waited for: 9 -> 10; matrix products, arithmetic and copies ran while one was open for 15% -> 1% of each run, Pallas kernels for 0% -> 1%
where the time goes in v1:
time: 141 us; the launch traced here: 140 us
  starting transfers between devices  72.1 us (51%)
  waiting for transfers between devices  40 us (28%)
  blocking collectives  14.7 us (10%)
  Pallas kernels  8.81 us (6%)
  local copies, waits for them, and re-layouts  2.93 us (2%)
    ppermute x12, starting transfers between devices, partner(): return lax.ppermute(block, 'context', pairs)  52.7 us
    ppermute x12, waiting for transfers between devices, partner(): return lax.ppermute(block, 'context', pairs)  40 us
    ppermute x4, starting transfers between devices, ring(): return lax.ppermute(block, 'context', pairs)  15.9 us
    all_to_all x1, blocking collectives, body(): kv = lax.all_to_all(pack(key, value), 'head', 0, 0)  14.7 us
    pallas_call x1, Pallas kernels, body(): call(attend_kernel, (shape(TOKENS, SPAN), shape(TOKENS, SPAN), shape(TOKE...  6.59 us
    all_to_all x1, starting transfers between devices, body(): qg = lax.all_to_all(pack(query, cotangent), 'head', 0, 0)  3.49 us
  transfers between devices with their start and end apart: 17, of which 10 were waited for; matrix products, arithmetic and copies ran while one was open for 1% of the time, Pallas kernels for 1%

profile of v1, /device:TPU:2, one launch (start us, length us, event | category | flops | bytes accessed | tf_op | source)
XLA Modules:
  0.0 139.8 jit_solution(15662699531976189717)
XLA Ops:
  0.6 0.9 copy-done
  1.6 0.9 copy-done.1
  2.6 14.7 %all_to_all.10.kv = bf16[8,128,256]{2,1,0:T(8,128)(2,1)S(1)} all-to-all(bf16[8,128,256]{2,1,0:T(8,128)(2,1)S(1)} %shard_map.75), channel_id=1, replica_groups=mesh['context'=64,'head'=8] {'head'}, dimensions={0} | all-to-all | bytes 1048576 | tf_op jit(solution)/shard_map/all_to_all | solution.py:182
  17.2 0.2 shard_map.77
  17.5 4.0 %collective-permute-start.2 = (bf16[1,512]{1,0:T(2,128)(2,1)S(1)}, bf16[1,512]{1,0:T(2,128)(2,1)S(1)}, u32[]{:S(2)}, u32[]{:S(2)}) collective-permute-start(bf16[1,512]{1,0:T(2,128)(2,1)S(1)} %slice.119), channel_id=1, source_target_pairs={{0,256},{8,264},{16,272},{24,280},{32,288},{40,296},{48,304},{56,3... | collective-permute-start | bytes 3080 | tf_op jit(solution)/shard_map/ppermute | solution.py:180
  21.5 2.9 %collective-permute-done.2 = bf16[1,512]{1,0:T(2,128)(2,1)S(1)} collective-permute-done((bf16[1,512]{1,0:T(2,128)(2,1)S(1)}, bf16[1,512]{1,0:T(2,128)(2,1)S(1)}, u32[]{:S(2)}, u32[]{:S(2)}) %collective-permute-start.2) | collective-permute-done | bytes 1056 | tf_op jit(solution)/shard_map/ppermute | solution.py:180
  24.5 6.0 %collective-permute-start.3 = (bf16[3,512]{1,0:T(4,128)(2,1)S(1)}, bf16[3,512]{1,0:T(4,128)(2,1)S(1)}, u32[]{:S(2)}, u32[]{:S(2)}) collective-permute-start(bf16[3,512]{1,0:T(4,128)(2,1)S(1)} %pad_maximum_fusion.2), channel_id=1, source_target_pairs={{0,128},{8,136},{16,144},{24,152},{32,160},{40,168},{48,176},{56,1... | collective-permute-start | bytes 9224 | tf_op jit(solution)/shard_map/ppermute | solution.py:180
  30.4 0.8 shard_map.76
  31.3 3.5 %all-to-all-start.1 = ((bf16[8,128,256]{2,1,0:T(8,128)(2,1)}), bf16[8,128,256]{2,1,0:T(8,128)(2,1)S(1)}, u32[]{:S(2)}, u32[]{:S(2)}) async-start(bf16[8,128,256]{2,1,0:T(8,128)(2,1)} %shard_map.76), calls=%async_computation.1 | async-start | bytes 1048576 | tf_op jit(solution)/shard_map/all_to_all | solution.py:183
  34.8 0.0 collective-permute-done.3
  34.8 12.2 %collective-permute-start.4 = (bf16[8,512]{1,0:T(8,128)(2,1)S(1)}, bf16[8,512]{1,0:T(8,128)(2,1)S(1)}, u32[]{:S(2)}, u32[]{:S(2)}) collective-permute-start(bf16[8,512]{1,0:T(8,128)(2,1)S(1)} %pad_maximum_fusion.1), channel_id=1, source_target_pairs={{0,64},{8,72},{16,80},{24,88},{32,96},{40,104},{48,112},{56,120},{... | collective-permute-start | bytes 24584 | tf_op jit(solution)/shard_map/ppermute | solution.py:180
  47.1 2.9 %collective-permute-start = (bf16[4,128,256]{2,1,0:T(8,128)(2,1)S(1)}, bf16[4,128,256]{2,1,0:T(8,128)(2,1)S(1)}, u32[]{:S(2)}, u32[]{:S(2)}) collective-permute-start(bf16[4,128,256]{2,1,0:T(8,128)(2,1)S(1)} %get-tuple-element.21), channel_id=1, source_target_pairs={{0,8},{8,16},{16,24},{24,32},{32,40},{40,48},{48,56},{56,64},{64,7... | collective-permute-start | bytes 786440 | tf_op jit(solution)/shard_map/ppermute | solution.py:176
  50.1 5.0 %collective-permute-start.1 = (bf16[4,128,256]{2,1,0:T(8,128)(2,1)S(1)}, bf16[4,128,256]{2,1,0:T(8,128)(2,1)S(1)}, u32[]{:S(2)}, u32[]{:S(2)}) collective-permute-start(bf16[4,128,256]{2,1,0:T(8,128)(2,1)S(1)} %get-tuple-element.20), channel_id=1, source_target_pairs={{0,504},{8,0},{16,8},{24,16},{32,24},{40,32},{48,40},{56,48},{64,5... | collective-permute-start | bytes 786440 | tf_op jit(solution)/shard_map/ppermute | solution.py:176
  55.1 0.0 collective-permute-done.4
  55.1 3.4 %collective-permute-start.5 = (bf16[20,512]{1,0:T(8,128)(2,1)S(1)}, bf16[20,512]{1,0:T(8,128)(2,1)S(1)}, u32[]{:S(2)}, u32[]{:S(2)}) collective-permute-start(bf16[20,512]{1,0:T(8,128)(2,1)S(1)} %pad_maximum_fusion), channel_id=1, source_target_pairs={{0,32},{8,40},{16,48},{24,56},{32,0},{40,8},{48,16},{56,24},{64,96... | collective-permute-start | bytes 61448 | tf_op jit(solution)/shard_map/ppermute | solution.py:180
  58.5 6.2 %collective-permute-done.5 = bf16[20,512]{1,0:T(8,128)(2,1)S(1)} collective-permute-done((bf16[20,512]{1,0:T(8,128)(2,1)S(1)}, bf16[20,512]{1,0:T(8,128)(2,1)S(1)}, u32[]{:S(2)}, u32[]{:S(2)}) %collective-permute-start.5) | collective-permute-done | bytes 20512 | tf_op jit(solution)/shard_map/ppermute | solution.py:180
  64.8 0.3 concatenate.36
  65.1 1.9 %collective-permute-start.6 = (bf16[48,512]{1,0:T(8,128)(2,1)S(1)}, bf16[48,512]{1,0:T(8,128)(2,1)S(1)}, u32[]{:S(2)}, u32[]{:S(2)}) collective-permute-start(bf16[48,512]{1,0:T(8,128)(2,1)S(1)} %concatenate.36), channel_id=1, source_target_pairs={{0,16},{8,24},{16,0},{24,8},{32,48},{40,56},{48,32},{56,40},{64,80... | collective-permute-start | bytes 147464 | tf_op jit(solution)/shard_map/ppermute | solution.py:180
  67.0 4.9 %collective-permute-done.6 = bf16[48,512]{1,0:T(8,128)(2,1)S(1)} collective-permute-done((bf16[48,512]{1,0:T(8,128)(2,1)S(1)}, bf16[48,512]{1,0:T(8,128)(2,1)S(1)}, u32[]{:S(2)}, u32[]{:S(2)}) %collective-permute-start.6) | collective-permute-done | bytes 49184 | tf_op jit(solution)/shard_map/ppermute | solution.py:180
  71.9 0.3 concatenate.37
  72.2 1.9 %collective-permute-start.7 = (bf16[112,512]{1,0:T(8,128)(2,1)S(1)}, bf16[112,512]{1,0:T(8,128)(2,1)S(1)}, u32[]{:S(2)}, u32[]{:S(2)}) collective-permute-start(bf16[112,512]{1,0:T(8,128)(2,1)S(1)} %concatenate.37), channel_id=1, source_target_pairs={{0,8},{8,0},{16,24},{24,16},{32,40},{40,32},{48,56},{56,48},{64,72... | collective-permute-start | bytes 344072 | tf_op jit(solution)/shard_map/ppermute | solution.py:180
  74.1 0.1 pad_add_fusion.spot
  74.2 4.7 %collective-permute-done.7 = bf16[112,512]{1,0:T(8,128)(2,1)S(1)} collective-permute-done((bf16[112,512]{1,0:T(8,128)(2,1)S(1)}, bf16[112,512]{1,0:T(8,128)(2,1)S(1)}, u32[]{:S(2)}, u32[]{:S(2)}) %collective-permute-start.7) | collective-permute-done | bytes 114720 | tf_op jit(solution)/shard_map/ppermute | solution.py:180
  78.9 0.3 concatenate.38.coarse
  79.2 0.0 all-to-all-done.1.qg
  79.2 0.0 collective-permute-done.low
  79.2 0.0 collective-permute-done.1.high
  79.2 6.6 %shard_map.78 = (bf16[512,256]{1,0:T(8,128)(2,1)}, bf16[512,256]{1,0:T(8,128)(2,1)}, f32[512,512]{1,0:T(8,128)S(1)}, bf16[256,512]{1,0:T(8,128)(2,1)S(1)}, bf16[...) custom-call(s32[2]{0:T(128)S(1)} %pad_add_fusion.spot, bf16[8,128,256]{2,1,0:T(8,128)(2,1)S(1)} %all_to_all.10.kv, ...), custom_call_target="tpu_custom_call" | custom-call | tf_op jit(solution)/shard_map/pallas_call | solution.py:191
  85.8 1.9 %collective-permute-start.10 = (bf16[112,512]{1,0:T(8,128)(2,1)S(1)}, bf16[112,512]{1,0:T(8,128)(2,1)S(1)}, u32[]{:S(2)}, u32[]{:S(2)}) collective-permute-start(bf16[112,512]{1,0:T(8,128)(2,1)S(1)} %slice.163), channel_id=1, source_target_pairs={{0,8},{8,0},{16,24},{24,16},{32,40},{40,32},{48,56},{56,48},{64,72... | collective-permute-start | bytes 344072 | tf_op jit(solution)/shard_map/ppermute | solution.py:180
  87.7 4.8 %collective-permute-done.10 = bf16[112,512]{1,0:T(8,128)(2,1)S(1)} collective-permute-done((bf16[112,512]{1,0:T(8,128)(2,1)S(1)}, bf16[112,512]{1,0:T(8,128)(2,1)S(1)}, u32[]{:S(2)}, u32[]{:S(2)}) %collective-permute-start.10) | collective-permute-done | bytes 114720 | tf_op jit(solution)/shard_map/ppermute | solution.py:180
  92.5 1.9 %collective-permute-start.11 = (bf16[48,512]{1,0:T(8,128)(2,1)S(1)}, bf16[48,512]{1,0:T(8,128)(2,1)S(1)}, u32[]{:S(2)}, u32[]{:S(2)}) collective-permute-start(bf16[48,512]{1,0:T(8,128)(2,1)S(1)} %slice.164), channel_id=1, source_target_pairs={{0,16},{8,24},{16,0},{24,8},{32,48},{40,56},{48,32},{56,40},{64,80... | collective-permute-start | bytes 147464 | tf_op jit(solution)/shard_map/ppermute | solution.py:180
  94.5 5.0 %collective-permute-done.11 = bf16[48,512]{1,0:T(8,128)(2,1)S(1)} collective-permute-done((bf16[48,512]{1,0:T(8,128)(2,1)S(1)}, bf16[48,512]{1,0:T(8,128)(2,1)S(1)}, u32[]{:S(2)}, u32[]{:S(2)}) %collective-permute-start.11) | collective-permute-done | bytes 49184 | tf_op jit(solution)/shard_map/ppermute | solution.py:180
  99.5 3.6 %collective-permute-start.12 = (bf16[20,512]{1,0:T(8,128)(2,1)S(1)}, bf16[20,512]{1,0:T(8,128)(2,1)S(1)}, u32[]{:S(2)}, u32[]{:S(2)}) collective-permute-start(bf16[20,512]{1,0:T(8,128)(2,1)S(1)} %slice.165), channel_id=1, source_target_pairs={{0,32},{8,40},{16,48},{24,56},{32,0},{40,8},{48,16},{56,24},{64,96... | collective-permute-start | bytes 61448 | tf_op jit(solution)/shard_map/ppermute | solution.py:180
  103.0 6.3 %collective-permute-done.12 = bf16[20,512]{1,0:T(8,128)(2,1)S(1)} collective-permute-done((bf16[20,512]{1,0:T(8,128)(2,1)S(1)}, bf16[20,512]{1,0:T(8,128)(2,1)S(1)}, u32[]{:S(2)}, u32[]{:S(2)}) %collective-permute-start.12) | collective-permute-done | bytes 20512 | tf_op jit(solution)/shard_map/ppermute | solution.py:180
  109.3 6.1 %collective-permute-start.13 = (bf16[8,512]{1,0:T(8,128)(2,1)S(1)}, bf16[8,512]{1,0:T(8,128)(2,1)S(1)}, u32[]{:S(2)}, u32[]{:S(2)}) collective-permute-start(bf16[8,512]{1,0:T(8,128)(2,1)S(1)} %slice.166), channel_id=1, source_target_pairs={{0,64},{8,72},{16,80},{24,88},{32,96},{40,104},{48,112},{56,120},{... | collective-permute-start | bytes 24584 | tf_op jit(solution)/shard_map/ppermute | solution.py:180
  115.4 3.3 %collective-permute-start.8 = (bf16[256,512]{1,0:T(8,128)(2,1)S(1)}, bf16[256,512]{1,0:T(8,128)(2,1)S(1)}, u32[]{:S(2)}, u32[]{:S(2)}) collective-permute-start(bf16[256,512]{1,0:T(8,128)(2,1)S(1)} %get-tuple-element.15), channel_id=1, source_target_pairs={{0,8},{8,16},{16,24},{24,32},{32,40},{40,48},{48,56},{56,64},{64,7... | collective-permute-start | bytes 786440 | tf_op jit(solution)/shard_map/ppermute | solution.py:176
  118.8 4.6 %collective-permute-start.9 = (bf16[256,512]{1,0:T(8,128)(2,1)S(1)}, bf16[256,512]{1,0:T(8,128)(2,1)S(1)}, u32[]{:S(2)}, u32[]{:S(2)}) collective-permute-start(bf16[256,512]{1,0:T(8,128)(2,1)S(1)} %get-tuple-element.16), channel_id=1, source_target_pairs={{0,504},{8,0},{16,8},{24,16},{32,24},{40,32},{48,40},{56,48},{64,5... | collective-permute-start | bytes 786440 | tf_op jit(solution)/shard_map/ppermute | solution.py:176
  123.4 0.3 collective-permute-done.13
  123.7 6.2 %collective-permute-start.14 = (bf16[3,512]{1,0:T(4,128)(2,1)S(1)}, bf16[3,512]{1,0:T(4,128)(2,1)S(1)}, u32[]{:S(2)}, u32[]{:S(2)}) collective-permute-start(bf16[3,512]{1,0:T(4,128)(2,1)S(1)} %slice.167), channel_id=1, source_target_pairs={{0,128},{8,136},{16,144},{24,152},{32,160},{40,168},{48,176},{56,1... | collective-permute-start | bytes 9224 | tf_op jit(solution)/shard_map/ppermute | solution.py:180
  130.0 1.6 %collective-permute-done.14 = bf16[3,512]{1,0:T(4,128)(2,1)S(1)} collective-permute-done((bf16[3,512]{1,0:T(4,128)(2,1)S(1)}, bf16[3,512]{1,0:T(4,128)(2,1)S(1)}, u32[]{:S(2)}, u32[]{:S(2)}) %collective-permute-start.14) | collective-permute-done | bytes 3104 | tf_op jit(solution)/shard_map/ppermute | solution.py:180
  131.5 3.5 %collective-permute-start.15 = (bf16[1,512]{1,0:T(2,128)(2,1)S(1)}, bf16[1,512]{1,0:T(2,128)(2,1)S(1)}, u32[]{:S(2)}, u32[]{:S(2)}) collective-permute-start(bf16[1,512]{1,0:T(2,128)(2,1)S(1)} %fusion.1), channel_id=1, source_target_pairs={{0,256},{8,264},{16,272},{24,280},{32,288},{40,296},{48,304},{56,3... | collective-permute-start | bytes 3080 | tf_op jit(solution)/shard_map/ppermute | solution.py:180
  135.1 0.0 slice-start
  135.1 0.0 slice-start.1
  135.2 0.0 slice-start.2
  135.2 0.0 slice-start.3
  135.2 0.0 slice-start.4
  135.2 3.3 %collective-permute-done.15 = bf16[1,512]{1,0:T(2,128)(2,1)S(1)} collective-permute-done((bf16[1,512]{1,0:T(2,128)(2,1)S(1)}, bf16[1,512]{1,0:T(2,128)(2,1)S(1)}, u32[]{:S(2)}, u32[]{:S(2)}) %collective-permute-start.15) | collective-permute-done | bytes 1056 | tf_op jit(solution)/shard_map/ppermute | solution.py:180
  138.6 1.2 shard_map.79
  (46 shorter events, 0.3 us)
Async XLA Ops:
  0.6 1.0 copy-start
  1.6 0.9 copy-start.1
  17.2 13.2 %copy-start.2 = (bf16[64,2048]{1,0:T(8,128)(2,1)S(1)}, bf16[64,2048]{1,0:T(8,128)(2,1)}, u32[]{:S(2)}) copy-start(bf16[64,2048]{1,0:T(8,128)(2,1)} %first.3) | copy-start | bytes 786436
  17.2 13.2 %copy-start.3 = (bf16[64,2048]{1,0:T(8,128)(2,1)S(1)}, bf16[64,2048]{1,0:T(8,128)(2,1)}, u32[]{:S(2)}) copy-start(bf16[64,2048]{1,0:T(8,128)(2,1)} %second.3) | copy-start | bytes 786436
  17.5 7.0 %collective-permute-start.2 = (bf16[1,512]{1,0:T(2,128)(2,1)S(1)}, bf16[1,512]{1,0:T(2,128)(2,1)S(1)}, u32[]{:S(2)}, u32[]{:S(2)}) collective-permute-start(bf16[1,512]{1,0:T(2,128)(2,1)S(1)} %slice.119), channel_id=1, source_target_pairs={{0,256},{8,264},{16,272},{24,280},{32,288},{40,296},{48,304},{56,3... | collective-permute-start | bytes 3080 | tf_op jit(solution)/shard_map/ppermute | solution.py:180
  24.5 10.3 %collective-permute-start.3 = (bf16[3,512]{1,0:T(4,128)(2,1)S(1)}, bf16[3,512]{1,0:T(4,128)(2,1)S(1)}, u32[]{:S(2)}, u32[]{:S(2)}) collective-permute-start(bf16[3,512]{1,0:T(4,128)(2,1)S(1)} %pad_maximum_fusion.2), channel_id=1, source_target_pairs={{0,128},{8,136},{16,144},{24,152},{32,160},{40,168},{48,176},{56,1... | collective-permute-start | bytes 9224 | tf_op jit(solution)/shard_map/ppermute | solution.py:180
  31.3 47.9 %all-to-all-start.1 = ((bf16[8,128,256]{2,1,0:T(8,128)(2,1)}), bf16[8,128,256]{2,1,0:T(8,128)(2,1)S(1)}, u32[]{:S(2)}, u32[]{:S(2)}) async-start(bf16[8,128,256]{2,1,0:T(8,128)(2,1)} %shard_map.76), calls=%async_computation.1 | async-start | bytes 1048576 | tf_op jit(solution)/shard_map/all_to_all | solution.py:183
  34.8 20.3 %collective-permute-start.4 = (bf16[8,512]{1,0:T(8,128)(2,1)S(1)}, bf16[8,512]{1,0:T(8,128)(2,1)S(1)}, u32[]{:S(2)}, u32[]{:S(2)}) collective-permute-start(bf16[8,512]{1,0:T(8,128)(2,1)S(1)} %pad_maximum_fusion.1), channel_id=1, source_target_pairs={{0,64},{8,72},{16,80},{24,88},{32,96},{40,104},{48,112},{56,120},{... | collective-permute-start | bytes 24584 | tf_op jit(solution)/shard_map/ppermute | solution.py:180
  47.1 32.1 %collective-permute-start = (bf16[4,128,256]{2,1,0:T(8,128)(2,1)S(1)}, bf16[4,128,256]{2,1,0:T(8,128)(2,1)S(1)}, u32[]{:S(2)}, u32[]{:S(2)}) collective-permute-start(bf16[4,128,256]{2,1,0:T(8,128)(2,1)S(1)} %get-tuple-element.21), channel_id=1, source_target_pairs={{0,8},{8,16},{16,24},{24,32},{32,40},{40,48},{48,56},{56,64},{64,7... | collective-permute-start | bytes 786440 | tf_op jit(solution)/shard_map/ppermute | solution.py:176
  50.1 29.1 %collective-permute-start.1 = (bf16[4,128,256]{2,1,0:T(8,128)(2,1)S(1)}, bf16[4,128,256]{2,1,0:T(8,128)(2,1)S(1)}, u32[]{:S(2)}, u32[]{:S(2)}) collective-permute-start(bf16[4,128,256]{2,1,0:T(8,128)(2,1)S(1)} %get-tuple-element.20), channel_id=1, source_target_pairs={{0,504},{8,0},{16,8},{24,16},{32,24},{40,32},{48,40},{56,48},{64,5... | collective-permute-start | bytes 786440 | tf_op jit(solution)/shard_map/ppermute | solution.py:176
  55.1 9.6 %collective-permute-start.5 = (bf16[20,512]{1,0:T(8,128)(2,1)S(1)}, bf16[20,512]{1,0:T(8,128)(2,1)S(1)}, u32[]{:S(2)}, u32[]{:S(2)}) collective-permute-start(bf16[20,512]{1,0:T(8,128)(2,1)S(1)} %pad_maximum_fusion), channel_id=1, source_target_pairs={{0,32},{8,40},{16,48},{24,56},{32,0},{40,8},{48,16},{56,24},{64,96... | collective-permute-start | bytes 61448 | tf_op jit(solution)/shard_map/ppermute | solution.py:180
  65.1 6.9 %collective-permute-start.6 = (bf16[48,512]{1,0:T(8,128)(2,1)S(1)}, bf16[48,512]{1,0:T(8,128)(2,1)S(1)}, u32[]{:S(2)}, u32[]{:S(2)}) collective-permute-start(bf16[48,512]{1,0:T(8,128)(2,1)S(1)} %concatenate.36), channel_id=1, source_target_pairs={{0,16},{8,24},{16,0},{24,8},{32,48},{40,56},{48,32},{56,40},{64,80... | collective-permute-start | bytes 147464 | tf_op jit(solution)/shard_map/ppermute | solution.py:180
  72.2 6.7 %collective-permute-start.7 = (bf16[112,512]{1,0:T(8,128)(2,1)S(1)}, bf16[112,512]{1,0:T(8,128)(2,1)S(1)}, u32[]{:S(2)}, u32[]{:S(2)}) collective-permute-start(bf16[112,512]{1,0:T(8,128)(2,1)S(1)} %concatenate.37), channel_id=1, source_target_pairs={{0,8},{8,0},{16,24},{24,16},{32,40},{40,32},{48,56},{56,48},{64,72... | collective-permute-start | bytes 344072 | tf_op jit(solution)/shard_map/ppermute | solution.py:180
  85.8 6.7 %collective-permute-start.10 = (bf16[112,512]{1,0:T(8,128)(2,1)S(1)}, bf16[112,512]{1,0:T(8,128)(2,1)S(1)}, u32[]{:S(2)}, u32[]{:S(2)}) collective-permute-start(bf16[112,512]{1,0:T(8,128)(2,1)S(1)} %slice.163), channel_id=1, source_target_pairs={{0,8},{8,0},{16,24},{24,16},{32,40},{40,32},{48,56},{56,48},{64,72... | collective-permute-start | bytes 344072 | tf_op jit(solution)/shard_map/ppermute | solution.py:180
  92.5 42.6 %copy-start.4 = (bf16[112,512]{1,0:T(8,128)(2,1)}, bf16[112,512]{1,0:T(8,128)(2,1)S(1)}, u32[]{:S(2)}) copy-start(bf16[112,512]{1,0:T(8,128)(2,1)S(1)} %collective-permute-done.10) | copy-start | bytes 344068
  92.5 6.9 %collective-permute-start.11 = (bf16[48,512]{1,0:T(8,128)(2,1)S(1)}, bf16[48,512]{1,0:T(8,128)(2,1)S(1)}, u32[]{:S(2)}, u32[]{:S(2)}) collective-permute-start(bf16[48,512]{1,0:T(8,128)(2,1)S(1)} %slice.164), channel_id=1, source_target_pairs={{0,16},{8,24},{16,0},{24,8},{32,48},{40,56},{48,32},{56,40},{64,80... | collective-permute-start | bytes 147464 | tf_op jit(solution)/shard_map/ppermute | solution.py:180
  99.4 35.7 %copy-start.5 = (bf16[48,512]{1,0:T(8,128)(2,1)}, bf16[48,512]{1,0:T(8,128)(2,1)S(1)}, u32[]{:S(2)}) copy-start(bf16[48,512]{1,0:T(8,128)(2,1)S(1)} %collective-permute-done.11) | copy-start | bytes 147460
  99.5 9.9 %collective-permute-start.12 = (bf16[20,512]{1,0:T(8,128)(2,1)S(1)}, bf16[20,512]{1,0:T(8,128)(2,1)S(1)}, u32[]{:S(2)}, u32[]{:S(2)}) collective-permute-start(bf16[20,512]{1,0:T(8,128)(2,1)S(1)} %slice.165), channel_id=1, source_target_pairs={{0,32},{8,40},{16,48},{24,56},{32,0},{40,8},{48,16},{56,24},{64,96... | collective-permute-start | bytes 61448 | tf_op jit(solution)/shard_map/ppermute | solution.py:180
  109.3 25.8 %copy-start.6 = (bf16[20,512]{1,0:T(8,128)(2,1)}, bf16[20,512]{1,0:T(8,128)(2,1)S(1)}, u32[]{:S(2)}) copy-start(bf16[20,512]{1,0:T(8,128)(2,1)S(1)} %collective-permute-done.12) | copy-start | bytes 61444
  109.3 14.4 %collective-permute-start.13 = (bf16[8,512]{1,0:T(8,128)(2,1)S(1)}, bf16[8,512]{1,0:T(8,128)(2,1)S(1)}, u32[]{:S(2)}, u32[]{:S(2)}) collective-permute-start(bf16[8,512]{1,0:T(8,128)(2,1)S(1)} %slice.166), channel_id=1, source_target_pairs={{0,64},{8,72},{16,80},{24,88},{32,96},{40,104},{48,112},{56,120},{... | collective-permute-start | bytes 24584 | tf_op jit(solution)/shard_map/ppermute | solution.py:180
  115.4 23.2 %collective-permute-start.8 = (bf16[256,512]{1,0:T(8,128)(2,1)S(1)}, bf16[256,512]{1,0:T(8,128)(2,1)S(1)}, u32[]{:S(2)}, u32[]{:S(2)}) collective-permute-start(bf16[256,512]{1,0:T(8,128)(2,1)S(1)} %get-tuple-element.15), channel_id=1, source_target_pairs={{0,8},{8,16},{16,24},{24,32},{32,40},{40,48},{48,56},{56,64},{64,7... | collective-permute-start | bytes 786440 | tf_op jit(solution)/shard_map/ppermute | solution.py:176
  118.8 19.8 %collective-permute-start.9 = (bf16[256,512]{1,0:T(8,128)(2,1)S(1)}, bf16[256,512]{1,0:T(8,128)(2,1)S(1)}, u32[]{:S(2)}, u32[]{:S(2)}) collective-permute-start(bf16[256,512]{1,0:T(8,128)(2,1)S(1)} %get-tuple-element.16), channel_id=1, source_target_pairs={{0,504},{8,0},{16,8},{24,16},{32,24},{40,32},{48,40},{56,48},{64,5... | collective-permute-start | bytes 786440 | tf_op jit(solution)/shard_map/ppermute | solution.py:176
  123.7 11.4 %copy-start.7 = (bf16[8,512]{1,0:T(8,128)(2,1)}, bf16[8,512]{1,0:T(8,128)(2,1)S(1)}, u32[]{:S(2)}) copy-start(bf16[8,512]{1,0:T(8,128)(2,1)S(1)} %collective-permute-done.13) | copy-start | bytes 24580
  123.7 7.8 %collective-permute-start.14 = (bf16[3,512]{1,0:T(4,128)(2,1)S(1)}, bf16[3,512]{1,0:T(4,128)(2,1)S(1)}, u32[]{:S(2)}, u32[]{:S(2)}) collective-permute-start(bf16[3,512]{1,0:T(4,128)(2,1)S(1)} %slice.167), channel_id=1, source_target_pairs={{0,128},{8,136},{16,144},{24,152},{32,160},{40,168},{48,176},{56,1... | collective-permute-start | bytes 9224 | tf_op jit(solution)/shard_map/ppermute | solution.py:180
  131.5 3.6 %copy-start.8 = (bf16[3,512]{1,0:T(4,128)(2,1)}, bf16[3,512]{1,0:T(4,128)(2,1)S(1)}, u32[]{:S(2)}) copy-start(bf16[3,512]{1,0:T(4,128)(2,1)S(1)} %collective-permute-done.14) | copy-start | bytes 9220
  131.5 7.0 %collective-permute-start.15 = (bf16[1,512]{1,0:T(2,128)(2,1)S(1)}, bf16[1,512]{1,0:T(2,128)(2,1)S(1)}, u32[]{:S(2)}, u32[]{:S(2)}) collective-permute-start(bf16[1,512]{1,0:T(2,128)(2,1)S(1)} %fusion.1), channel_id=1, source_target_pairs={{0,256},{8,264},{16,272},{24,280},{32,288},{40,296},{48,304},{56,3... | collective-permute-start | bytes 3080 | tf_op jit(solution)/shard_map/ppermute | solution.py:180
  135.1 3.4 %slice-start = ((bf16[112,512]{1,0:T(8,128)(2,1)}), bf16[32,512]{1,0:T(8,128)(2,1)S(1)}, s32[]{:S(2)}) async-start(bf16[112,512]{1,0:T(8,128)(2,1)} %copy-done.4), calls=%async_computation.2 | async-start | bytes 65536 | tf_op jit(solution)/shard_map/slice | solution.py:215
  135.1 3.4 %slice-start.1 = ((bf16[48,512]{1,0:T(8,128)(2,1)}), bf16[16,512]{1,0:T(8,128)(2,1)S(1)}, s32[]{:S(2)}) async-start(bf16[48,512]{1,0:T(8,128)(2,1)} %copy-done.5), calls=%async_computation.3 | async-start | bytes 32768 | tf_op jit(solution)/shard_map/slice | solution.py:215
  135.2 3.4 %slice-start.2 = ((bf16[20,512]{1,0:T(8,128)(2,1)}), bf16[8,512]{1,0:T(8,128)(2,1)S(1)}, s32[]{:S(2)}) async-start(bf16[20,512]{1,0:T(8,128)(2,1)} %copy-done.6), calls=%async_computation.4 | async-start | bytes 16384 | tf_op jit(solution)/shard_map/slice | solution.py:215
  135.2 3.4 %slice-start.3 = ((bf16[8,512]{1,0:T(8,128)(2,1)}), bf16[4,512]{1,0:T(4,128)(2,1)S(1)}, s32[]{:S(2)}) async-start(bf16[8,512]{1,0:T(8,128)(2,1)} %copy-done.7), calls=%async_computation.5 | async-start | bytes 8192 | tf_op jit(solution)/shard_map/slice | solution.py:215
  135.2 3.4 %slice-start.4 = ((bf16[3,512]{1,0:T(4,128)(2,1)}), bf16[2,512]{1,0:T(2,128)(2,1)S(1)}, s32[]{:S(2)}) async-start(bf16[3,512]{1,0:T(4,128)(2,1)} %copy-done.8), calls=%async_computation.6 | async-start | bytes 4096 | tf_op jit(solution)/shard_map/slice | solution.py:215

commit v2 on v1

v2 whole, which is shorter than its diff:
```python
import math

import jax
import jax.numpy as jnp
from jax import lax
from jax.experimental import pallas as pl
from jax.experimental.pallas import tpu as pltpu
from jax.sharding import PartitionSpec as P

HEAD_DIM = 128
LEAF = 256
RATIO = 16
TOKENS = 512
SPAN = 256
SHARES = 8
SHARE = 64
LEVELS = 6
OWN = 64
COUNT = [32 >> level for level in range(LEVELS)]
START = [64 - (64 >> level) for level in range(LEVELS)]
PEERS = 8
FAR_ROWS = 8
NEAR_ROWS = 32
HELD = 12
NEAR = PEERS * NEAR_ROWS
COARSE = NEAR + COUNT[0]
F32 = jnp.float32
BF16 = jnp.bfloat16
VMEM = pl.BlockSpec(memory_space=pltpu.VMEM)
SMEM = pl.BlockSpec(memory_space=pltpu.SMEM)
LIMIT = pltpu.CompilerParams(vmem_limit_bytes=48 * 1024 * 1024)
NN = ((1,), (0,))
NT = ((1,), (1,))


def dot(left, right, over):
    return lax.dot_general(left, right, (over, ((), ())), preferred_element_type=F32)


def call(kernel, out_shape, scratch=(), specs=None, count=1):
    return pl.pallas_call(
        kernel,
        out_shape=out_shape,
        in_specs=specs or [VMEM] * count,
        out_specs=jax.tree.map(lambda _: VMEM, out_shape),
        scratch_shapes=scratch,
        compiler_params=LIMIT,
    )


def shape(*sizes, kind=BF16):
    return jax.ShapeDtypeStruct(sizes, kind)


def grid(rows, columns):
    return (
        lax.broadcasted_iota(jnp.int32, (rows, columns), 0),
        lax.broadcasted_iota(jnp.int32, (rows, columns), 1),
    )


def ones(hit):
    return jnp.where(hit, 1.0, 0.0).astype(BF16)


def pick(index, cases, last):
    result = last
    for bound, value in reversed(cases):
        result = jnp.where(index < bound, value, result)
    return result


def far_slot(offset, row):
    count = pick(offset, [(1, 0), (2, 4), (4, 2)], 1)
    start = pick(offset, [(2, START[3]), (4, START[4])], START[5])
    return row < count, start + row


def near_slot(offset, row):
    own = row - HELD
    count = pick(offset, [(2, 0), (4, COUNT[1])], COUNT[2])
    start = pick(offset, [(4, START[1])], START[2])
    return (own >= 0) & (own < count), start + own


def held_slot(row):
    offset = pick(row, [(4, 1), (6, 2), (8, 3)], row - 4)
    return row < HELD, offset, pick(row, [(4, row), (8, row & 1)], 0)


def pack_kernel(key, value, query, cotangent, packed):
    for share in range(SHARES):
        columns = slice(share * SPAN, (share + 1) * SPAN)
        for part, source in enumerate((key, value, query, cotangent)):
            packed[share, part * SHARE : (part + 1) * SHARE, :] = source[:, columns]


def pack(*sources):
    return call(pack_kernel, shape(SHARES, 4 * SHARE, SPAN), count=4)(*sources)


def pool_kernel(spot, whole, pooled, far_send, to_next, to_prev):
    row, token = grid(OWN, TOKENS)
    weight = jnp.zeros((OWN, TOKENS), F32)
    for level in range(LEVELS):
        shift = 4 + level
        hit = row == START[level] + lax.shift_right_logical(token, shift)
        weight = jnp.where(hit, 1.0 / (1 << shift), weight)
    weight = weight.astype(BF16)
    for part in range(2):
        rows = whole[:, part * SHARE : (part + 1) * SHARE, :].reshape(TOKENS, SPAN)
        means = dot(weight, rows, NN).astype(BF16)
        pooled[:, part * SPAN : (part + 1) * SPAN] = means
        place = slice(TOKENS + part * COUNT[0], TOKENS + (part + 1) * COUNT[0])
        to_next[place, :] = means[: COUNT[0]]
        to_prev[place, :] = means[: COUNT[0]]
    row, column = grid(OWN, OWN)
    valid, source = far_slot((row >> 3) ^ (spot[0] >> 3), row & 7)
    far_send[...] = (
        dot(ones(valid & (column == source)), pooled[...], NN)
        .astype(BF16)
        .reshape(PEERS, FAR_ROWS, 2 * SPAN)
    )
    to_prev[:TOKENS, :] = whole[: SHARES // 2, : 2 * SHARE, :].reshape(TOKENS, SPAN)
    to_next[:TOKENS, :] = whole[SHARES // 2 :, : 2 * SHARE, :].reshape(TOKENS, SPAN)


def near_kernel(spot, pooled, far, near_send):
    far_at, near_at = spot[0] >> 3, spot[0] & 7
    row, column = grid(NEAR, OWN)
    inside = row & (NEAR_ROWS - 1)
    valid, source = near_slot((row >> 5) ^ near_at, inside)
    own = dot(ones(valid & (column == source)), pooled[...], NN)
    valid, offset, place = held_slot(inside)
    hit = valid & (column == (offset ^ far_at) * FAR_ROWS + place)
    held = dot(ones(hit), far[...].reshape(PEERS * FAR_ROWS, 2 * SPAN), NN)
    near_send[...] = (own + held).astype(BF16).reshape(PEERS, NEAR_ROWS, 2 * SPAN)


def far_kernel(spot, near, far_send):
    row, column = grid(OWN, NEAR)
    valid, offset, place = held_slot(column & (NEAR_ROWS - 1))
    hit = valid & (offset == ((row >> 3) ^ (spot[0] >> 3))) & (place == (row & 7))
    far_send[...] = (
        dot(ones(hit), near[...].reshape(NEAR, 2 * SPAN), NN)
        .astype(BF16)
        .reshape(PEERS, FAR_ROWS, 2 * SPAN)
    )


def attend_kernel(
    spot, whole, low, high, near_rows,
    attended, query_grad, centre, to_prev, to_next, near_send,
    keys, values, key_grad, value_grad, far_keys, far_values,
):
    factor = HEAD_DIM ** (-0.5)
    binary = factor * math.log2(math.e)
    position = spot[0]
    bias_low = jnp.where(position == 0, -1e30, 0.0).astype(F32)
    bias_high = jnp.where(position == spot[1] - 1, -1e30, 0.0).astype(F32)
    even = (position & 1) == 0
    row = lax.broadcasted_iota(jnp.int32, (COARSE, LEAF), 0)
    inside = row & (NEAR_ROWS - 1)
    valid, _ = near_slot((row >> 5) ^ (position & 7), inside)
    valid = valid | (inside < HELD) | (row >= NEAR)
    far_bias = jnp.where(valid, math.log2(RATIO), -1e30)
    for head in range(2):
        columns = slice(head * HEAD_DIM, (head + 1) * HEAD_DIM)
        for part, store, far_store in ((0, keys, far_keys), (1, values, far_values)):
            rows = slice(part * SHARE, (part + 1) * SHARE)
            place = slice(part * SPAN + head * HEAD_DIM, part * SPAN + (head + 1) * HEAD_DIM)
            level_zero = slice(TOKENS + part * COUNT[0], TOKENS + (part + 1) * COUNT[0])
            half = SHARES // 2
            store[:LEAF, :] = (
                low[:TOKENS, columns].reshape(half, 2 * SHARE, HEAD_DIM)[:, rows].reshape(LEAF, HEAD_DIM)
            )
            store[LEAF : LEAF + TOKENS, :] = whole[:, rows, columns].reshape(TOKENS, HEAD_DIM)
            store[LEAF + TOKENS :, :] = (
                high[:TOKENS, columns].reshape(half, 2 * SHARE, HEAD_DIM)[:, rows].reshape(LEAF, HEAD_DIM)
            )
            far_store[:NEAR, :] = near_rows[:, :, place].reshape(NEAR, HEAD_DIM)

            @pl.when(even)
            def _():
                far_store[NEAR:, :] = high[level_zero, columns]

            @pl.when(jnp.logical_not(even))
            def _():
                far_store[NEAR:, :] = low[level_zero, columns]

        far_key = far_keys[...]
        far_value = far_values[...]
        key_t = jnp.transpose(keys[...])
        value_t = jnp.transpose(values[...])
        far_key_t = jnp.transpose(far_key)
        far_value_t = jnp.transpose(far_value)
        far_key_grad = jnp.zeros((COARSE, HEAD_DIM), F32)
        far_value_grad = jnp.zeros((COARSE, HEAD_DIM), F32)
        for block in range(2):
            query = whole[4 * block : 4 * block + 4, 2 * SHARE : 3 * SHARE, columns].reshape(LEAF, HEAD_DIM)
            grad = whole[4 * block : 4 * block + 4, 3 * SHARE :, columns].reshape(LEAF, HEAD_DIM)
            window = slice(block * LEAF, block * LEAF + 3 * LEAF)
            near = dot(keys[window, :], query, NT) * binary
            if block == 0:
                near = jnp.concatenate([near[:LEAF] + bias_low, near[LEAF:]], axis=0)
            else:
                near = jnp.concatenate([near[: 2 * LEAF], near[2 * LEAF :] + bias_high], axis=0)
            far = dot(far_key, query, NT) * binary + far_bias
            top = jnp.maximum(
                jnp.max(near, axis=0, keepdims=True), jnp.max(far, axis=0, keepdims=True)
            )
            near = jnp.exp2(near - top)
            far = jnp.exp2(far - top)
            total = jnp.sum(near, axis=0, keepdims=True) + jnp.sum(far, axis=0, keepdims=True)
            inverse = 1.0 / total
            near = near * inverse
            far = far * inverse
            near_low = near.astype(BF16)
            far_low = far.astype(BF16)
            mixed_t = dot(value_t[:, window], near_low, NN) + dot(far_value_t, far_low, NN)
            grad_t = jnp.transpose(grad.astype(F32))
            delta = jnp.sum(grad_t * mixed_t, axis=0, keepdims=True)
            near_score = (near * (dot(values[window, :], grad, NT) - delta)).astype(BF16)
            far_score = (far * (dot(far_value, grad, NT) - delta)).astype(BF16)
            query_t = dot(key_t[:, window], near_score, NN) + dot(far_key_t, far_score, NN)
            out = slice(block * LEAF, (block + 1) * LEAF)
            attended[out, columns] = jnp.transpose(mixed_t).astype(BF16)
            query_grad[out, columns] = jnp.transpose(query_t * factor).astype(BF16)
            near_key_grad = dot(near_score, query, NN) * factor
            near_value_grad = dot(near_low, grad, NN)
            far_key_grad = far_key_grad + dot(far_score, query, NN) * factor
            far_value_grad = far_value_grad + dot(far_low, grad, NN)
            if block == 0:
                key_grad[: 3 * LEAF, :] = near_key_grad
                value_grad[: 3 * LEAF, :] = near_value_grad
            else:
                key_grad[LEAF : 3 * LEAF, :] += near_key_grad[: 2 * LEAF]
                value_grad[LEAF : 3 * LEAF, :] += near_value_grad[: 2 * LEAF]
                key_grad[3 * LEAF :, :] = near_key_grad[2 * LEAF :]
                value_grad[3 * LEAF :, :] = near_value_grad[2 * LEAF :]
        for part, store, far_grad in ((0, key_grad, far_key_grad), (1, value_grad, far_value_grad)):
            place = slice(part * SPAN + head * HEAD_DIM, part * SPAN + (head + 1) * HEAD_DIM)
            to_prev[:LEAF, place] = store[:LEAF, :].astype(BF16)
            centre[:, place] = store[LEAF : LEAF + TOKENS, :]
            to_next[:LEAF, place] = store[LEAF + TOKENS :, :].astype(BF16)
            far_low = far_grad.astype(BF16)
            to_prev[LEAF:, place] = far_low[NEAR:]
            to_next[LEAF:, place] = far_low[NEAR:]
            near_send[:, :, place] = far_low[:NEAR].reshape(PEERS, NEAR_ROWS, HEAD_DIM)


def finish_kernel(spot, centre, from_prev, from_next, near, far, key_grad, value_grad, level_zero):
    position = spot[0]

    @pl.when((position & 1) == 0)
    def _():
        level_zero[...] = from_next[LEAF:, :]

    @pl.when((position & 1) == 1)
    def _():
        level_zero[...] = from_prev[LEAF:, :]

    token, column = grid(TOKENS, COUNT[0])
    weight = jnp.where((token >> 4) == column, 1.0 / RATIO, 0.0).astype(BF16)
    spread = centre[...] + dot(weight, level_zero[...], NN)
    token, column = grid(TOKENS, NEAR)
    offset = (column >> 5) ^ (position & 7)
    own = (column & (NEAR_ROWS - 1)) - HELD
    hit_one = (offset >= 2) & (offset < 4) & ((token >> 5) == own)
    hit_two = (offset >= 4) & ((token >> 6) == own)
    weight = jnp.where(hit_one, 1.0 / 32, jnp.where(hit_two, 1.0 / 64, 0.0)).astype(BF16)
    spread = spread + dot(weight, near[...].reshape(NEAR, 2 * SPAN), NN)
    token, column = grid(TOKENS, OWN)
    offset = (column >> 3) ^ (position >> 3)
    place = column & 7
    hit_three = (offset == 1) & ((token >> 7) == place)
    hit_four = (offset >= 2) & (offset < 4) & ((token >> 8) == place)
    hit_five = (offset >= 4) & (place == 0)
    weight = jnp.where(hit_three, 1.0 / 128, jnp.where(hit_four, 1.0 / 256, 0.0))
    weight = jnp.where(hit_five, 1.0 / 512, weight).astype(BF16)
    spread = spread + dot(weight, far[...].reshape(OWN, 2 * SPAN), NN)
    low = spread[:LEAF] + from_prev[:LEAF, :].astype(F32)
    high = spread[LEAF:] + from_next[:LEAF, :].astype(F32)
    key_grad[:LEAF, :] = low[:, :SPAN].astype(BF16)
    key_grad[LEAF:, :] = high[:, :SPAN].astype(BF16)
    value_grad[:LEAF, :] = low[:, SPAN:].astype(BF16)
    value_grad[LEAF:, :] = high[:, SPAN:].astype(BF16)


FAR_GROUPS = [[far * PEERS + near for far in range(PEERS)] for near in range(PEERS)]
NEAR_GROUPS = [[far * PEERS + near for near in range(PEERS)] for far in range(PEERS)]


def body(query, key, value, cotangent):
    devices = lax.axis_size("context")
    position = lax.axis_index("context")
    spot = jnp.stack([position, jnp.int32(devices)])

    def ring(block, step):
        pairs = [(source, (source + step) % devices) for source in range(devices)]
        return lax.ppermute(block, "context", pairs)

    def exchange(block, groups):
        return lax.all_to_all(block, "context", 0, 0, axis_index_groups=groups)

    whole = lax.all_to_all(pack(key, value, query, cotangent), "head", 0, 0)
    slots = shape(PEERS, NEAR_ROWS, 2 * SPAN)
    far_slots = shape(PEERS, FAR_ROWS, 2 * SPAN)
    rim = shape(TOKENS + 2 * COUNT[0], SPAN)
    pooled, far_send, to_next, to_prev = call(
        pool_kernel, (shape(OWN, 2 * SPAN), far_slots, rim, rim), specs=[SMEM, VMEM]
    )(spot, whole)
    low = ring(to_next, 1)
    high = ring(to_prev, -1)
    far = exchange(far_send, FAR_GROUPS)
    near_send = call(near_kernel, slots, specs=[SMEM] + [VMEM] * 2)(spot, pooled, far)
    near = exchange(near_send, NEAR_GROUPS)
    rim_grad = shape(LEAF + COUNT[0], 2 * SPAN)
    attended, query_grad, centre, to_prev, to_next, near_send = call(
        attend_kernel,
        (
            shape(TOKENS, SPAN),
            shape(TOKENS, SPAN),
            shape(TOKENS, 2 * SPAN, kind=F32),
            rim_grad,
            rim_grad,
            slots,
        ),
        [
            pltpu.VMEM((2 * LEAF + TOKENS, HEAD_DIM), BF16),
            pltpu.VMEM((2 * LEAF + TOKENS, HEAD_DIM), BF16),
            pltpu.VMEM((2 * LEAF + TOKENS, HEAD_DIM), F32),
            pltpu.VMEM((2 * LEAF + TOKENS, HEAD_DIM), F32),
            pltpu.VMEM((COARSE, HEAD_DIM), BF16),
            pltpu.VMEM((COARSE, HEAD_DIM), BF16),
        ],
        [SMEM] + [VMEM] * 4,
    )(spot, whole, low, high, near)
    from_next = ring(to_prev, -1)
    from_prev = ring(to_next, 1)
    near = exchange(near_send, NEAR_GROUPS)
    far_send = call(far_kernel, far_slots, specs=[SMEM, VMEM])(spot, near)
    far = exchange(far_send, FAR_GROUPS)
    key_grad, value_grad = call(
        finish_kernel,
        (shape(TOKENS, SPAN), shape(TOKENS, SPAN)),
        [pltpu.VMEM((COUNT[0], 2 * SPAN), BF16)],
        [SMEM] + [VMEM] * 5,
    )(spot, centre, from_prev, from_next, near, far)
    return attended, query_grad, key_grad, value_grad


def solution(mesh):
    spec = P(("context", "head"), None)
    out = P("context", "head")
    return jax.shard_map(
        body, mesh=mesh, in_specs=(spec,) * 4, out_specs=(out,) * 4, check_vma=False
    )
```

time: 141 us -> 137 us (0.972)
  starting transfers between devices: 72.1 us -> 41.2 us
  blocking collectives: 14.7 us -> 31.5 us
  Pallas kernels: 8.81 us -> 14 us
  waiting for transfers between devices: 40 us -> 45.1 us
    ppermute x12 -> x0, starting transfers between devices: 52.7 us -> none  [partner(): return lax.ppermute(block, 'context', pairs)]
    ppermute x12 -> x0, waiting for transfers between devices: 40 us -> none  [partner(): return lax.ppermute(block, 'context', pairs)]
    all_to_all x1 -> x4, waiting for transfers between devices: 0.01 us -> 37.8 us  [the longest x3 22 us: exchange(): return lax.all_to_all(block, 'context', 0, 0, axis_index_groups=groups)]
    all_to_all x1 -> x4, starting transfers between devices: 3.49 us -> 25.3 us  [the longest x3 20.8 us: exchange(): return lax.all_to_all(block, 'context', 0, 0, axis_index_groups=groups)]
    all_to_all x1, blocking collectives: 14.7 us -> 31.5 us  [exchange(): return lax.all_to_all(block, 'context', 0, 0, axis_index_groups=groups)]
    ppermute x4, waiting for transfers between devices: 0.01 us -> 7.29 us  [ring(): return lax.ppermute(block, 'context', pairs)]
    pallas_call x4 -> x5, Pallas kernels: 2.23 us -> 6.7 us  [the longest x1 1.9 us: body(): call(finish_kernel, (shape(TOKENS, SPAN), shape(TOKENS, SPAN)), [pltpu.VM...]
    unnamed x18 -> x8, local copies, waits for them, and re-layouts: 1.92 us -> 3.79 us
  transfers between devices with their start and end apart: 17 -> 8, of which waited for: 10 -> 6; matrix products, arithmetic and copies ran while one was open for 1% -> 0% of each run, Pallas kernels for 1% -> 1%
where the time goes in v2:
time: 137 us; the launch traced here: 136 us
  waiting for transfers between devices  45.1 us (33%)
  starting transfers between devices  41.2 us (30%)
  blocking collectives  31.5 us (23%)
  Pallas kernels  14 us (10%)
  local copies, waits for them, and re-layouts  3.79 us (3%)
    all_to_all x1, blocking collectives, exchange(): return lax.all_to_all(block, 'context', 0, 0, axis_index_groups=groups)  31.5 us
    all_to_all x3, waiting for transfers between devices, exchange(): return lax.all_to_all(block, 'context', 0, 0, axis_index_groups=groups)  22 us
    all_to_all x3, starting transfers between devices, exchange(): return lax.all_to_all(block, 'context', 0, 0, axis_index_groups=groups)  20.8 us
    all_to_all x1, waiting for transfers between devices, body(): whole = lax.all_to_all(pack(key, value, query, cotangent), 'head', 0, 0)  15.9 us
    ppermute x4, starting transfers between devices, ring(): return lax.ppermute(block, 'context', pairs)  15.9 us
    ppermute x4, waiting for transfers between devices, ring(): return lax.ppermute(block, 'context', pairs)  7.29 us
    pallas_call x1, Pallas kernels, body(): call(attend_kernel, (shape(TOKENS, SPAN), shape(TOKENS, SPAN), shape(TOKE...  7.29 us
    all_to_all x1, starting transfers between devices, body(): whole = lax.all_to_all(pack(key, value, query, cotangent), 'head', 0, 0)  4.47 us
  transfers between devices with their start and end apart: 8, of which 6 were waited for; matrix products, arithmetic and copies ran while one was open for 0% of the time, Pallas kernels for 1%

profile of v2, /device:TPU:2, one launch (start us, length us, event | category | flops | bytes accessed | tf_op | source)
XLA Modules:
  0.0 136.4 jit_solution(8460497403608749836)
XLA Ops:
  0.6 0.0 copy-start
  0.6 0.9 copy-done
  1.6 0.0 copy-start.1
  1.6 0.9 copy-done.1
  2.5 0.0 copy-start.2
  2.5 0.9 copy-done.2
  3.5 0.0 copy-start.3
  3.5 0.9 copy-done.3
  4.4 1.1 shard_map.75
  5.5 4.5 %all-to-all-start = ((bf16[8,256,256]{2,1,0:T(8,128)(2,1)}), bf16[8,256,256]{2,1,0:T(8,128)(2,1)S(1)}, u32[]{:S(2)}, u32[]{:S(2)}) async-start(bf16[8,256,256]{2,1,0:T(8,128)(2,1)} %shard_map.75), calls=%async_computation | async-start | bytes 2097152 | tf_op jit(solution)/shard_map/all_to_all | solution.py:306
  10.0 0.1 pad_add_fusion.spot
  10.0 15.9 %all-to-all-done.whole = bf16[8,256,256]{2,1,0:T(8,128)(2,1)S(1)} async-done(((bf16[8,256,256]{2,1,0:T(8,128)(2,1)}), bf16[8,256,256]{2,1,0:T(8,128)(2,1)S(1)}, u32[]{:S(2)}, u32[]{:S(2)}) %all-to-all-start) | async-done | bytes 1048608 | tf_op jit(solution)/shard_map/all_to_all | solution.py:306
  25.9 0.9 shard_map.76
  26.8 31.5 %all_to_all.25.far = bf16[8,8,512]{2,1,0:T(8,128)(2,1)S(1)} all-to-all(bf16[8,8,512]{2,1,0:T(8,128)(2,1)S(1)} %get-tuple-element.19), channel_id=1, replica_groups={{0,64,128,192,256,320,384,448},{8,72,136,200,264,328,392,456},{16,80,14..., dimensions={0} | all-to-all | bytes 131072 | tf_op jit(solution)/shard_map/all_to_all | solution.py:304
  58.3 1.5 %shard_map.77 = bf16[8,32,512]{2,1,0:T(8,128)(2,1)} custom-call(s32[2]{0:T(128)S(1)} %pad_add_fusion.spot, bf16[64,512]{1,0:T(8,128)(2,1)S(1)} %get-tuple-element.18.pooled, bf16[8,8,512]{2,1,0:T(8,128)(2,1)S(1)} %all_to_all.25.far), custom_call_target="tpu_custom_call" | custom-call | tf_op jit(solution)/shard_map/pallas_call | solution.py:316
  59.8 5.0 %all-to-all-start.2 = ((bf16[8,32,512]{2,1,0:T(8,128)(2,1)}), bf16[8,32,512]{2,1,0:T(8,128)(2,1)S(1)}, u32[]{:S(2)}, u32[]{:S(2)}) async-start(bf16[8,32,512]{2,1,0:T(8,128)(2,1)} %shard_map.77), calls=%async_computation.2 | async-start | bytes 524288 | tf_op jit(solution)/shard_map/all_to_all | solution.py:304
  64.9 3.9 %collective-permute-start = (bf16[576,256]{1,0:T(8,128)(2,1)S(1)}, bf16[576,256]{1,0:T(8,128)(2,1)S(1)}, u32[]{:S(2)}, u32[]{:S(2)}) collective-permute-start(bf16[576,256]{1,0:T(8,128)(2,1)S(1)} %get-tuple-element.16), channel_id=1, source_target_pairs={{0,8},{8,16},{16,24},{24,32},{32,40},{40,48},{48,56},{56,64},{64,7... | collective-permute-start | bytes 884744 | tf_op jit(solution)/shard_map/ppermute | solution.py:301
  68.8 4.0 %collective-permute-start.1 = (bf16[576,256]{1,0:T(8,128)(2,1)S(1)}, bf16[576,256]{1,0:T(8,128)(2,1)S(1)}, u32[]{:S(2)}, u32[]{:S(2)}) collective-permute-start(bf16[576,256]{1,0:T(8,128)(2,1)S(1)} %get-tuple-element.17), channel_id=1, source_target_pairs={{0,504},{8,0},{16,8},{24,16},{32,24},{40,32},{48,40},{56,48},{64,5... | collective-permute-start | bytes 884744 | tf_op jit(solution)/shard_map/ppermute | solution.py:301
  72.8 3.0 %collective-permute-done.low = bf16[576,256]{1,0:T(8,128)(2,1)S(1)} collective-permute-done((bf16[576,256]{1,0:T(8,128)(2,1)S(1)}, bf16[576,256]{1,0:T(8,128)(2,1)S(1)}, u32[]{:S(2)}, u32[]{:S(2)}) %collective-permute-start) | collective-permute-done | bytes 294944 | tf_op jit(solution)/shard_map/ppermute | solution.py:301
  75.8 4.3 %collective-permute-done.1.high = bf16[576,256]{1,0:T(8,128)(2,1)S(1)} collective-permute-done((bf16[576,256]{1,0:T(8,128)(2,1)S(1)}, bf16[576,256]{1,0:T(8,128)(2,1)S(1)}, u32[]{:S(2)}, u32[]{:S(2)}) %collective-permute-start.1) | collective-permute-done | bytes 294944 | tf_op jit(solution)/shard_map/ppermute | solution.py:301
  80.1 0.2 all-to-all-done.2.near_rows
  80.3 7.3 %shard_map.78 = (bf16[512,256]{1,0:T(8,128)(2,1)}, bf16[512,256]{1,0:T(8,128)(2,1)}, f32[512,512]{1,0:T(8,128)S(1)}, bf16[288,512]{1,0:T(8,128)(2,1)S(1)}, bf16[...) custom-call(s32[2]{0:T(128)S(1)} %pad_add_fusion.spot, bf16[8,256,256]{2,1,0:T(8,128)(2,1)S(1)} %all-to-all-done.whole, ...), custom_call_target="tpu_custom_call" | custom-call | tf_op jit(solution)/shard_map/pallas_call | solution.py:319
  87.6 8.9 %all-to-all-start.3 = ((bf16[8,32,512]{2,1,0:T(8,128)(2,1)}), bf16[8,32,512]{2,1,0:T(8,128)(2,1)S(1)}, u32[]{:S(2)}, u32[]{:S(2)}) async-start(bf16[8,32,512]{2,1,0:T(8,128)(2,1)} %get-tuple-element.25), calls=%async_computation.3 | async-start | bytes 524288 | tf_op jit(solution)/shard_map/all_to_all | solution.py:304
  96.5 3.9 %collective-permute-start.2 = (bf16[288,512]{1,0:T(8,128)(2,1)S(1)}, bf16[288,512]{1,0:T(8,128)(2,1)S(1)}, u32[]{:S(2)}, u32[]{:S(2)}) collective-permute-start(bf16[288,512]{1,0:T(8,128)(2,1)S(1)} %get-tuple-element.23), channel_id=1, source_target_pairs={{0,8},{8,16},{16,24},{24,32},{32,40},{40,48},{48,56},{56,64},{64,7... | collective-permute-start | bytes 884744 | tf_op jit(solution)/shard_map/ppermute | solution.py:301
  100.4 4.0 %collective-permute-start.3 = (bf16[288,512]{1,0:T(8,128)(2,1)S(1)}, bf16[288,512]{1,0:T(8,128)(2,1)S(1)}, u32[]{:S(2)}, u32[]{:S(2)}) collective-permute-start(bf16[288,512]{1,0:T(8,128)(2,1)S(1)} %get-tuple-element.24), channel_id=1, source_target_pairs={{0,504},{8,0},{16,8},{24,16},{32,24},{40,32},{48,40},{56,48},{64,5... | collective-permute-start | bytes 884744 | tf_op jit(solution)/shard_map/ppermute | solution.py:301
  104.5 8.2 %all-to-all-done.3.near = bf16[8,32,512]{2,1,0:T(8,128)(2,1)S(1)} async-done(((bf16[8,32,512]{2,1,0:T(8,128)(2,1)}), bf16[8,32,512]{2,1,0:T(8,128)(2,1)S(1)}, u32[]{:S(2)}, u32[]{:S(2)}) %all-to-all-start.3) | async-done | bytes 262176 | tf_op jit(solution)/shard_map/all_to_all | solution.py:304
  112.6 1.3 shard_map.79
  114.0 6.9 %all-to-all-start.4 = ((bf16[8,8,512]{2,1,0:T(8,128)(2,1)}), bf16[8,8,512]{2,1,0:T(8,128)(2,1)S(1)}, u32[]{:S(2)}, u32[]{:S(2)}) async-start(bf16[8,8,512]{2,1,0:T(8,128)(2,1)} %shard_map.79), calls=%async_computation.4 | async-start | bytes 131072 | tf_op jit(solution)/shard_map/all_to_all | solution.py:304
  120.9 0.0 collective-permute-done.2.from_prev
  120.9 0.0 collective-permute-done.3.from_next
  120.9 13.6 %all-to-all-done.4.far = bf16[8,8,512]{2,1,0:T(8,128)(2,1)S(1)} async-done(((bf16[8,8,512]{2,1,0:T(8,128)(2,1)}), bf16[8,8,512]{2,1,0:T(8,128)(2,1)S(1)}, u32[]{:S(2)}, u32[]{:S(2)}) %all-to-all-start.4) | async-done | bytes 65568 | tf_op jit(solution)/shard_map/all_to_all | solution.py:304
  134.5 1.9 %shard_map.80 = (bf16[512,256]{1,0:T(8,128)(2,1)}, bf16[512,256]{1,0:T(8,128)(2,1)}) custom-call(s32[2]{0:T(128)S(1)} %pad_add_fusion.spot, f32[512,512]{1,0:T(8,128)S(1)} %get-tuple-element.22.centre, bf16[288,512]{1,0:T(8,128)(2,1)S(1)} %collective-permute-done.2.from_prev, bf16[288,512]{1,0:T(8,128)(2,1)S(1)} %collective-permute-done.3.from_next, ...), custom_call_target="tpu_custom_call" | custom-call | tf_op jit(solution)/shard_map/pallas_call | solution.py:344
Async XLA Ops:
  0.6 1.0 copy-start
  1.6 0.9 copy-start.1
  2.5 0.9 copy-start.2
  3.5 0.9 copy-start.3
  5.5 20.4 %all-to-all-start = ((bf16[8,256,256]{2,1,0:T(8,128)(2,1)}), bf16[8,256,256]{2,1,0:T(8,128)(2,1)S(1)}, u32[]{:S(2)}, u32[]{:S(2)}) async-start(bf16[8,256,256]{2,1,0:T(8,128)(2,1)} %shard_map.75), calls=%async_computation | async-start | bytes 2097152 | tf_op jit(solution)/shard_map/all_to_all | solution.py:306
  59.8 20.5 %all-to-all-start.2 = ((bf16[8,32,512]{2,1,0:T(8,128)(2,1)}), bf16[8,32,512]{2,1,0:T(8,128)(2,1)S(1)}, u32[]{:S(2)}, u32[]{:S(2)}) async-start(bf16[8,32,512]{2,1,0:T(8,128)(2,1)} %shard_map.77), calls=%async_computation.2 | async-start | bytes 524288 | tf_op jit(solution)/shard_map/all_to_all | solution.py:304
  64.9 10.9 %collective-permute-start = (bf16[576,256]{1,0:T(8,128)(2,1)S(1)}, bf16[576,256]{1,0:T(8,128)(2,1)S(1)}, u32[]{:S(2)}, u32[]{:S(2)}) collective-permute-start(bf16[576,256]{1,0:T(8,128)(2,1)S(1)} %get-tuple-element.16), channel_id=1, source_target_pairs={{0,8},{8,16},{16,24},{24,32},{32,40},{40,48},{48,56},{56,64},{64,7... | collective-permute-start | bytes 884744 | tf_op jit(solution)/shard_map/ppermute | solution.py:301
  68.8 11.3 %collective-permute-start.1 = (bf16[576,256]{1,0:T(8,128)(2,1)S(1)}, bf16[576,256]{1,0:T(8,128)(2,1)S(1)}, u32[]{:S(2)}, u32[]{:S(2)}) collective-permute-start(bf16[576,256]{1,0:T(8,128)(2,1)S(1)} %get-tuple-element.17), channel_id=1, source_target_pairs={{0,504},{8,0},{16,8},{24,16},{32,24},{40,32},{48,40},{56,48},{64,5... | collective-permute-start | bytes 884744 | tf_op jit(solution)/shard_map/ppermute | solution.py:301
  87.6 25.1 %all-to-all-start.3 = ((bf16[8,32,512]{2,1,0:T(8,128)(2,1)}), bf16[8,32,512]{2,1,0:T(8,128)(2,1)S(1)}, u32[]{:S(2)}, u32[]{:S(2)}) async-start(bf16[8,32,512]{2,1,0:T(8,128)(2,1)} %get-tuple-element.25), calls=%async_computation.3 | async-start | bytes 524288 | tf_op jit(solution)/shard_map/all_to_all | solution.py:304
  96.5 24.3 %collective-permute-start.2 = (bf16[288,512]{1,0:T(8,128)(2,1)S(1)}, bf16[288,512]{1,0:T(8,128)(2,1)S(1)}, u32[]{:S(2)}, u32[]{:S(2)}) collective-permute-start(bf16[288,512]{1,0:T(8,128)(2,1)S(1)} %get-tuple-element.23), channel_id=1, source_target_pairs={{0,8},{8,16},{16,24},{24,32},{32,40},{40,48},{48,56},{56,64},{64,7... | collective-permute-start | bytes 884744 | tf_op jit(solution)/shard_map/ppermute | solution.py:301
  100.4 20.4 %collective-permute-start.3 = (bf16[288,512]{1,0:T(8,128)(2,1)S(1)}, bf16[288,512]{1,0:T(8,128)(2,1)S(1)}, u32[]{:S(2)}, u32[]{:S(2)}) collective-permute-start(bf16[288,512]{1,0:T(8,128)(2,1)S(1)} %get-tuple-element.24), channel_id=1, source_target_pairs={{0,504},{8,0},{16,8},{24,16},{32,24},{40,32},{48,40},{56,48},{64,5... | collective-permute-start | bytes 884744 | tf_op jit(solution)/shard_map/ppermute | solution.py:301
  114.0 20.5 %all-to-all-start.4 = ((bf16[8,8,512]{2,1,0:T(8,128)(2,1)}), bf16[8,8,512]{2,1,0:T(8,128)(2,1)S(1)}, u32[]{:S(2)}, u32[]{:S(2)}) async-start(bf16[8,8,512]{2,1,0:T(8,128)(2,1)} %shard_map.79), calls=%async_computation.4 | async-start | bytes 131072 | tf_op jit(solution)/shard_map/all_to_all | solution.py:304

commit v3 on v1

v3 whole, which is shorter than its diff:
```python
import math

import jax
import jax.numpy as jnp
from jax import lax
from jax.experimental import pallas as pl
from jax.experimental.pallas import tpu as pltpu
from jax.sharding import PartitionSpec as P

HEAD_DIM = 128
LEAF = 256
RATIO = 16
TOKENS = 512
SPAN = 256
SHARES = 8
SHARE = 64
LEVELS = 6
OWN = 64
COUNT = [32 >> level for level in range(LEVELS)]
START = [64 - (64 >> level) for level in range(LEVELS)]
PEERS = 64
SLOT = 8
SLOTS = PEERS * SLOT
FAR = 4 * 32
COARSE = FAR + 2 * COUNT[1] + COUNT[0]
F32 = jnp.float32
BF16 = jnp.bfloat16
VMEM = pl.BlockSpec(memory_space=pltpu.VMEM)
SMEM = pl.BlockSpec(memory_space=pltpu.SMEM)
ANY = pl.BlockSpec(memory_space=pl.ANY)
LIMIT = pltpu.CompilerParams(vmem_limit_bytes=24 * 1024 * 1024)
NN = ((1,), (0,))
NT = ((1,), (1,))


def dot(left, right, over):
    return lax.dot_general(left, right, (over, ((), ())), preferred_element_type=F32)


def call(kernel, out_shape, scratch=(), specs=None, count=1):
    return pl.pallas_call(
        kernel,
        out_shape=out_shape,
        in_specs=specs or [VMEM] * count,
        out_specs=jax.tree.map(lambda _: VMEM, out_shape),
        scratch_shapes=scratch,
        compiler_params=LIMIT,
    )


def shape(*sizes, kind=BF16):
    return jax.ShapeDtypeStruct(sizes, kind)


def grid(rows, columns):
    return (
        lax.broadcasted_iota(jnp.int32, (rows, columns), 0),
        lax.broadcasted_iota(jnp.int32, (rows, columns), 1),
    )


def ones(hit):
    return jnp.where(hit, 1.0, 0.0).astype(BF16)


def pick(index, cases, last):
    result = last
    for bound, value in reversed(cases):
        result = jnp.where(index < bound, value, result)
    return result


def slot_row(offset, row):
    count = pick(offset, [(4, 0), (8, COUNT[2]), (16, COUNT[3]), (32, COUNT[4])], COUNT[5])
    start = pick(offset, [(8, START[2]), (16, START[3]), (32, START[4])], START[5])
    return row < count, start + row


def slot_of(row):
    offset = pick(row, [(32, 4 + (row >> 3)), (64, row >> 2), (96, (row >> 1) - 16)], row - 64)
    return offset, pick(row, [(32, row & 7), (64, row & 3), (96, row & 1)], 0)


def pack_kernel(key, value, query, cotangent, packed, rows, held, arrived, left):
    incoming = [
        pltpu.make_async_copy(source, rows.at[part], arrived.at[part])
        for part, source in enumerate((key, value, query, cotangent))
    ]
    for copy in incoming:
        copy.start()
    outgoing = []
    for part, copy in enumerate(incoming):
        copy.wait()
        place = slice(part * SHARE, (part + 1) * SHARE)
        for share in range(SHARES):
            held[share, place, :] = rows[part, :, share * SPAN : (share + 1) * SPAN]
        outgoing.append(
            pltpu.make_async_copy(held.at[:, place, :], packed.at[:, place, :], left.at[part])
        )
        outgoing[-1].start()
    for copy in outgoing:
        copy.wait()


def pack(*sources):
    return pl.pallas_call(
        pack_kernel,
        out_shape=shape(SHARES, 4 * SHARE, SPAN),
        in_specs=[ANY] * 4,
        out_specs=ANY,
        scratch_shapes=[
            pltpu.VMEM((4, SHARE, SHARES * SPAN), BF16),
            pltpu.VMEM((SHARES, 4 * SHARE, SPAN), BF16),
            pltpu.SemaphoreType.DMA((4,)),
            pltpu.SemaphoreType.DMA((4,)),
        ],
        compiler_params=pltpu.CompilerParams(vmem_limit_bytes=60 * 1024 * 1024),
    )(*sources)


def pool_kernel(spot, whole, level_one, slots, to_next, to_prev):
    row, token = grid(OWN, TOKENS)
    weight = jnp.zeros((OWN, TOKENS), F32)
    for level in range(LEVELS):
        shift = 4 + level
        hit = row == START[level] + lax.shift_right_logical(token, shift)
        weight = jnp.where(hit, 1.0 / (1 << shift), weight)
    weight = weight.astype(BF16)
    row, column = grid(SLOTS, OWN)
    valid, source = slot_row((row >> 3) ^ spot[0], row & 7)
    spread = ones(valid & (column == source))
    for part in range(2):
        rows = whole[:, part * SHARE : (part + 1) * SHARE, :].reshape(TOKENS, SPAN)
        means = dot(weight, rows, NN).astype(BF16)
        columns = slice(part * SPAN, (part + 1) * SPAN)
        level_one[:, columns] = means[START[1] : START[1] + COUNT[1]]
        place = slice(TOKENS + part * COUNT[0], TOKENS + (part + 1) * COUNT[0])
        to_next[place, :] = means[: COUNT[0]]
        to_prev[place, :] = means[: COUNT[0]]
        slots[:, :, columns] = dot(spread, means, NN).astype(BF16).reshape(PEERS, SLOT, SPAN)
    to_prev[:TOKENS, :] = whole[: SHARES // 2, : 2 * SHARE, :].reshape(TOKENS, SPAN)
    to_next[:TOKENS, :] = whole[SHARES // 2 :, : 2 * SHARE, :].reshape(TOKENS, SPAN)


def select_kernel(spot, _after, gather, scatter):
    row, column = grid(FAR, SLOTS)
    offset, place = slot_of(row)
    gather[...] = ones(column == (offset ^ spot[0]) * SLOT + place)
    row, column = grid(SLOTS, FAR)
    offset, place = slot_of(column)
    scatter[...] = ones(row == (offset ^ spot[0]) * SLOT + place)


def part_rows(part):
    return slice(part * SHARE, (part + 1) * SHARE)


def part_columns(part, head):
    return slice(part * SPAN + head * HEAD_DIM, part * SPAN + (head + 1) * HEAD_DIM)


def load(whole, part, block, columns):
    half = SHARES // 2
    return whole[block * half : (block + 1) * half, part_rows(part), columns].reshape(LEAF, HEAD_DIM)


def ext(whole, low, high, part, columns, store):
    half = SHARES // 2
    for place, rim in ((0, low), (LEAF + TOKENS, high)):
        store[place : place + LEAF, :] = (
            rim[:TOKENS, columns]
            .reshape(half, 2 * SHARE, HEAD_DIM)[:, part_rows(part)]
            .reshape(LEAF, HEAD_DIM)
        )
    store[LEAF : LEAF + TOKENS, :] = whole[:, part_rows(part), columns].reshape(TOKENS, HEAD_DIM)


def near_scores(spot, keys, query, block):
    window = slice(block * LEAF, block * LEAF + 3 * LEAF)
    near = dot(keys[window, :], query, NT) * (HEAD_DIM ** (-0.5) * math.log2(math.e))
    if block == 0:
        bias = jnp.where(spot[0] == 0, -1e30, 0.0).astype(F32)
        return jnp.concatenate([near[:LEAF] + bias, near[LEAF:]], axis=0)
    bias = jnp.where(spot[0] == spot[1] - 1, -1e30, 0.0).astype(F32)
    return jnp.concatenate([near[: 2 * LEAF], near[2 * LEAF :] + bias], axis=0)


def forward_kernel(
    spot, whole, low, high, slots, two, three, gather, scatter,
    attended, far_query, stats, slots_back, two_back, three_back, zero_back,
    keys, values, coarse,
):
    factor = HEAD_DIM ** (-0.5)
    binary = factor * math.log2(math.e)
    even = (spot[0] & 1) == 0
    for rim, flag in ((high, even), (low, jnp.logical_not(even))):

        @pl.when(flag)
        def _():
            for part in range(2):
                summary = slice(TOKENS + part * COUNT[0], TOKENS + (part + 1) * COUNT[0])
                coarse[COARSE - COUNT[0] :, part * SPAN : (part + 1) * SPAN] = rim[summary, :]

    coarse[:FAR, :] = dot(gather[...], slots[...].reshape(SLOTS, 2 * SPAN), NN).astype(BF16)
    coarse[FAR : FAR + COUNT[1], :] = two[...]
    coarse[FAR + COUNT[1] : FAR + 2 * COUNT[1], :] = three[...]
    heads, units = range(2), [(head, block) for head in range(2) for block in range(2)]
    columns = [slice(head * HEAD_DIM, (head + 1) * HEAD_DIM) for head in heads]
    for head in heads:
        ext(whole, low, high, 0, columns[head], keys.at[head])
        ext(whole, low, high, 1, columns[head], values.at[head])
    far_key = [coarse[:, part_columns(0, head)] for head in heads]
    far_value = [coarse[:, part_columns(1, head)] for head in heads]
    value_t = [jnp.transpose(values[head]) for head in heads]
    far_key_t = [jnp.transpose(far_key[head]) for head in heads]
    far_value_t = [jnp.transpose(far_value[head]) for head in heads]
    query = [load(whole, 2, block, columns[head]) for head, block in units]
    grad = [load(whole, 3, block, columns[head]) for head, block in units]
    state = []
    for unit, (head, block) in enumerate(units):
        near = near_scores(spot, keys.at[head], query[unit], block)
        far = dot(far_key[head], query[unit], NT) * binary + math.log2(RATIO)
        slope = dot(far_value[head], grad[unit], NT)
        state.append((near, far, slope))
    lows = []
    for unit, (head, block) in enumerate(units):
        near, far, slope = state[unit]
        top = jnp.maximum(jnp.max(near, axis=0, keepdims=True), jnp.max(far, axis=0, keepdims=True))
        near = jnp.exp2(near - top)
        far = jnp.exp2(far - top)
        total = jnp.sum(near, axis=0, keepdims=True) + jnp.sum(far, axis=0, keepdims=True)
        inverse = 1.0 / total
        far = far * inverse
        far_low = far.astype(BF16)
        near_low = (near * inverse).astype(BF16)
        stats[unit : unit + 1, :] = top
        stats[4 + unit : 5 + unit, :] = inverse
        window = slice(block * LEAF, block * LEAF + 3 * LEAF)
        mixed_t = dot(value_t[head][:, window], near_low, NN) + dot(far_value_t[head], far_low, NN)
        lows.append((far, far_low, mixed_t, slope))
    key_grads, value_grads = [], []
    for unit, (head, block) in enumerate(units):
        far, far_low, mixed_t, slope = lows[unit]
        grad_t = jnp.transpose(grad[unit].astype(F32))
        delta = jnp.sum(grad_t * mixed_t, axis=0, keepdims=True)
        stats[8 + unit : 9 + unit, :] = delta
        score = (far * (slope - delta)).astype(BF16)
        far_query[unit] = dot(far_key_t[head], score, NN)
        rows = slice(block * LEAF, (block + 1) * LEAF)
        attended[rows, columns[head]] = jnp.transpose(mixed_t).astype(BF16)
        key_grads.append(dot(score, query[unit], NN))
        value_grads.append(dot(far_low, grad[unit], NN))
    for head in heads:
        key_grad = ((key_grads[2 * head] + key_grads[2 * head + 1]) * factor).astype(BF16)
        value_grad = (value_grads[2 * head] + value_grads[2 * head + 1]).astype(BF16)
        for part, far_grad in ((0, key_grad), (1, value_grad)):
            place = part_columns(part, head)
            two_back[:, place] = far_grad[FAR : FAR + COUNT[1]]
            three_back[:, place] = far_grad[FAR + COUNT[1] : FAR + 2 * COUNT[1]]
            zero_back[:, place] = far_grad[FAR + 2 * COUNT[1] :]
            slots_back[:, :, place] = (
                dot(scatter[...], far_grad[:FAR], NN).astype(BF16).reshape(PEERS, SLOT, HEAD_DIM)
            )


def backward_kernel(
    spot, whole, low, high, stats, far_query, level_zero,
    query_grad, centre, to_prev, to_next,
    keys, values, key_grad, value_grad,
):
    factor = HEAD_DIM ** (-0.5)
    for head in range(2):
        columns = slice(head * HEAD_DIM, (head + 1) * HEAD_DIM)
        ext(whole, low, high, 0, columns, keys)
        ext(whole, low, high, 1, columns, values)
        key_t = jnp.transpose(keys[...])
        for block in range(2):
            unit = 2 * head + block
            query = load(whole, 2, block, columns)
            grad = load(whole, 3, block, columns)
            window = slice(block * LEAF, block * LEAF + 3 * LEAF)
            near = near_scores(spot, keys, query, block)
            near = jnp.exp2(near - stats[unit : unit + 1, :]) * stats[4 + unit : 5 + unit, :]
            near_low = near.astype(BF16)
            slope = dot(values[window, :], grad, NT) - stats[8 + unit : 9 + unit, :]
            score = (near * slope).astype(BF16)
            query_t = dot(key_t[:, window], score, NN) + far_query[unit]
            query_grad[block * LEAF : (block + 1) * LEAF, columns] = jnp.transpose(
                query_t * factor
            ).astype(BF16)
            near_key_grad = dot(score, query, NN) * factor
            near_value_grad = dot(near_low, grad, NN)
            if block == 0:
                key_grad[: 3 * LEAF, :] = near_key_grad
                value_grad[: 3 * LEAF, :] = near_value_grad
            else:
                key_grad[LEAF : 3 * LEAF, :] += near_key_grad[: 2 * LEAF]
                value_grad[LEAF : 3 * LEAF, :] += near_value_grad[: 2 * LEAF]
                key_grad[3 * LEAF :, :] = near_key_grad[2 * LEAF :]
                value_grad[3 * LEAF :, :] = near_value_grad[2 * LEAF :]
        for part, store in ((0, key_grad), (1, value_grad)):
            place = part_columns(part, head)
            to_prev[:LEAF, place] = store[:LEAF, :].astype(BF16)
            centre[:, place] = store[LEAF : LEAF + TOKENS, :]
            to_next[:LEAF, place] = store[LEAF + TOKENS :, :].astype(BF16)
    to_prev[LEAF:, :] = level_zero[...]
    to_next[LEAF:, :] = level_zero[...]


def gather_kernel(
    spot, centre, from_prev, from_next, two, three, total, weight, level_zero
):
    even = (spot[0] & 1) == 0
    for rim, flag in ((from_next, even), (from_prev, jnp.logical_not(even))):

        @pl.when(flag)
        def _():
            level_zero[...] = rim[LEAF:, :]

    token, column = grid(TOKENS, COUNT[0])
    own = jnp.where((token >> 4) == column, 1.0 / RATIO, 0.0).astype(BF16)
    spread = centre[...] + dot(own, level_zero[...], NN)
    token, column = grid(TOKENS, COUNT[1])
    own = jnp.where((token >> 5) == column, 1.0 / (2 * RATIO), 0.0).astype(BF16)
    spread = spread + dot(own, two[...], NN) + dot(own, three[...], NN)
    total[:LEAF, :] = spread[:LEAF] + from_prev[:LEAF, :].astype(F32)
    total[LEAF:, :] = spread[LEAF:] + from_next[:LEAF, :].astype(F32)
    token, column = grid(TOKENS, SLOTS)
    valid, source = slot_row((column >> 3) ^ spot[0], column & 7)
    result = jnp.zeros((TOKENS, SLOTS), F32)
    for level in range(2, LEVELS):
        shift = 4 + level
        hit = valid & (source == START[level] + (token >> shift))
        result = jnp.where(hit, 1.0 / (1 << shift), result)
    weight[...] = result.astype(BF16)


def finish_kernel(total, weight, slots, key_grad, value_grad):
    rows = slots[...].reshape(SLOTS, 2 * SPAN)
    result = (total[...] + dot(weight[...], rows, NN)).astype(BF16)
    key_grad[...] = result[:, :SPAN]
    value_grad[...] = result[:, SPAN:]


def body(query, key, value, cotangent):
    devices = lax.axis_size("context")
    position = lax.axis_index("context")
    spot = jnp.stack([position, jnp.int32(devices)])

    def ring(block, step):
        pairs = [(source, (source + step) % devices) for source in range(devices)]
        return lax.ppermute(block, "context", pairs)

    def partner(block, offset):
        pairs = [(source, source ^ offset) for source in range(devices)]
        return lax.ppermute(block, "context", pairs)

    whole = lax.all_to_all(pack(key, value, query, cotangent), "head", 0, 0)
    slots = shape(PEERS, SLOT, 2 * SPAN)
    rim = shape(TOKENS + 2 * COUNT[0], SPAN)
    one = shape(COUNT[1], 2 * SPAN)
    level_one, slots_out, to_next, to_prev = call(
        pool_kernel, (one, slots, rim, rim), specs=[SMEM, VMEM]
    )(spot, whole)
    slots_in = lax.all_to_all(slots_out, "context", 0, 0)
    low = ring(to_next, 1)
    high = ring(to_prev, -1)
    two = partner(level_one, 2)
    three = partner(level_one, 3)
    gather, scatter = call(
        select_kernel, (shape(FAR, SLOTS), shape(SLOTS, FAR)), specs=[SMEM, VMEM]
    )(spot, level_one)
    span = 2 * LEAF + TOKENS
    attended, far_query, stats, slots_back, two_back, three_back, zero_back = call(
        forward_kernel,
        (
            shape(TOKENS, SPAN),
            shape(4, HEAD_DIM, LEAF, kind=F32),
            shape(16, LEAF, kind=F32),
            slots,
            one,
            one,
            shape(COUNT[0], 2 * SPAN),
        ),
        [pltpu.VMEM((2, span, HEAD_DIM), BF16)] * 2 + [pltpu.VMEM((COARSE, 2 * SPAN), BF16)],
        [SMEM] + [VMEM] * 8,
    )(spot, whole, low, high, slots_in, two, three, gather, scatter)
    slots_back = lax.all_to_all(slots_back, "context", 0, 0)
    two_back = partner(two_back, 2)
    three_back = partner(three_back, 3)
    rim_grad = shape(LEAF + COUNT[0], 2 * SPAN)
    query_grad, centre, to_prev, to_next = call(
        backward_kernel,
        (shape(TOKENS, SPAN), shape(TOKENS, 2 * SPAN, kind=F32), rim_grad, rim_grad),
        [pltpu.VMEM((span, HEAD_DIM), BF16)] * 2 + [pltpu.VMEM((span, HEAD_DIM), F32)] * 2,
        [SMEM] + [VMEM] * 6,
    )(spot, whole, low, high, stats, far_query, zero_back)
    from_next = ring(to_prev, -1)
    from_prev = ring(to_next, 1)
    total, weight = call(
        gather_kernel,
        (shape(TOKENS, 2 * SPAN, kind=F32), shape(TOKENS, SLOTS)),
        [pltpu.VMEM((COUNT[0], 2 * SPAN), BF16)],
        [SMEM] + [VMEM] * 5,
    )(spot, centre, from_prev, from_next, two_back, three_back)
    key_grad, value_grad = call(
        finish_kernel, (shape(TOKENS, SPAN), shape(TOKENS, SPAN)), count=3
    )(total, weight, slots_back)
    return attended, query_grad, key_grad, value_grad


def solution(mesh):
    spec = P(("context", "head"), None)
    out = P("context", "head")
    return jax.shard_map(
        body, mesh=mesh, in_specs=(spec,) * 4, out_specs=(out,) * 4, check_vma=False
    )
```

time: 141 us -> 130 us (0.922)
  the two profiles are of different devices: /device:TPU:2 before, /device:TPU:1 now
where the time goes in v3:
time: 130 us
  starting transfers between devices  61.9 us (48%)
  waiting for transfers between devices  51.3 us (39%)
  Pallas kernels  15.5 us (12%)
    ppermute x4, waiting for transfers between devices, partner(): return lax.ppermute(block, 'context', pairs)  32.6 us
    ppermute x4, starting transfers between devices, ring(): return lax.ppermute(block, 'context', pairs)  17.2 us
    all_to_all x1, waiting for transfers between devices, body(): whole = lax.all_to_all(pack(key, value, query, cotangent), 'head', 0, 0)  15 us
    all_to_all x1, starting transfers between devices, body(): slots_in = lax.all_to_all(slots_out, 'context', 0, 0)  13.9 us
    all_to_all x1, starting transfers between devices, body(): slots_back = lax.all_to_all(slots_back, 'context', 0, 0)  12 us
    all_to_all x1, starting transfers between devices, body(): whole = lax.all_to_all(pack(key, value, query, cotangent), 'head', 0, 0)  10.3 us
    ppermute x4, starting transfers between devices, partner(): return lax.ppermute(block, 'context', pairs)  8.52 us
    pallas_call x1, Pallas kernels, body(): call(forward_kernel, (shape(TOKENS, SPAN), shape(4, HEAD_DIM, LEAF, kind=...  4.21 us
  transfers between devices with their start and end apart: 11, of which 7 were waited for; matrix products, arithmetic and copies ran while one was open for 0% of the time, Pallas kernels for 5%

profile of v3, /device:TPU:1, one launch (start us, length us, event | category | flops | bytes accessed | tf_op | source)
XLA Modules:
  0.0 129.6 jit_solution(635390456419418043)
XLA Ops:
  0.6 2.0 %shard_map.75 = bf16[8,256,256]{2,1,0:T(8,128)(2,1)} custom-call(bf16[64,2048]{1,0:T(8,128)(2,1)} %key.1, bf16[64,2048]{1,0:T(8,128)(2,1)} %value.1, bf16[64,2048]{1,0:T(8,128)(2,1)} %query.1, bf16[64,2048]{1,0:T(8,128)(2,1)} %cotangent.1), custom_call_target="tpu_custom_call" | custom-call | tf_op jit(solution)/shard_map/pallas_call | solution.py:106
  2.6 10.3 %all-to-all-start = ((bf16[8,256,256]{2,1,0:T(8,128)(2,1)}), bf16[8,256,256]{2,1,0:T(8,128)(2,1)S(1)}, u32[]{:S(2)}, u32[]{:S(2)}) async-start(bf16[8,256,256]{2,1,0:T(8,128)(2,1)} %shard_map.75), calls=%async_computation | async-start | bytes 2097152 | tf_op jit(solution)/shard_map/all_to_all | solution.py:358
  13.0 0.1 pad_add_fusion.spot
  13.1 15.0 %all-to-all-done.whole = bf16[8,256,256]{2,1,0:T(8,128)(2,1)S(1)} async-done(((bf16[8,256,256]{2,1,0:T(8,128)(2,1)}), bf16[8,256,256]{2,1,0:T(8,128)(2,1)S(1)}, u32[]{:S(2)}, u32[]{:S(2)}) %all-to-all-start) | async-done | bytes 1048608 | tf_op jit(solution)/shard_map/all_to_all | solution.py:358
  28.1 2.0 %shard_map.76 = (bf16[16,512]{1,0:T(8,128)(2,1)S(1)}, bf16[64,8,512]{2,1,0:T(8,128)(2,1)}, bf16[576,256]{1,0:T(8,128)(2,1)S(1)}, bf16[576,256]{1,0:T(8,128)(2,1)S(1)}) custom-call(s32[2]{0:T(128)S(1)} %pad_add_fusion.spot, bf16[8,256,256]{2,1,0:T(8,128)(2,1)S(1)} %all-to-all-done.whole), custom_call_target="tpu_custom_call" | custom-call | tf_op jit(solution)/shard_map/pallas_call | solution.py:362
  30.1 13.9 %all-to-all-start.1 = ((bf16[64,8,512]{2,1,0:T(8,128)(2,1)}), bf16[64,8,512]{2,1,0:T(8,128)(2,1)S(1)}, u32[]{:S(2)}, u32[]{:S(2)}) async-start(bf16[64,8,512]{2,1,0:T(8,128)(2,1)} %get-tuple-element.27), calls=%async_computation.1 | async-start | bytes 1048576 | tf_op jit(solution)/shard_map/all_to_all | solution.py:365
  44.1 2.9 %collective-permute-start = (bf16[576,256]{1,0:T(8,128)(2,1)S(1)}, bf16[576,256]{1,0:T(8,128)(2,1)S(1)}, u32[]{:S(2)}, u32[]{:S(2)}) collective-permute-start(bf16[576,256]{1,0:T(8,128)(2,1)S(1)} %get-tuple-element.25), channel_id=1, source_target_pairs={{0,8},{8,16},{16,24},{24,32},{32,40},{40,48},{48,56},{56,64},{64,7... | collective-permute-start | bytes 884744 | tf_op jit(solution)/shard_map/ppermute | solution.py:352
  47.0 5.7 %collective-permute-start.1 = (bf16[576,256]{1,0:T(8,128)(2,1)S(1)}, bf16[576,256]{1,0:T(8,128)(2,1)S(1)}, u32[]{:S(2)}, u32[]{:S(2)}) collective-permute-start(bf16[576,256]{1,0:T(8,128)(2,1)S(1)} %get-tuple-element.26), channel_id=1, source_target_pairs={{0,504},{8,0},{16,8},{24,16},{32,24},{40,32},{48,40},{56,48},{64,5... | collective-permute-start | bytes 884744 | tf_op jit(solution)/shard_map/ppermute | solution.py:352
  52.7 2.3 %collective-permute-start.3 = (bf16[16,512]{1,0:T(8,128)(2,1)S(1)}, bf16[16,512]{1,0:T(8,128)(2,1)S(1)}, u32[]{:S(2)}, u32[]{:S(2)}) collective-permute-start(bf16[16,512]{1,0:T(8,128)(2,1)S(1)} %get-tuple-element.28._after), channel_id=1, source_target_pairs={{0,24},{8,16},{16,8},{24,0},{32,56},{40,48},{48,40},{56,32},{64,88... | collective-permute-start | bytes 49160 | tf_op jit(solution)/shard_map/ppermute | solution.py:356
  55.0 1.9 %collective-permute-start.2 = (bf16[16,512]{1,0:T(8,128)(2,1)S(1)}, bf16[16,512]{1,0:T(8,128)(2,1)S(1)}, u32[]{:S(2)}, u32[]{:S(2)}) collective-permute-start(bf16[16,512]{1,0:T(8,128)(2,1)S(1)} %get-tuple-element.28._after), channel_id=1, source_target_pairs={{0,16},{8,24},{16,0},{24,8},{32,48},{40,56},{48,32},{56,40},{64,80... | collective-permute-start | bytes 49160 | tf_op jit(solution)/shard_map/ppermute | solution.py:356
  56.9 0.6 shard_map.77
  57.6 17.5 %collective-permute-done.3.three = bf16[16,512]{1,0:T(8,128)(2,1)S(1)} collective-permute-done((bf16[16,512]{1,0:T(8,128)(2,1)S(1)}, bf16[16,512]{1,0:T(8,128)(2,1)S(1)}, u32[]{:S(2)}, u32[]{:S(2)}) %collective-permute-start.3) | collective-permute-done | bytes 16416 | tf_op jit(solution)/shard_map/ppermute | solution.py:356
  75.0 0.6 collective-permute-done.2.two
  75.7 1.8 %collective-permute-done.low = bf16[576,256]{1,0:T(8,128)(2,1)S(1)} collective-permute-done((bf16[576,256]{1,0:T(8,128)(2,1)S(1)}, bf16[576,256]{1,0:T(8,128)(2,1)S(1)}, u32[]{:S(2)}, u32[]{:S(2)}) %collective-permute-start) | collective-permute-done | bytes 294944 | tf_op jit(solution)/shard_map/ppermute | solution.py:352
  77.4 0.0 collective-permute-done.1.high
  77.4 0.0 all-to-all-done.1.slots
  77.4 4.2 %shard_map.78 = (bf16[512,256]{1,0:T(8,128)(2,1)}, f32[4,128,256]{2,1,0:T(8,128)S(1)}, f32[16,256]{1,0:T(8,128)S(1)}, bf16[64,8,512]{2,1,0:T(8,128)(2,1)}, bf16[...) custom-call(s32[2]{0:T(128)S(1)} %pad_add_fusion.spot, ...), custom_call_target="tpu_custom_call" | custom-call | tf_op jit(solution)/shard_map/pallas_call | solution.py:374
  81.6 12.0 %all-to-all-start.2 = ((bf16[64,8,512]{2,1,0:T(8,128)(2,1)}), bf16[64,8,512]{2,1,0:T(8,128)(2,1)S(1)}, u32[]{:S(2)}, u32[]{:S(2)}) async-start(bf16[64,8,512]{2,1,0:T(8,128)(2,1)} %get-tuple-element.43), calls=%async_computation.2 | async-start | bytes 1048576 | tf_op jit(solution)/shard_map/all_to_all | solution.py:388
  93.6 4.0 %shard_map.79 = (bf16[512,256]{1,0:T(8,128)(2,1)}, f32[512,512]{1,0:T(8,128)S(1)}, bf16[288,512]{1,0:T(8,128)(2,1)S(1)}, bf16[288,512]{1,0:T(8,128)(2,1)S(1)}) custom-call(s32[2]{0:T(128)S(1)} %pad_add_fusion.spot, bf16[8,256,256]{2,1,0:T(8,128)(2,1)S(1)} %all-to-all-done.whole, bf16[576,256]{1,0:T(8,128)(2,1)S(1)} %collective-permute-done.low, ...), custom_call_target="tpu_custom_call" | custom-call | tf_op jit(solution)/shard_map/pallas_call | solution.py:392
  97.6 2.9 %collective-permute-start.4 = (bf16[288,512]{1,0:T(8,128)(2,1)S(1)}, bf16[288,512]{1,0:T(8,128)(2,1)S(1)}, u32[]{:S(2)}, u32[]{:S(2)}) collective-permute-start(bf16[288,512]{1,0:T(8,128)(2,1)S(1)} %get-tuple-element.37), channel_id=1, source_target_pairs={{0,8},{8,16},{16,24},{24,32},{32,40},{40,48},{48,56},{56,64},{64,7... | collective-permute-start | bytes 884744 | tf_op jit(solution)/shard_map/ppermute | solution.py:352
  100.5 5.7 %collective-permute-start.5 = (bf16[288,512]{1,0:T(8,128)(2,1)S(1)}, bf16[288,512]{1,0:T(8,128)(2,1)S(1)}, u32[]{:S(2)}, u32[]{:S(2)}) collective-permute-start(bf16[288,512]{1,0:T(8,128)(2,1)S(1)} %get-tuple-element.38), channel_id=1, source_target_pairs={{0,504},{8,0},{16,8},{24,16},{32,24},{40,32},{48,40},{56,48},{64,5... | collective-permute-start | bytes 884744 | tf_op jit(solution)/shard_map/ppermute | solution.py:352
  106.2 1.9 %collective-permute-start.6 = (bf16[16,512]{1,0:T(8,128)(2,1)S(1)}, bf16[16,512]{1,0:T(8,128)(2,1)S(1)}, u32[]{:S(2)}, u32[]{:S(2)}) collective-permute-start(bf16[16,512]{1,0:T(8,128)(2,1)S(1)} %get-tuple-element.39), channel_id=1, source_target_pairs={{0,16},{8,24},{16,0},{24,8},{32,48},{40,56},{48,32},{56,40},{64,80... | collective-permute-start | bytes 49160 | tf_op jit(solution)/shard_map/ppermute | solution.py:356
  108.1 2.3 %collective-permute-start.7 = (bf16[16,512]{1,0:T(8,128)(2,1)S(1)}, bf16[16,512]{1,0:T(8,128)(2,1)S(1)}, u32[]{:S(2)}, u32[]{:S(2)}) collective-permute-start(bf16[16,512]{1,0:T(8,128)(2,1)S(1)} %get-tuple-element.40), channel_id=1, source_target_pairs={{0,24},{8,16},{16,8},{24,0},{32,56},{40,48},{48,40},{56,32},{64,88... | collective-permute-start | bytes 49160 | tf_op jit(solution)/shard_map/ppermute | solution.py:356
  110.5 14.2 %collective-permute-done.6.two = bf16[16,512]{1,0:T(8,128)(2,1)S(1)} collective-permute-done((bf16[16,512]{1,0:T(8,128)(2,1)S(1)}, bf16[16,512]{1,0:T(8,128)(2,1)S(1)}, u32[]{:S(2)}, u32[]{:S(2)}) %collective-permute-start.6) | collective-permute-done | bytes 16416 | tf_op jit(solution)/shard_map/ppermute | solution.py:356
  124.6 0.4 collective-permute-done.7.three
  125.0 1.9 %collective-permute-done.4.from_prev = bf16[288,512]{1,0:T(8,128)(2,1)S(1)} collective-permute-done((bf16[288,512]{1,0:T(8,128)(2,1)S(1)}, bf16[288,512]{1,0:T(8,128)(2,1)S(1)}, u32[]{:S(2)}, u32[]{:S(2)}) %collective-permute-start.4) | collective-permute-done | bytes 294944 | tf_op jit(solution)/shard_map/ppermute | solution.py:352
  126.9 0.0 collective-permute-done.5.from_next
  126.9 1.5 %shard_map.80 = (f32[512,512]{1,0:T(8,128)S(1)}, bf16[512,512]{1,0:T(8,128)(2,1)S(1)}) custom-call(s32[2]{0:T(128)S(1)} %pad_add_fusion.spot, f32[512,512]{1,0:T(8,128)S(1)} %get-tuple-element.36.centre, bf16[288,512]{1,0:T(8,128)(2,1)S(1)} %collective-permute-done.4.from_prev, bf16[288,512]{1,0:T(8,128)(2,1)S(1)} %collective-permute-done.5.from_next, ...), custom_call_target="tpu_custom_call" | custom-call | tf_op jit(solution)/shard_map/pallas_call | solution.py:400
  128.4 0.0 all-to-all-done.2.slots
  128.4 1.2 shard_map.81
Async XLA Ops:
  2.6 25.5 %all-to-all-start = ((bf16[8,256,256]{2,1,0:T(8,128)(2,1)}), bf16[8,256,256]{2,1,0:T(8,128)(2,1)S(1)}, u32[]{:S(2)}, u32[]{:S(2)}) async-start(bf16[8,256,256]{2,1,0:T(8,128)(2,1)} %shard_map.75), calls=%async_computation | async-start | bytes 2097152 | tf_op jit(solution)/shard_map/all_to_all | solution.py:358
  30.1 47.3 %all-to-all-start.1 = ((bf16[64,8,512]{2,1,0:T(8,128)(2,1)}), bf16[64,8,512]{2,1,0:T(8,128)(2,1)S(1)}, u32[]{:S(2)}, u32[]{:S(2)}) async-start(bf16[64,8,512]{2,1,0:T(8,128)(2,1)} %get-tuple-element.27), calls=%async_computation.1 | async-start | bytes 1048576 | tf_op jit(solution)/shard_map/all_to_all | solution.py:365
  44.1 33.4 %collective-permute-start = (bf16[576,256]{1,0:T(8,128)(2,1)S(1)}, bf16[576,256]{1,0:T(8,128)(2,1)S(1)}, u32[]{:S(2)}, u32[]{:S(2)}) collective-permute-start(bf16[576,256]{1,0:T(8,128)(2,1)S(1)} %get-tuple-element.25), channel_id=1, source_target_pairs={{0,8},{8,16},{16,24},{24,32},{32,40},{40,48},{48,56},{56,64},{64,7... | collective-permute-start | bytes 884744 | tf_op jit(solution)/shard_map/ppermute | solution.py:352
  47.0 30.4 %collective-permute-start.1 = (bf16[576,256]{1,0:T(8,128)(2,1)S(1)}, bf16[576,256]{1,0:T(8,128)(2,1)S(1)}, u32[]{:S(2)}, u32[]{:S(2)}) collective-permute-start(bf16[576,256]{1,0:T(8,128)(2,1)S(1)} %get-tuple-element.26), channel_id=1, source_target_pairs={{0,504},{8,0},{16,8},{24,16},{32,24},{40,32},{48,40},{56,48},{64,5... | collective-permute-start | bytes 884744 | tf_op jit(solution)/shard_map/ppermute | solution.py:352
  52.7 22.4 %collective-permute-start.3 = (bf16[16,512]{1,0:T(8,128)(2,1)S(1)}, bf16[16,512]{1,0:T(8,128)(2,1)S(1)}, u32[]{:S(2)}, u32[]{:S(2)}) collective-permute-start(bf16[16,512]{1,0:T(8,128)(2,1)S(1)} %get-tuple-element.28._after), channel_id=1, source_target_pairs={{0,24},{8,16},{16,8},{24,0},{32,56},{40,48},{48,40},{56,32},{64,88... | collective-permute-start | bytes 49160 | tf_op jit(solution)/shard_map/ppermute | solution.py:356
  55.0 20.6 %collective-permute-start.2 = (bf16[16,512]{1,0:T(8,128)(2,1)S(1)}, bf16[16,512]{1,0:T(8,128)(2,1)S(1)}, u32[]{:S(2)}, u32[]{:S(2)}) collective-permute-start(bf16[16,512]{1,0:T(8,128)(2,1)S(1)} %get-tuple-element.28._after), channel_id=1, source_target_pairs={{0,16},{8,24},{16,0},{24,8},{32,48},{40,56},{48,32},{56,40},{64,80... | collective-permute-start | bytes 49160 | tf_op jit(solution)/shard_map/ppermute | solution.py:356
  81.6 46.7 %all-to-all-start.2 = ((bf16[64,8,512]{2,1,0:T(8,128)(2,1)}), bf16[64,8,512]{2,1,0:T(8,128)(2,1)S(1)}, u32[]{:S(2)}, u32[]{:S(2)}) async-start(bf16[64,8,512]{2,1,0:T(8,128)(2,1)} %get-tuple-element.43), calls=%async_computation.2 | async-start | bytes 1048576 | tf_op jit(solution)/shard_map/all_to_all | solution.py:388
  97.6 29.3 %collective-permute-start.4 = (bf16[288,512]{1,0:T(8,128)(2,1)S(1)}, bf16[288,512]{1,0:T(8,128)(2,1)S(1)}, u32[]{:S(2)}, u32[]{:S(2)}) collective-permute-start(bf16[288,512]{1,0:T(8,128)(2,1)S(1)} %get-tuple-element.37), channel_id=1, source_target_pairs={{0,8},{8,16},{16,24},{24,32},{32,40},{40,48},{48,56},{56,64},{64,7... | collective-permute-start | bytes 884744 | tf_op jit(solution)/shard_map/ppermute | solution.py:352
  100.5 26.4 %collective-permute-start.5 = (bf16[288,512]{1,0:T(8,128)(2,1)S(1)}, bf16[288,512]{1,0:T(8,128)(2,1)S(1)}, u32[]{:S(2)}, u32[]{:S(2)}) collective-permute-start(bf16[288,512]{1,0:T(8,128)(2,1)S(1)} %get-tuple-element.38), channel_id=1, source_target_pairs={{0,504},{8,0},{16,8},{24,16},{32,24},{40,32},{48,40},{56,48},{64,5... | collective-permute-start | bytes 884744 | tf_op jit(solution)/shard_map/ppermute | solution.py:352
  106.2 18.4 %collective-permute-start.6 = (bf16[16,512]{1,0:T(8,128)(2,1)S(1)}, bf16[16,512]{1,0:T(8,128)(2,1)S(1)}, u32[]{:S(2)}, u32[]{:S(2)}) collective-permute-start(bf16[16,512]{1,0:T(8,128)(2,1)S(1)} %get-tuple-element.39), channel_id=1, source_target_pairs={{0,16},{8,24},{16,0},{24,8},{32,48},{40,56},{48,32},{56,40},{64,80... | collective-permute-start | bytes 49160 | tf_op jit(solution)/shard_map/ppermute | solution.py:356
  108.1 16.9 %collective-permute-start.7 = (bf16[16,512]{1,0:T(8,128)(2,1)S(1)}, bf16[16,512]{1,0:T(8,128)(2,1)S(1)}, u32[]{:S(2)}, u32[]{:S(2)}) collective-permute-start(bf16[16,512]{1,0:T(8,128)(2,1)S(1)} %get-tuple-element.40), channel_id=1, source_target_pairs={{0,24},{8,16},{16,8},{24,0},{32,56},{40,48},{48,40},{56,32},{64,88... | collective-permute-start | bytes 49160 | tf_op jit(solution)/shard_map/ppermute | solution.py:356

commit v4 on v3

--- a/solution.py
+++ b/solution.py
@@ -18,11 +18,15 @@
 OWN = 64
 COUNT = [32 >> level for level in range(LEVELS)]
 START = [64 - (64 >> level) for level in range(LEVELS)]
-PEERS = 64
-SLOT = 8
-SLOTS = PEERS * SLOT
-FAR = 4 * 32
-COARSE = FAR + 2 * COUNT[1] + COUNT[0]
+FAR_PEERS = 16
+FAR_ROWS = 8
+FAR = FAR_PEERS * FAR_ROWS
+NEAR_PEERS = 4
+NEAR_BITS = 2
+NEAR_ROWS = 48
+HELD = 32
+NEAR = NEAR_PEERS * NEAR_ROWS
+COARSE = COUNT[0] + NEAR_PEERS * HELD + 2 * COUNT[1]
 F32 = jnp.float32
 BF16 = jnp.bfloat16
 VMEM = pl.BlockSpec(memory_space=pltpu.VMEM)
@@ -37,7 +41,7 @@
     return lax.dot_general(left, right, (over, ((), ())), preferred_element_type=F32)
 
 
-def call(kernel, out_shape, scratch=(), specs=None, count=1):
+def call(kernel, out_shape, scratch=(), specs=None, count=1, cost=None):
     return pl.pallas_call(
         kernel,
         out_shape=out_shape,
@@ -45,6 +49,7 @@
         out_specs=jax.tree.map(lambda _: VMEM, out_shape),
         scratch_shapes=scratch,
         compiler_params=LIMIT,
+        cost_estimate=cost,
     )
 
 
@@ -70,15 +75,24 @@
     return result
 
 
-def slot_row(offset, row):
-    count = pick(offset, [(4, 0), (8, COUNT[2]), (16, COUNT[3]), (32, COUNT[4])], COUNT[5])
-    start = pick(offset, [(8, START[2]), (16, START[3]), (32, START[4])], START[5])
+def far_slot(offset, row):
+    count = pick(offset, [(1, 0), (2, COUNT[2]), (4, COUNT[3]), (8, COUNT[4])], COUNT[5])
+    start = pick(offset, [(2, START[2]), (4, START[3]), (8, START[4])], START[5])
     return row < count, start + row
 
 
-def slot_of(row):
-    offset = pick(row, [(32, 4 + (row >> 3)), (64, row >> 2), (96, (row >> 1) - 16)], row - 64)
-    return offset, pick(row, [(32, row & 7), (64, row & 3), (96, row & 1)], 0)
+def near_slot(offset, row):
+    return (offset >= 2) & (row >= HELD), START[1] + row - HELD
+
+
+def held_slot(row):
+    offset = pick(row, [(8, 1), (16, row >> 2), (24, (row >> 1) - 4)], row - 16)
+    return row < HELD, offset, pick(row, [(8, row), (16, row & 3), (24, row & 1)], 0)
+
+
+def near_place(index):
+    slot = pick(index, [(NEAR_ROWS, 0), (2 * NEAR_ROWS, 1), (3 * NEAR_ROWS, 2)], 3)
+    return slot, index - slot * NEAR_ROWS
 
 
 def pack_kernel(key, value, query, cotangent, packed, rows, held, arrived, left):
@@ -118,7 +132,7 @@
     )(*sources)
 
 
-def pool_kernel(spot, whole, level_one, slots, to_next, to_prev):
+def pool_kernel(spot, whole, pooled, far_send, to_next, to_prev):
     row, token = grid(OWN, TOKENS)
     weight = jnp.zeros((OWN, TOKENS), F32)
     for level in range(LEVELS):
@@ -126,29 +140,45 @@
         hit = row == START[level] + lax.shift_right_logical(token, shift)
         weight = jnp.where(hit, 1.0 / (1 << shift), weight)
     weight = weight.astype(BF16)
-    row, column = grid(SLOTS, OWN)
-    valid, source = slot_row((row >> 3) ^ spot[0], row & 7)
+    row, column = grid(FAR, OWN)
+    valid, source = far_slot((row >> 3) ^ (spot[0] >> NEAR_BITS), row & 7)
     spread = ones(valid & (column == source))
     for part in range(2):
         rows = whole[:, part * SHARE : (part + 1) * SHARE, :].reshape(TOKENS, SPAN)
         means = dot(weight, rows, NN).astype(BF16)
         columns = slice(part * SPAN, (part + 1) * SPAN)
-        level_one[:, columns] = means[START[1] : START[1] + COUNT[1]]
+        pooled[:, columns] = means
         place = slice(TOKENS + part * COUNT[0], TOKENS + (part + 1) * COUNT[0])
         to_next[place, :] = means[: COUNT[0]]
         to_prev[place, :] = means[: COUNT[0]]
-        slots[:, :, columns] = dot(spread, means, NN).astype(BF16).reshape(PEERS, SLOT, SPAN)
+        far_send[:, :, columns] = dot(spread, means, NN).astype(BF16).reshape(FAR_PEERS, FAR_ROWS, SPAN)
     to_prev[:TOKENS, :] = whole[: SHARES // 2, : 2 * SHARE, :].reshape(TOKENS, SPAN)
     to_next[:TOKENS, :] = whole[SHARES // 2 :, : 2 * SHARE, :].reshape(TOKENS, SPAN)
 
 
-def select_kernel(spot, _after, gather, scatter):
-    row, column = grid(FAR, SLOTS)
-    offset, place = slot_of(row)
-    gather[...] = ones(column == (offset ^ spot[0]) * SLOT + place)
-    row, column = grid(SLOTS, FAR)
-    offset, place = slot_of(column)
-    scatter[...] = ones(row == (offset ^ spot[0]) * SLOT + place)
+def own_kernel(spot, pooled, _low, _high, own, gather):
+    far_at, near_at = spot[0] >> NEAR_BITS, spot[0] & (NEAR_PEERS - 1)
+    index, column = grid(NEAR, OWN)
+    slot, inside = near_place(index)
+    valid, source = near_slot(slot ^ near_at, inside)
+    own[...] = dot(ones(valid & (column == source)), pooled[...], NN)
+    index, column = grid(NEAR, FAR)
+    slot, inside = near_place(index)
+    valid, offset, place = held_slot(inside)
+    gather[...] = ones(valid & (column == (offset ^ far_at) * FAR_ROWS + place))
+
+
+def near_kernel(own, gather, far, near_send):
+    held = dot(gather[...], far[...].reshape(FAR, 2 * SPAN), NN)
+    near_send[...] = (own[...] + held).astype(BF16).reshape(NEAR_PEERS, NEAR_ROWS, 2 * SPAN)
+
+
+def far_send_kernel(scatter, near, far_send):
+    far_send[...] = (
+        dot(scatter[...], near[...].reshape(NEAR, 2 * SPAN), NN)
+        .astype(BF16)
+        .reshape(FAR_PEERS, FAR_ROWS, 2 * SPAN)
+    )
 
 
 def part_rows(part):
@@ -186,8 +216,8 @@
 
 
 def forward_kernel(
-    spot, whole, low, high, slots, two, three, gather, scatter,
-    attended, far_query, stats, slots_back, two_back, three_back, zero_back,
+    spot, whole, low, high, near_rows,
+    attended, far_query, stats, near_send, zero_back,
     keys, values, coarse,
 ):
     factor = HEAD_DIM ** (-0.5)
@@ -201,9 +231,13 @@
                 summary = slice(TOKENS + part * COUNT[0], TOKENS + (part + 1) * COUNT[0])
                 coarse[COARSE - COUNT[0] :, part * SPAN : (part + 1) * SPAN] = rim[summary, :]
 
-    coarse[:FAR, :] = dot(gather[...], slots[...].reshape(SLOTS, 2 * SPAN), NN).astype(BF16)
-    coarse[FAR : FAR + COUNT[1], :] = two[...]
-    coarse[FAR + COUNT[1] : FAR + 2 * COUNT[1], :] = three[...]
+    near_at = spot[0] & (NEAR_PEERS - 1)
+    for slot in range(NEAR_PEERS):
+        coarse[slot * HELD : (slot + 1) * HELD, :] = near_rows[slot, :HELD, :]
+    first = NEAR_PEERS * HELD
+    for offset in (2, 3):
+        start = first + (offset - 2) * COUNT[1]
+        coarse[start : start + COUNT[1], :] = near_rows[near_at ^ offset, HELD:, :]
     heads, units = range(2), [(head, block) for head in range(2) for block in range(2)]
     columns = [slice(head * HEAD_DIM, (head + 1) * HEAD_DIM) for head in heads]
     for head in heads:
@@ -255,17 +289,19 @@
         value_grad = (value_grads[2 * head] + value_grads[2 * head + 1]).astype(BF16)
         for part, far_grad in ((0, key_grad), (1, value_grad)):
             place = part_columns(part, head)
-            two_back[:, place] = far_grad[FAR : FAR + COUNT[1]]
-            three_back[:, place] = far_grad[FAR + COUNT[1] : FAR + 2 * COUNT[1]]
-            zero_back[:, place] = far_grad[FAR + 2 * COUNT[1] :]
-            slots_back[:, :, place] = (
-                dot(scatter[...], far_grad[:FAR], NN).astype(BF16).reshape(PEERS, SLOT, HEAD_DIM)
-            )
+            zero_back[:, place] = far_grad[first + 2 * COUNT[1] :]
+            for slot in range(NEAR_PEERS):
+                near_send[slot, :HELD, place] = far_grad[slot * HELD : (slot + 1) * HELD]
+            for offset in (0, 1):
+                near_send[near_at ^ offset, HELD:, place] = jnp.zeros((COUNT[1], HEAD_DIM), BF16)
+            for offset in (2, 3):
+                start = first + (offset - 2) * COUNT[1]
+                near_send[near_at ^ offset, HELD:, place] = far_grad[start : start + COUNT[1]]
 
 
 def backward_kernel(
     spot, whole, low, high, stats, far_query, level_zero,
-    query_grad, centre, to_prev, to_next,
+    query_grad, centre, to_prev, to_next, scatter,
     keys, values, key_grad, value_grad,
 ):
     factor = HEAD_DIM ** (-0.5)
@@ -305,10 +341,15 @@
             to_next[:LEAF, place] = store[LEAF + TOKENS :, :].astype(BF16)
     to_prev[LEAF:, :] = level_zero[...]
     to_next[LEAF:, :] = level_zero[...]
+    row, column = grid(FAR, NEAR)
+    _, inside = near_place(column)
+    valid, offset, place = held_slot(inside)
+    hit = valid & (offset == ((row >> 3) ^ (spot[0] >> NEAR_BITS))) & (place == (row & 7))
+    scatter[...] = ones(hit)
 
 
 def gather_kernel(
-    spot, centre, from_prev, from_next, two, three, total, weight, level_zero
+    spot, centre, from_prev, from_next, near, total, weight, level_zero
 ):
     even = (spot[0] & 1) == 0
     for rim, flag in ((from_next, even), (from_prev, jnp.logical_not(even))):
@@ -322,12 +363,14 @@
     spread = centre[...] + dot(own, level_zero[...], NN)
     token, column = grid(TOKENS, COUNT[1])
     own = jnp.where((token >> 5) == column, 1.0 / (2 * RATIO), 0.0).astype(BF16)
-    spread = spread + dot(own, two[...], NN) + dot(own, three[...], NN)
+    near_at = spot[0] & (NEAR_PEERS - 1)
+    for offset in (2, 3):
+        spread = spread + dot(own, near[near_at ^ offset, HELD:, :], NN)
     total[:LEAF, :] = spread[:LEAF] + from_prev[:LEAF, :].astype(F32)
     total[LEAF:, :] = spread[LEAF:] + from_next[:LEAF, :].astype(F32)
-    token, column = grid(TOKENS, SLOTS)
-    valid, source = slot_row((column >> 3) ^ spot[0], column & 7)
-    result = jnp.zeros((TOKENS, SLOTS), F32)
+    token, column = grid(TOKENS, FAR)
+    valid, source = far_slot((column >> 3) ^ (spot[0] >> NEAR_BITS), column & 7)
+    result = jnp.zeros((TOKENS, FAR), F32)
     for level in range(2, LEVELS):
         shift = 4 + level
         hit = valid & (source == START[level] + (token >> shift))
@@ -335,11 +378,15 @@
     weight[...] = result.astype(BF16)
 
 
-def finish_kernel(total, weight, slots, key_grad, value_grad):
-    rows = slots[...].reshape(SLOTS, 2 * SPAN)
+def finish_kernel(total, weight, far, key_grad, value_grad):
+    rows = far[...].reshape(FAR, 2 * SPAN)
     result = (total[...] + dot(weight[...], rows, NN)).astype(BF16)
     key_grad[...] = result[:, :SPAN]
     value_grad[...] = result[:, SPAN:]
+
+
+FAR_GROUPS = [[far * NEAR_PEERS + near for far in range(FAR_PEERS)] for near in range(NEAR_PEERS)]
+NEAR_GROUPS = [[far * NEAR_PEERS + near for near in range(NEAR_PEERS)] for far in range(FAR_PEERS)]
 
 
 def body(query, key, value, cotangent):
@@ -351,61 +398,67 @@
         pairs = [(source, (source + step) % devices) for source in range(devices)]
         return lax.ppermute(block, "context", pairs)
 
-    def partner(block, offset):
-        pairs = [(source, source ^ offset) for source in range(devices)]
-        return lax.ppermute(block, "context", pairs)
+    def exchange(block, groups):
+        return lax.all_to_all(block, "context", 0, 0, axis_index_groups=groups)
 
     whole = lax.all_to_all(pack(key, value, query, cotangent), "head", 0, 0)
-    slots = shape(PEERS, SLOT, 2 * SPAN)
+    near_slots = shape(NEAR_PEERS, NEAR_ROWS, 2 * SPAN)
+    far_slots = shape(FAR_PEERS, FAR_ROWS, 2 * SPAN)
     rim = shape(TOKENS + 2 * COUNT[0], SPAN)
-    one = shape(COUNT[1], 2 * SPAN)
-    level_one, slots_out, to_next, to_prev = call(
-        pool_kernel, (one, slots, rim, rim), specs=[SMEM, VMEM]
+    pooled, far_send, to_next, to_prev = call(
+        pool_kernel, (shape(OWN, 2 * SPAN), far_slots, rim, rim), specs=[SMEM, VMEM]
     )(spot, whole)
-    slots_in = lax.all_to_all(slots_out, "context", 0, 0)
     low = ring(to_next, 1)
     high = ring(to_prev, -1)
-    two = partner(level_one, 2)
-    three = partner(level_one, 3)
-    gather, scatter = call(
-        select_kernel, (shape(FAR, SLOTS), shape(SLOTS, FAR)), specs=[SMEM, VMEM]
-    )(spot, level_one)
+    far = exchange(far_send, FAR_GROUPS)
+    own, gather = call(
+        own_kernel,
+        (shape(NEAR, 2 * SPAN, kind=F32), shape(NEAR, FAR)),
+        specs=[SMEM] + [VMEM] * 3,
+        cost=pl.CostEstimate(flops=5000000000, bytes_accessed=0, transcendentals=0),
+    )(spot, pooled, low, high)
+    near = exchange(call(near_kernel, near_slots, count=3)(own, gather, far), NEAR_GROUPS)
     span = 2 * LEAF + TOKENS
-    attended, far_query, stats, slots_back, two_back, three_back, zero_back = call(
+    attended, far_query, stats, near_send, zero_back = call(
         forward_kernel,
         (
             shape(TOKENS, SPAN),
             shape(4, HEAD_DIM, LEAF, kind=F32),
             shape(16, LEAF, kind=F32),
-            slots,
-            one,
-            one,
+            near_slots,
             shape(COUNT[0], 2 * SPAN),
         ),
         [pltpu.VMEM((2, span, HEAD_DIM), BF16)] * 2 + [pltpu.VMEM((COARSE, 2 * SPAN), BF16)],
-        [SMEM] + [VMEM] * 8,
-    )(spot, whole, low, high, slots_in, two, three, gather, scatter)
-    slots_back = lax.all_to_all(slots_back, "context", 0, 0)
-    two_back = partner(two_back, 2)
-    three_back = partner(three_back, 3)
+        [SMEM] + [VMEM] * 4,
+    )(spot, whole, low, high, near)
+    near = exchange(near_send, NEAR_GROUPS)
     rim_grad = shape(LEAF + COUNT[0], 2 * SPAN)
-    query_grad, centre, to_prev, to_next = call(
+    query_grad, centre, to_prev, to_next, scatter = call(
         backward_kernel,
-        (shape(TOKENS, SPAN), shape(TOKENS, 2 * SPAN, kind=F32), rim_grad, rim_grad),
+        (
+            shape(TOKENS, SPAN),
+            shape(TOKENS, 2 * SPAN, kind=F32),
+            rim_grad,
+            rim_grad,
+            shape(FAR, NEAR),
+        ),
         [pltpu.VMEM((span, HEAD_DIM), BF16)] * 2 + [pltpu.VMEM((span, HEAD_DIM), F32)] * 2,
         [SMEM] + [VMEM] * 6,
+        cost=None,
     )(spot, whole, low, high, stats, far_query, zero_back)
     from_next = ring(to_prev, -1)
     from_prev = ring(to_next, 1)
+    far = exchange(call(far_send_kernel, far_slots, count=2)(scatter, near), FAR_GROUPS)
     total, weight = call(
         gather_kernel,
-        (shape(TOKENS, 2 * SPAN, kind=F32), shape(TOKENS, SLOTS)),
+        (shape(TOKENS, 2 * SPAN, kind=F32), shape(TOKENS, FAR)),
         [pltpu.VMEM((COUNT[0], 2 * SPAN), BF16)],
-        [SMEM] + [VMEM] * 5,
-    )(spot, centre, from_prev, from_next, two_back, three_back)
+        [SMEM] + [VMEM] * 4,
+        cost=pl.CostEstimate(flops=5000000000, bytes_accessed=0, transcendentals=0),
+    )(spot, centre, from_prev, from_next, near)
     key_grad, value_grad = call(
         finish_kernel, (shape(TOKENS, SPAN), shape(TOKENS, SPAN)), count=3
-    )(total, weight, slots_back)
+    )(total, weight, far)
     return attended, query_grad, key_grad, value_grad
 
 

time: 130 us -> 117 us (0.900)
  the two profiles are of different devices: /device:TPU:1 before, /device:TPU:8 now
where the time goes in v4:
time: 117 us; the launch traced here: 116 us
  starting transfers between devices  46.2 us (39%)
  waiting for transfers between devices  43.9 us (38%)
  Pallas kernels  15.5 us (13%)
  blocking collectives  9.69 us (8%)
    all_to_all x3, waiting for transfers between devices, exchange(): return lax.all_to_all(block, 'context', 0, 0, axis_index_groups=groups)  26.3 us
    ppermute x4, starting transfers between devices, ring(): return lax.ppermute(block, 'context', pairs)  20.3 us
    all_to_all x3, starting transfers between devices, exchange(): return lax.all_to_all(block, 'context', 0, 0, axis_index_groups=groups)  16.7 us
    all_to_all x1, waiting for transfers between devices, body(): whole = lax.all_to_all(pack(key, value, query, cotangent), 'head', 0, 0)  14.5 us
    all_to_all x1, blocking collectives, exchange(): return lax.all_to_all(block, 'context', 0, 0, axis_index_groups=groups)  9.69 us
    all_to_all x1, starting transfers between devices, body(): whole = lax.all_to_all(pack(key, value, query, cotangent), 'head', 0, 0)  9.3 us
    pallas_call x1, Pallas kernels, body(): call(backward_kernel, (shape(TOKENS, SPAN), shape(TOKENS, 2 * SPAN, kind=...  4.1 us
    pallas_call x1, Pallas kernels, body(): call(forward_kernel, (shape(TOKENS, SPAN), shape(4, HEAD_DIM, LEAF, kind=...  3.69 us
  transfers between devices with their start and end apart: 8, of which 4 were waited for; matrix products, arithmetic and copies ran while one was open for 0% of the time, Pallas kernels for 6%

profile of v4, /device:TPU:8, one launch (start us, length us, event | category | flops | bytes accessed | tf_op | source)
XLA Modules:
  0.0 116.2 jit_solution(4041589649371979848)
XLA Ops:
  0.6 2.0 %shard_map.75 = bf16[8,256,256]{2,1,0:T(8,128)(2,1)} custom-call(bf16[64,2048]{1,0:T(8,128)(2,1)} %key.1, bf16[64,2048]{1,0:T(8,128)(2,1)} %value.1, bf16[64,2048]{1,0:T(8,128)(2,1)} %query.1, bf16[64,2048]{1,0:T(8,128)(2,1)} %cotangent.1), custom_call_target="tpu_custom_call" | custom-call | tf_op jit(solution)/shard_map/pallas_call | solution.py:120
  2.7 9.3 %all-to-all-start = ((bf16[8,256,256]{2,1,0:T(8,128)(2,1)}), bf16[8,256,256]{2,1,0:T(8,128)(2,1)S(1)}, u32[]{:S(2)}, u32[]{:S(2)}) async-start(bf16[8,256,256]{2,1,0:T(8,128)(2,1)} %shard_map.75), calls=%async_computation | async-start | bytes 2097152 | tf_op jit(solution)/shard_map/all_to_all | solution.py:404
  12.0 0.1 pad_add_fusion.spot
  12.0 14.5 %all-to-all-done.whole = bf16[8,256,256]{2,1,0:T(8,128)(2,1)S(1)} async-done(((bf16[8,256,256]{2,1,0:T(8,128)(2,1)}), bf16[8,256,256]{2,1,0:T(8,128)(2,1)S(1)}, u32[]{:S(2)}, u32[]{:S(2)}) %all-to-all-start) | async-done | bytes 1048608 | tf_op jit(solution)/shard_map/all_to_all | solution.py:404
  26.5 1.7 %shard_map.76 = (bf16[64,512]{1,0:T(8,128)(2,1)S(1)}, bf16[16,8,512]{2,1,0:T(8,128)(2,1)}, bf16[576,256]{1,0:T(8,128)(2,1)S(1)}, bf16[576,256]{1,0:T(8,128)(2,1)S(1)}) custom-call(s32[2]{0:T(128)S(1)} %pad_add_fusion.spot, bf16[8,256,256]{2,1,0:T(8,128)(2,1)S(1)} %all-to-all-done.whole), custom_call_target="tpu_custom_call" | custom-call | tf_op jit(solution)/shard_map/pallas_call | solution.py:408
  28.2 1.9 %collective-permute-start = (bf16[576,256]{1,0:T(8,128)(2,1)S(1)}, bf16[576,256]{1,0:T(8,128)(2,1)S(1)}, u32[]{:S(2)}, u32[]{:S(2)}) collective-permute-start(bf16[576,256]{1,0:T(8,128)(2,1)S(1)} %get-tuple-element.24), channel_id=1, source_target_pairs={{0,8},{8,16},{16,24},{24,32},{32,40},{40,48},{48,56},{56,64},{64,7... | collective-permute-start | bytes 884744 | tf_op jit(solution)/shard_map/ppermute | solution.py:399
  30.2 9.2 %collective-permute-start.1 = (bf16[576,256]{1,0:T(8,128)(2,1)S(1)}, bf16[576,256]{1,0:T(8,128)(2,1)S(1)}, u32[]{:S(2)}, u32[]{:S(2)}) collective-permute-start(bf16[576,256]{1,0:T(8,128)(2,1)S(1)} %get-tuple-element.25), channel_id=1, source_target_pairs={{0,504},{8,0},{16,8},{24,16},{32,24},{40,32},{48,40},{56,48},{64,5... | collective-permute-start | bytes 884744 | tf_op jit(solution)/shard_map/ppermute | solution.py:399
  39.4 9.2 %all-to-all-start.1 = ((bf16[16,8,512]{2,1,0:T(8,128)(2,1)}), bf16[16,8,512]{2,1,0:T(8,128)(2,1)S(1)}, u32[]{:S(2)}, u32[]{:S(2)}) async-start(bf16[16,8,512]{2,1,0:T(8,128)(2,1)} %get-tuple-element.29), calls=%async_computation.1 | async-start | bytes 262144 | tf_op jit(solution)/shard_map/all_to_all | solution.py:402
  48.6 0.0 collective-permute-done._low.low
  48.6 0.0 collective-permute-done.1._high.high
  48.6 0.7 shard_map.77
  49.3 15.1 %all-to-all-done.1.far = bf16[16,8,512]{2,1,0:T(8,128)(2,1)S(1)} async-done(((bf16[16,8,512]{2,1,0:T(8,128)(2,1)}), bf16[16,8,512]{2,1,0:T(8,128)(2,1)S(1)}, u32[]{:S(2)}, u32[]{:S(2)}) %all-to-all-start.1) | async-done | bytes 131104 | tf_op jit(solution)/shard_map/all_to_all | solution.py:402
  64.4 0.2 shard_map.78
  64.6 9.7 %all_to_all.25.near_rows = bf16[4,48,512]{2,1,0:T(8,128)(2,1)S(1)} all-to-all(bf16[4,48,512]{2,1,0:T(8,128)(2,1)S(1)} %shard_map.78), channel_id=1, replica_groups={{0,8,16,24},{32,40,48,56},{64,72,80,88},{96,104,112,120},{128,136,144,1..., dimensions={0} | all-to-all | bytes 393216 | tf_op jit(solution)/shard_map/all_to_all | solution.py:402
  74.3 3.7 %shard_map.79 = (bf16[512,256]{1,0:T(8,128)(2,1)}, f32[4,128,256]{2,1,0:T(8,128)S(1)}, f32[16,256]{1,0:T(8,128)S(1)}, bf16[4,48,512]{2,1,0:T(8,128)(2,1)}, bf16[32,512]{1,0:T(8,128)(2,1)S(1)}) custom-call(s32[2]{0:T(128)S(1)} %pad_add_fusion.spot, bf16[8,256,256]{2,1,0:T(8,128)(2,1)S(1)} %all-to-all-done.whole, ...), custom_call_target="tpu_custom_call" | custom-call | tf_op jit(solution)/shard_map/pallas_call | solution.py:422
  78.0 3.4 %all-to-all-start.3 = ((bf16[4,48,512]{2,1,0:T(8,128)(2,1)}), bf16[4,48,512]{2,1,0:T(8,128)(2,1)S(1)}, u32[]{:S(2)}, u32[]{:S(2)}) async-start(bf16[4,48,512]{2,1,0:T(8,128)(2,1)} %get-tuple-element.38), calls=%async_computation.3 | async-start | bytes 393216 | tf_op jit(solution)/shard_map/all_to_all | solution.py:402
  81.4 4.1 %shard_map.80 = (bf16[512,256]{1,0:T(8,128)(2,1)}, f32[512,512]{1,0:T(8,128)S(1)}, bf16[288,512]{1,0:T(8,128)(2,1)}, bf16[288,512]{1,0:T(8,128)(2,1)}, bf16[128,192]{1,0:T(8,128)(2,1)S(1)}) custom-call(s32[2]{0:T(128)S(1)} %pad_add_fusion.spot, bf16[8,256,256]{2,1,0:T(8,128)(2,1)S(1)} %all-to-all-done.whole, ...), custom_call_target="tpu_custom_call" | custom-call | tf_op jit(solution)/shard_map/pallas_call | solution.py:436
  85.5 3.9 %collective-permute-start.2 = (bf16[288,512]{1,0:T(8,128)(2,1)}, bf16[288,512]{1,0:T(8,128)(2,1)S(1)}, u32[]{:S(2)}, u32[]{:S(2)}) collective-permute-start(bf16[288,512]{1,0:T(8,128)(2,1)} %get-tuple-element.36), channel_id=1, source_target_pairs={{0,8},{8,16},{16,24},{24,32},{32,40},{40,48},{48,56},{56,64},{64,7... | collective-permute-start | bytes 884744 | tf_op jit(solution)/shard_map/ppermute | solution.py:399
  89.3 5.3 %collective-permute-start.3 = (bf16[288,512]{1,0:T(8,128)(2,1)}, bf16[288,512]{1,0:T(8,128)(2,1)S(1)}, u32[]{:S(2)}, u32[]{:S(2)}) collective-permute-start(bf16[288,512]{1,0:T(8,128)(2,1)} %get-tuple-element.37), channel_id=1, source_target_pairs={{0,504},{8,0},{16,8},{24,16},{32,24},{40,32},{48,40},{56,48},{64,5... | collective-permute-start | bytes 884744 | tf_op jit(solution)/shard_map/ppermute | solution.py:399
  94.6 0.0 all-to-all-done.3.near
  94.6 0.8 shard_map.82
  95.5 4.1 %all-to-all-start.4 = ((bf16[16,8,512]{2,1,0:T(8,128)(2,1)}), bf16[16,8,512]{2,1,0:T(8,128)(2,1)S(1)}, u32[]{:S(2)}, u32[]{:S(2)}) async-start(bf16[16,8,512]{2,1,0:T(8,128)(2,1)} %shard_map.82), calls=%async_computation.4 | async-start | bytes 262144 | tf_op jit(solution)/shard_map/all_to_all | solution.py:402
  99.6 0.0 collective-permute-done.2.from_prev
  99.6 3.1 %collective-permute-done.3.from_next = bf16[288,512]{1,0:T(8,128)(2,1)S(1)} collective-permute-done((bf16[288,512]{1,0:T(8,128)(2,1)}, bf16[288,512]{1,0:T(8,128)(2,1)S(1)}, u32[]{:S(2)}, u32[]{:S(2)}) %collective-permute-start.3) | collective-permute-done | bytes 294944 | tf_op jit(solution)/shard_map/ppermute | solution.py:399
  102.7 1.2 %shard_map.81 = (f32[512,512]{1,0:T(8,128)S(1)}, bf16[512,128]{1,0:T(8,128)(2,1)S(1)}) custom-call(s32[2]{0:T(128)S(1)} %pad_add_fusion.spot, f32[512,512]{1,0:T(8,128)S(1)} %get-tuple-element.35.centre, bf16[288,512]{1,0:T(8,128)(2,1)S(1)} %collective-permute-done.2.from_prev, bf16[288,512]{1,0:T(8,128)(2,1)S(1)} %collective-permute-done.3.from_next, ...), custom_call_target="tpu_custom_call" | custom-call | flops 5000000000 | tf_op jit(solution)/shard_map/pallas_call | solution.py:452
  103.9 11.2 %all-to-all-done.4.far = bf16[16,8,512]{2,1,0:T(8,128)(2,1)S(1)} async-done(((bf16[16,8,512]{2,1,0:T(8,128)(2,1)}), bf16[16,8,512]{2,1,0:T(8,128)(2,1)S(1)}, u32[]{:S(2)}, u32[]{:S(2)}) %all-to-all-start.4) | async-done | bytes 131104 | tf_op jit(solution)/shard_map/all_to_all | solution.py:402
  115.1 1.1 shard_map.83
Async XLA Ops:
  2.7 23.8 %all-to-all-start = ((bf16[8,256,256]{2,1,0:T(8,128)(2,1)}), bf16[8,256,256]{2,1,0:T(8,128)(2,1)S(1)}, u32[]{:S(2)}, u32[]{:S(2)}) async-start(bf16[8,256,256]{2,1,0:T(8,128)(2,1)} %shard_map.75), calls=%async_computation | async-start | bytes 2097152 | tf_op jit(solution)/shard_map/all_to_all | solution.py:404
  28.2 20.3 %collective-permute-start = (bf16[576,256]{1,0:T(8,128)(2,1)S(1)}, bf16[576,256]{1,0:T(8,128)(2,1)S(1)}, u32[]{:S(2)}, u32[]{:S(2)}) collective-permute-start(bf16[576,256]{1,0:T(8,128)(2,1)S(1)} %get-tuple-element.24), channel_id=1, source_target_pairs={{0,8},{8,16},{16,24},{24,32},{32,40},{40,48},{48,56},{56,64},{64,7... | collective-permute-start | bytes 884744 | tf_op jit(solution)/shard_map/ppermute | solution.py:399
  30.2 18.4 %collective-permute-start.1 = (bf16[576,256]{1,0:T(8,128)(2,1)S(1)}, bf16[576,256]{1,0:T(8,128)(2,1)S(1)}, u32[]{:S(2)}, u32[]{:S(2)}) collective-permute-start(bf16[576,256]{1,0:T(8,128)(2,1)S(1)} %get-tuple-element.25), channel_id=1, source_target_pairs={{0,504},{8,0},{16,8},{24,16},{32,24},{40,32},{48,40},{56,48},{64,5... | collective-permute-start | bytes 884744 | tf_op jit(solution)/shard_map/ppermute | solution.py:399
  39.4 25.0 %all-to-all-start.1 = ((bf16[16,8,512]{2,1,0:T(8,128)(2,1)}), bf16[16,8,512]{2,1,0:T(8,128)(2,1)S(1)}, u32[]{:S(2)}, u32[]{:S(2)}) async-start(bf16[16,8,512]{2,1,0:T(8,128)(2,1)} %get-tuple-element.29), calls=%async_computation.1 | async-start | bytes 262144 | tf_op jit(solution)/shard_map/all_to_all | solution.py:402
  78.0 16.6 %all-to-all-start.3 = ((bf16[4,48,512]{2,1,0:T(8,128)(2,1)}), bf16[4,48,512]{2,1,0:T(8,128)(2,1)S(1)}, u32[]{:S(2)}, u32[]{:S(2)}) async-start(bf16[4,48,512]{2,1,0:T(8,128)(2,1)} %get-tuple-element.38), calls=%async_computation.3 | async-start | bytes 393216 | tf_op jit(solution)/shard_map/all_to_all | solution.py:402
  85.5 14.1 %collective-permute-start.2 = (bf16[288,512]{1,0:T(8,128)(2,1)}, bf16[288,512]{1,0:T(8,128)(2,1)S(1)}, u32[]{:S(2)}, u32[]{:S(2)}) collective-permute-start(bf16[288,512]{1,0:T(8,128)(2,1)} %get-tuple-element.36), channel_id=1, source_target_pairs={{0,8},{8,16},{16,24},{24,32},{32,40},{40,48},{48,56},{56,64},{64,7... | collective-permute-start | bytes 884744 | tf_op jit(solution)/shard_map/ppermute | solution.py:399
  89.3 13.4 %collective-permute-start.3 = (bf16[288,512]{1,0:T(8,128)(2,1)}, bf16[288,512]{1,0:T(8,128)(2,1)S(1)}, u32[]{:S(2)}, u32[]{:S(2)}) collective-permute-start(bf16[288,512]{1,0:T(8,128)(2,1)} %get-tuple-element.37), channel_id=1, source_target_pairs={{0,504},{8,0},{16,8},{24,16},{32,24},{40,32},{48,40},{56,48},{64,5... | collective-permute-start | bytes 884744 | tf_op jit(solution)/shard_map/ppermute | solution.py:399
  95.5 19.6 %all-to-all-start.4 = ((bf16[16,8,512]{2,1,0:T(8,128)(2,1)}), bf16[16,8,512]{2,1,0:T(8,128)(2,1)S(1)}, u32[]{:S(2)}, u32[]{:S(2)}) async-start(bf16[16,8,512]{2,1,0:T(8,128)(2,1)} %shard_map.82), calls=%async_computation.4 | async-start | bytes 262144 | tf_op jit(solution)/shard_map/all_to_all | solution.py:402

commit v5 on v4

--- a/solution.py
+++ b/solution.py
@@ -156,7 +156,7 @@
     to_next[:TOKENS, :] = whole[SHARES // 2 :, : 2 * SHARE, :].reshape(TOKENS, SPAN)
 
 
-def own_kernel(spot, pooled, _low, _high, own, gather):
+def own_kernel(spot, pooled, own, gather, scatter, weight):
     far_at, near_at = spot[0] >> NEAR_BITS, spot[0] & (NEAR_PEERS - 1)
     index, column = grid(NEAR, OWN)
     slot, inside = near_place(index)
@@ -166,6 +166,18 @@
     slot, inside = near_place(index)
     valid, offset, place = held_slot(inside)
     gather[...] = ones(valid & (column == (offset ^ far_at) * FAR_ROWS + place))
+    row, column = grid(FAR, NEAR)
+    _, inside = near_place(column)
+    valid, offset, place = held_slot(inside)
+    scatter[...] = ones(valid & (offset == ((row >> 3) ^ far_at)) & (place == (row & 7)))
+    token, column = grid(TOKENS, FAR)
+    valid, source = far_slot((column >> 3) ^ far_at, column & 7)
+    result = jnp.zeros((TOKENS, FAR), F32)
+    for level in range(2, LEVELS):
+        shift = 4 + level
+        hit = valid & (source == START[level] + (token >> shift))
+        result = jnp.where(hit, 1.0 / (1 << shift), result)
+    weight[...] = result.astype(BF16)
 
 
 def near_kernel(own, gather, far, near_send):
@@ -179,6 +191,10 @@
         .astype(BF16)
         .reshape(FAR_PEERS, FAR_ROWS, 2 * SPAN)
     )
+
+
+COLUMNS = [slice(head * HEAD_DIM, (head + 1) * HEAD_DIM) for head in range(2)]
+UNITS = [(head, block) for head in range(2) for block in range(2)]
 
 
 def part_rows(part):
@@ -215,10 +231,28 @@
     return jnp.concatenate([near[: 2 * LEAF], near[2 * LEAF :] + bias], axis=0)
 
 
-def forward_kernel(
-    spot, whole, low, high, near_rows,
+def near_forward_kernel(spot, whole, low, high, mixed, stats, keys, values):
+    for head, columns in enumerate(COLUMNS):
+        ext(whole, low, high, 0, columns, keys.at[head])
+        ext(whole, low, high, 1, columns, values.at[head])
+    value_t = [jnp.transpose(values[head]) for head in range(2)]
+    scores = [
+        near_scores(spot, keys.at[head], load(whole, 2, block, COLUMNS[head]), block)
+        for head, block in UNITS
+    ]
+    for unit, (head, block) in enumerate(UNITS):
+        top = jnp.max(scores[unit], axis=0, keepdims=True)
+        near = jnp.exp2(scores[unit] - top)
+        stats[unit : unit + 1, :] = top
+        stats[4 + unit : 5 + unit, :] = jnp.sum(near, axis=0, keepdims=True)
+        window = slice(block * LEAF, block * LEAF + 3 * LEAF)
+        mixed[unit] = dot(value_t[head][:, window], near.astype(BF16), NN)
+
+
+def far_kernel(
+    spot, whole, low, high, near_rows, mixed, near_stats,
     attended, far_query, stats, near_send, zero_back,
-    keys, values, coarse,
+    coarse,
 ):
     factor = HEAD_DIM ** (-0.5)
     binary = factor * math.log2(math.e)
@@ -238,53 +272,42 @@
     for offset in (2, 3):
         start = first + (offset - 2) * COUNT[1]
         coarse[start : start + COUNT[1], :] = near_rows[near_at ^ offset, HELD:, :]
-    heads, units = range(2), [(head, block) for head in range(2) for block in range(2)]
-    columns = [slice(head * HEAD_DIM, (head + 1) * HEAD_DIM) for head in heads]
-    for head in heads:
-        ext(whole, low, high, 0, columns[head], keys.at[head])
-        ext(whole, low, high, 1, columns[head], values.at[head])
-    far_key = [coarse[:, part_columns(0, head)] for head in heads]
-    far_value = [coarse[:, part_columns(1, head)] for head in heads]
-    value_t = [jnp.transpose(values[head]) for head in heads]
-    far_key_t = [jnp.transpose(far_key[head]) for head in heads]
-    far_value_t = [jnp.transpose(far_value[head]) for head in heads]
-    query = [load(whole, 2, block, columns[head]) for head, block in units]
-    grad = [load(whole, 3, block, columns[head]) for head, block in units]
-    state = []
-    for unit, (head, block) in enumerate(units):
-        near = near_scores(spot, keys.at[head], query[unit], block)
-        far = dot(far_key[head], query[unit], NT) * binary + math.log2(RATIO)
-        slope = dot(far_value[head], grad[unit], NT)
-        state.append((near, far, slope))
-    lows = []
-    for unit, (head, block) in enumerate(units):
-        near, far, slope = state[unit]
-        top = jnp.maximum(jnp.max(near, axis=0, keepdims=True), jnp.max(far, axis=0, keepdims=True))
-        near = jnp.exp2(near - top)
-        far = jnp.exp2(far - top)
-        total = jnp.sum(near, axis=0, keepdims=True) + jnp.sum(far, axis=0, keepdims=True)
+    key = [coarse[:, part_columns(0, head)] for head in range(2)]
+    value = [coarse[:, part_columns(1, head)] for head in range(2)]
+    key_t = [jnp.transpose(key[head]) for head in range(2)]
+    value_t = [jnp.transpose(value[head]) for head in range(2)]
+    query = [load(whole, 2, block, COLUMNS[head]) for head, block in UNITS]
+    grad = [load(whole, 3, block, COLUMNS[head]) for head, block in UNITS]
+    scores = [
+        dot(key[head], query[unit], NT) * binary + math.log2(RATIO)
+        for unit, (head, _) in enumerate(UNITS)
+    ]
+    slopes = [dot(value[head], grad[unit], NT) for unit, (head, _) in enumerate(UNITS)]
+    probs, lows, outs = [], [], []
+    for unit, (head, block) in enumerate(UNITS):
+        near_top = near_stats[unit : unit + 1, :]
+        top = jnp.maximum(near_top, jnp.max(scores[unit], axis=0, keepdims=True))
+        far = jnp.exp2(scores[unit] - top)
+        shrink = jnp.exp2(near_top - top)
+        total = near_stats[4 + unit : 5 + unit, :] * shrink + jnp.sum(far, axis=0, keepdims=True)
         inverse = 1.0 / total
-        far = far * inverse
-        far_low = far.astype(BF16)
-        near_low = (near * inverse).astype(BF16)
         stats[unit : unit + 1, :] = top
         stats[4 + unit : 5 + unit, :] = inverse
-        window = slice(block * LEAF, block * LEAF + 3 * LEAF)
-        mixed_t = dot(value_t[head][:, window], near_low, NN) + dot(far_value_t[head], far_low, NN)
-        lows.append((far, far_low, mixed_t, slope))
+        probs.append(far * inverse)
+        lows.append(probs[unit].astype(BF16))
+        outs.append(mixed[unit] * (shrink * inverse) + dot(value_t[head], lows[unit], NN))
     key_grads, value_grads = [], []
-    for unit, (head, block) in enumerate(units):
-        far, far_low, mixed_t, slope = lows[unit]
+    for unit, (head, block) in enumerate(UNITS):
         grad_t = jnp.transpose(grad[unit].astype(F32))
-        delta = jnp.sum(grad_t * mixed_t, axis=0, keepdims=True)
+        delta = jnp.sum(grad_t * outs[unit], axis=0, keepdims=True)
         stats[8 + unit : 9 + unit, :] = delta
-        score = (far * (slope - delta)).astype(BF16)
-        far_query[unit] = dot(far_key_t[head], score, NN)
+        score = (probs[unit] * (slopes[unit] - delta)).astype(BF16)
+        far_query[unit] = dot(key_t[head], score, NN)
         rows = slice(block * LEAF, (block + 1) * LEAF)
-        attended[rows, columns[head]] = jnp.transpose(mixed_t).astype(BF16)
+        attended[rows, COLUMNS[head]] = jnp.transpose(outs[unit]).astype(BF16)
         key_grads.append(dot(score, query[unit], NN))
-        value_grads.append(dot(far_low, grad[unit], NN))
-    for head in heads:
+        value_grads.append(dot(lows[unit], grad[unit], NN))
+    for head in range(2):
         key_grad = ((key_grads[2 * head] + key_grads[2 * head + 1]) * factor).astype(BF16)
         value_grad = (value_grads[2 * head] + value_grads[2 * head + 1]).astype(BF16)
         for part, far_grad in ((0, key_grad), (1, value_grad)):
@@ -301,55 +324,45 @@
 
 def backward_kernel(
     spot, whole, low, high, stats, far_query, level_zero,
-    query_grad, centre, to_prev, to_next, scatter,
-    keys, values, key_grad, value_grad,
+    query_grad, centre, to_prev, to_next,
+    keys, values,
 ):
     factor = HEAD_DIM ** (-0.5)
+    for head, columns in enumerate(COLUMNS):
+        ext(whole, low, high, 0, columns, keys.at[head])
+        ext(whole, low, high, 1, columns, values.at[head])
+    key_t = [jnp.transpose(keys[head]) for head in range(2)]
+    query = [load(whole, 2, block, COLUMNS[head]) for head, block in UNITS]
+    grad = [load(whole, 3, block, COLUMNS[head]) for head, block in UNITS]
+    windows = [slice(block * LEAF, block * LEAF + 3 * LEAF) for block in range(2)]
+    lows, scores = [], []
+    for unit, (head, block) in enumerate(UNITS):
+        near = near_scores(spot, keys.at[head], query[unit], block)
+        slope = dot(values[head, windows[block], :], grad[unit], NT)
+        near = jnp.exp2(near - stats[unit : unit + 1, :]) * stats[4 + unit : 5 + unit, :]
+        lows.append(near.astype(BF16))
+        scores.append((near * (slope - stats[8 + unit : 9 + unit, :])).astype(BF16))
+    for unit, (head, block) in enumerate(UNITS):
+        query_t = dot(key_t[head][:, windows[block]], scores[unit], NN) + far_query[unit]
+        rows = slice(block * LEAF, (block + 1) * LEAF)
+        query_grad[rows, COLUMNS[head]] = jnp.transpose(query_t * factor).astype(BF16)
     for head in range(2):
-        columns = slice(head * HEAD_DIM, (head + 1) * HEAD_DIM)
-        ext(whole, low, high, 0, columns, keys)
-        ext(whole, low, high, 1, columns, values)
-        key_t = jnp.transpose(keys[...])
-        for block in range(2):
-            unit = 2 * head + block
-            query = load(whole, 2, block, columns)
-            grad = load(whole, 3, block, columns)
-            window = slice(block * LEAF, block * LEAF + 3 * LEAF)
-            near = near_scores(spot, keys, query, block)
-            near = jnp.exp2(near - stats[unit : unit + 1, :]) * stats[4 + unit : 5 + unit, :]
-            near_low = near.astype(BF16)
-            slope = dot(values[window, :], grad, NT) - stats[8 + unit : 9 + unit, :]
-            score = (near * slope).astype(BF16)
-            query_t = dot(key_t[:, window], score, NN) + far_query[unit]
-            query_grad[block * LEAF : (block + 1) * LEAF, columns] = jnp.transpose(
-                query_t * factor
-            ).astype(BF16)
-            near_key_grad = dot(score, query, NN) * factor
-            near_value_grad = dot(near_low, grad, NN)
-            if block == 0:
-                key_grad[: 3 * LEAF, :] = near_key_grad
-                value_grad[: 3 * LEAF, :] = near_value_grad
-            else:
-                key_grad[LEAF : 3 * LEAF, :] += near_key_grad[: 2 * LEAF]
-                value_grad[LEAF : 3 * LEAF, :] += near_value_grad[: 2 * LEAF]
-                key_grad[3 * LEAF :, :] = near_key_grad[2 * LEAF :]
-                value_grad[3 * LEAF :, :] = near_value_grad[2 * LEAF :]
-        for part, store in ((0, key_grad), (1, value_grad)):
+        for part, lefts, rights, scale in ((0, scores, query, factor), (1, lows, grad, None)):
             place = part_columns(part, head)
-            to_prev[:LEAF, place] = store[:LEAF, :].astype(BF16)
-            centre[:, place] = store[LEAF : LEAF + TOKENS, :]
-            to_next[:LEAF, place] = store[LEAF + TOKENS :, :].astype(BF16)
+            first, second = 2 * head, 2 * head + 1
+            early = dot(lefts[first], rights[first], NN)
+            late = dot(lefts[second], rights[second], NN)
+            if scale is not None:
+                early, late = early * scale, late * scale
+            to_prev[:LEAF, place] = early[:LEAF].astype(BF16)
+            centre[:, place] = (early[LEAF:] + late[: 2 * LEAF]).astype(BF16)
+            to_next[:LEAF, place] = late[2 * LEAF :].astype(BF16)
     to_prev[LEAF:, :] = level_zero[...]
     to_next[LEAF:, :] = level_zero[...]
-    row, column = grid(FAR, NEAR)
-    _, inside = near_place(column)
-    valid, offset, place = held_slot(inside)
-    hit = valid & (offset == ((row >> 3) ^ (spot[0] >> NEAR_BITS))) & (place == (row & 7))
-    scatter[...] = ones(hit)
 
 
 def gather_kernel(
-    spot, centre, from_prev, from_next, near, total, weight, level_zero
+    spot, centre, from_prev, from_next, near, total, level_zero
 ):
     even = (spot[0] & 1) == 0
     for rim, flag in ((from_next, even), (from_prev, jnp.logical_not(even))):
@@ -360,7 +373,7 @@
 
     token, column = grid(TOKENS, COUNT[0])
     own = jnp.where((token >> 4) == column, 1.0 / RATIO, 0.0).astype(BF16)
-    spread = centre[...] + dot(own, level_zero[...], NN)
+    spread = centre[...].astype(F32) + dot(own, level_zero[...], NN)
     token, column = grid(TOKENS, COUNT[1])
     own = jnp.where((token >> 5) == column, 1.0 / (2 * RATIO), 0.0).astype(BF16)
     near_at = spot[0] & (NEAR_PEERS - 1)
@@ -368,14 +381,6 @@
         spread = spread + dot(own, near[near_at ^ offset, HELD:, :], NN)
     total[:LEAF, :] = spread[:LEAF] + from_prev[:LEAF, :].astype(F32)
     total[LEAF:, :] = spread[LEAF:] + from_next[:LEAF, :].astype(F32)
-    token, column = grid(TOKENS, FAR)
-    valid, source = far_slot((column >> 3) ^ (spot[0] >> NEAR_BITS), column & 7)
-    result = jnp.zeros((TOKENS, FAR), F32)
-    for level in range(2, LEVELS):
-        shift = 4 + level
-        hit = valid & (source == START[level] + (token >> shift))
-        result = jnp.where(hit, 1.0 / (1 << shift), result)
-    weight[...] = result.astype(BF16)
 
 
 def finish_kernel(total, weight, far, key_grad, value_grad):
@@ -411,16 +416,29 @@
     low = ring(to_next, 1)
     high = ring(to_prev, -1)
     far = exchange(far_send, FAR_GROUPS)
-    own, gather = call(
+    own, gather, scatter, weight = call(
         own_kernel,
-        (shape(NEAR, 2 * SPAN, kind=F32), shape(NEAR, FAR)),
-        specs=[SMEM] + [VMEM] * 3,
-        cost=pl.CostEstimate(flops=5000000000, bytes_accessed=0, transcendentals=0),
-    )(spot, pooled, low, high)
+        (
+            shape(NEAR, 2 * SPAN, kind=F32),
+            shape(NEAR, FAR),
+            shape(FAR, NEAR),
+            shape(TOKENS, FAR),
+        ),
+        specs=[SMEM, VMEM],
+        cost=None,
+    )(spot, pooled)
     near = exchange(call(near_kernel, near_slots, count=3)(own, gather, far), NEAR_GROUPS)
     span = 2 * LEAF + TOKENS
+    sides = [pltpu.VMEM((2, span, HEAD_DIM), BF16)] * 2
+    mixed, near_stats = call(
+        near_forward_kernel,
+        (shape(4, HEAD_DIM, LEAF, kind=F32), shape(8, LEAF, kind=F32)),
+        sides,
+        [SMEM] + [VMEM] * 3,
+        cost=pl.CostEstimate(flops=5000000000, bytes_accessed=0, transcendentals=0),
+    )(spot, whole, low, high)
     attended, far_query, stats, near_send, zero_back = call(
-        forward_kernel,
+        far_kernel,
         (
             shape(TOKENS, SPAN),
             shape(4, HEAD_DIM, LEAF, kind=F32),
@@ -428,30 +446,24 @@
             near_slots,
             shape(COUNT[0], 2 * SPAN),
         ),
-        [pltpu.VMEM((2, span, HEAD_DIM), BF16)] * 2 + [pltpu.VMEM((COARSE, 2 * SPAN), BF16)],
-        [SMEM] + [VMEM] * 4,
-    )(spot, whole, low, high, near)
+        [pltpu.VMEM((COARSE, 2 * SPAN), BF16)],
+        [SMEM] + [VMEM] * 6,
+    )(spot, whole, low, high, near, mixed, near_stats)
     near = exchange(near_send, NEAR_GROUPS)
     rim_grad = shape(LEAF + COUNT[0], 2 * SPAN)
-    query_grad, centre, to_prev, to_next, scatter = call(
+    query_grad, centre, to_prev, to_next = call(
         backward_kernel,
-        (
-            shape(TOKENS, SPAN),
-            shape(TOKENS, 2 * SPAN, kind=F32),
-            rim_grad,
-            rim_grad,
-            shape(FAR, NEAR),
-        ),
-        [pltpu.VMEM((span, HEAD_DIM), BF16)] * 2 + [pltpu.VMEM((span, HEAD_DIM), F32)] * 2,
+        (shape(TOKENS, SPAN), shape(TOKENS, 2 * SPAN), rim_grad, rim_grad),
+        sides,
         [SMEM] + [VMEM] * 6,
         cost=None,
     )(spot, whole, low, high, stats, far_query, zero_back)
     from_next = ring(to_prev, -1)
     from_prev = ring(to_next, 1)
     far = exchange(call(far_send_kernel, far_slots, count=2)(scatter, near), FAR_GROUPS)
-    total, weight = call(
+    total = call(
         gather_kernel,
-        (shape(TOKENS, 2 * SPAN, kind=F32), shape(TOKENS, FAR)),
+        shape(TOKENS, 2 * SPAN, kind=F32),
         [pltpu.VMEM((COUNT[0], 2 * SPAN), BF16)],
         [SMEM] + [VMEM] * 4,
         cost=pl.CostEstimate(flops=5000000000, bytes_accessed=0, transcendentals=0),

time: 117 us -> 110 us (0.940)
  blocking collectives: 9.69 us -> 0 us
  starting transfers between devices: 46.2 us -> 52.6 us
  waiting for transfers between devices: 43.9 us -> 39.5 us
    all_to_all x1 -> x0, blocking collectives: 9.69 us -> none  [exchange(): return lax.all_to_all(block, 'context', 0, 0, axis_index_groups=groups)]
    all_to_all x3 -> x4, starting transfers between devices: 16.7 us -> 23.7 us  [exchange(): return lax.all_to_all(block, 'context', 0, 0, axis_index_groups=groups)]
    all_to_all x3 -> x4, waiting for transfers between devices: 26.3 us -> 21 us  [exchange(): return lax.all_to_all(block, 'context', 0, 0, axis_index_groups=groups)]
    pallas_call x4 -> x5, Pallas kernels: 9.68 us -> 9.81 us  [the longest x1 3.48 us: body(): call(backward_kernel, (shape(TOKENS, SPAN), shape(TOKENS, 2 * SPAN), rim_...]
  transfers between devices with their start and end apart: 8 -> 9, of which waited for: 4 -> 5; matrix products, arithmetic and copies ran while one was open for 0% -> 0% of each run, Pallas kernels for 6% -> 8%
where the time goes in v5:
time: 110 us; the launch traced here: 109 us
  starting transfers between devices  52.6 us (48%)
  waiting for transfers between devices  39.5 us (36%)
  Pallas kernels  16.3 us (15%)
    all_to_all x4, starting transfers between devices, exchange(): return lax.all_to_all(block, 'context', 0, 0, axis_index_groups=groups)  23.7 us
    all_to_all x4, waiting for transfers between devices, exchange(): return lax.all_to_all(block, 'context', 0, 0, axis_index_groups=groups)  21 us
    ppermute x4, starting transfers between devices, ring(): return lax.ppermute(block, 'context', pairs)  19.6 us
    all_to_all x1, waiting for transfers between devices, body(): whole = lax.all_to_all(pack(key, value, query, cotangent), 'head', 0, 0)  14.5 us
    all_to_all x1, starting transfers between devices, body(): whole = lax.all_to_all(pack(key, value, query, cotangent), 'head', 0, 0)  9.3 us
    ppermute x4, waiting for transfers between devices, ring(): return lax.ppermute(block, 'context', pairs)  4.02 us
    pallas_call x1, Pallas kernels, body(): call(backward_kernel, (shape(TOKENS, SPAN), shape(TOKENS, 2 * SPAN), rim_...  3.48 us
    pallas_call x1, Pallas kernels, body(): call(far_kernel, (shape(TOKENS, SPAN), shape(4, HEAD_DIM, LEAF, kind=F32)...  2.34 us
  transfers between devices with their start and end apart: 9, of which 5 were waited for; matrix products, arithmetic and copies ran while one was open for 0% of the time, Pallas kernels for 8%

profile of v5, /device:TPU:8, one launch (start us, length us, event | category | flops | bytes accessed | tf_op | source)
XLA Modules:
  0.0 109.3 jit_solution(16934550657002408042)
XLA Ops:
  0.6 2.0 %shard_map.75 = bf16[8,256,256]{2,1,0:T(8,128)(2,1)} custom-call(bf16[64,2048]{1,0:T(8,128)(2,1)} %key.1, bf16[64,2048]{1,0:T(8,128)(2,1)} %value.1, bf16[64,2048]{1,0:T(8,128)(2,1)} %query.1, bf16[64,2048]{1,0:T(8,128)(2,1)} %cotangent.1), custom_call_target="tpu_custom_call" | custom-call | tf_op jit(solution)/shard_map/pallas_call | solution.py:120
  2.6 9.3 %all-to-all-start = ((bf16[8,256,256]{2,1,0:T(8,128)(2,1)}), bf16[8,256,256]{2,1,0:T(8,128)(2,1)S(1)}, u32[]{:S(2)}, u32[]{:S(2)}) async-start(bf16[8,256,256]{2,1,0:T(8,128)(2,1)} %shard_map.75), calls=%async_computation | async-start | bytes 2097152 | tf_op jit(solution)/shard_map/all_to_all | solution.py:409
  11.9 0.1 pad_add_fusion.spot
  12.0 14.5 %all-to-all-done.whole = bf16[8,256,256]{2,1,0:T(8,128)(2,1)S(1)} async-done(((bf16[8,256,256]{2,1,0:T(8,128)(2,1)}), bf16[8,256,256]{2,1,0:T(8,128)(2,1)S(1)}, u32[]{:S(2)}, u32[]{:S(2)}) %all-to-all-start) | async-done | bytes 1048608 | tf_op jit(solution)/shard_map/all_to_all | solution.py:409
  26.5 1.7 %shard_map.76 = (bf16[64,512]{1,0:T(8,128)(2,1)S(1)}, bf16[16,8,512]{2,1,0:T(8,128)(2,1)}, bf16[576,256]{1,0:T(8,128)(2,1)S(1)}, bf16[576,256]{1,0:T(8,128)(2,1)S(1)}) custom-call(s32[2]{0:T(128)S(1)} %pad_add_fusion.spot, bf16[8,256,256]{2,1,0:T(8,128)(2,1)S(1)} %all-to-all-done.whole), custom_call_target="tpu_custom_call" | custom-call | tf_op jit(solution)/shard_map/pallas_call | solution.py:413
  28.2 13.3 %all-to-all-start.1 = ((bf16[16,8,512]{2,1,0:T(8,128)(2,1)}), bf16[16,8,512]{2,1,0:T(8,128)(2,1)S(1)}, u32[]{:S(2)}, u32[]{:S(2)}) async-start(bf16[16,8,512]{2,1,0:T(8,128)(2,1)} %get-tuple-element.30), calls=%async_computation.1 | async-start | bytes 262144 | tf_op jit(solution)/shard_map/all_to_all | solution.py:407
  41.5 2.9 %collective-permute-start = (bf16[576,256]{1,0:T(8,128)(2,1)S(1)}, bf16[576,256]{1,0:T(8,128)(2,1)S(1)}, u32[]{:S(2)}, u32[]{:S(2)}) collective-permute-start(bf16[576,256]{1,0:T(8,128)(2,1)S(1)} %get-tuple-element.25), channel_id=1, source_target_pairs={{0,8},{8,16},{16,24},{24,32},{32,40},{40,48},{48,56},{56,64},{64,7... | collective-permute-start | bytes 884744 | tf_op jit(solution)/shard_map/ppermute | solution.py:404
  44.4 7.5 %collective-permute-start.1 = (bf16[576,256]{1,0:T(8,128)(2,1)S(1)}, bf16[576,256]{1,0:T(8,128)(2,1)S(1)}, u32[]{:S(2)}, u32[]{:S(2)}) collective-permute-start(bf16[576,256]{1,0:T(8,128)(2,1)S(1)} %get-tuple-element.26), channel_id=1, source_target_pairs={{0,504},{8,0},{16,8},{24,16},{32,24},{40,32},{48,40},{56,48},{64,5... | collective-permute-start | bytes 884744 | tf_op jit(solution)/shard_map/ppermute | solution.py:404
  51.9 1.0 shard_map.77
  52.9 6.3 %all-to-all-done.1.far = bf16[16,8,512]{2,1,0:T(8,128)(2,1)S(1)} async-done(((bf16[16,8,512]{2,1,0:T(8,128)(2,1)}), bf16[16,8,512]{2,1,0:T(8,128)(2,1)S(1)}, u32[]{:S(2)}, u32[]{:S(2)}) %all-to-all-start.1) | async-done | bytes 131104 | tf_op jit(solution)/shard_map/all_to_all | solution.py:407
  59.3 0.9 shard_map.78
  60.1 3.6 %all-to-all-start.2 = ((bf16[4,48,512]{2,1,0:T(8,128)(2,1)}), bf16[4,48,512]{2,1,0:T(8,128)(2,1)S(1)}, u32[]{:S(2)}, u32[]{:S(2)}) async-start(bf16[4,48,512]{2,1,0:T(8,128)(2,1)} %shard_map.78), calls=%async_computation.2 | async-start | bytes 393216 | tf_op jit(solution)/shard_map/all_to_all | solution.py:407
  63.7 0.0 collective-permute-done.low
  63.7 0.0 collective-permute-done.1.high
  63.7 1.9 %shard_map.79 = (f32[4,128,256]{2,1,0:T(8,128)S(1)}, f32[8,256]{1,0:T(8,128)S(1)}) custom-call(s32[2]{0:T(128)S(1)} %pad_add_fusion.spot, bf16[8,256,256]{2,1,0:T(8,128)(2,1)S(1)} %all-to-all-done.whole, bf16[576,256]{1,0:T(8,128)(2,1)S(1)} %collective-permute-done.low, bf16[576,256]{1,0:T(8,128)(2,1)S(1)} %collective-permute-done.1.high), custom_call_target="tpu_custom_call" | custom-call | flops 5000000000 | tf_op jit(solution)/shard_map/pallas_call | solution.py:433
  65.6 4.3 %all-to-all-done.2.near_rows = bf16[4,48,512]{2,1,0:T(8,128)(2,1)S(1)} async-done(((bf16[4,48,512]{2,1,0:T(8,128)(2,1)}), bf16[4,48,512]{2,1,0:T(8,128)(2,1)S(1)}, u32[]{:S(2)}, u32[]{:S(2)}) %all-to-all-start.2) | async-done | bytes 196640 | tf_op jit(solution)/shard_map/all_to_all | solution.py:407
  70.0 2.3 %shard_map.80 = (bf16[512,256]{1,0:T(8,128)(2,1)}, f32[4,128,256]{2,1,0:T(8,128)S(1)}, f32[16,256]{1,0:T(8,128)S(1)}, bf16[4,48,512]{2,1,0:T(8,128)(2,1)}, bf16[32,512]{1,0:T(8,128)(2,1)S(1)}) custom-call(s32[2]{0:T(128)S(1)} %pad_add_fusion.spot, bf16[8,256,256]{2,1,0:T(8,128)(2,1)S(1)} %all-to-all-done.whole, ...), custom_call_target="tpu_custom_call" | custom-call | tf_op jit(solution)/shard_map/pallas_call | solution.py:440
  72.3 3.4 %all-to-all-start.3 = ((bf16[4,48,512]{2,1,0:T(8,128)(2,1)}), bf16[4,48,512]{2,1,0:T(8,128)(2,1)S(1)}, u32[]{:S(2)}, u32[]{:S(2)}) async-start(bf16[4,48,512]{2,1,0:T(8,128)(2,1)} %get-tuple-element.41), calls=%async_computation.3 | async-start | bytes 393216 | tf_op jit(solution)/shard_map/all_to_all | solution.py:407
  75.7 3.5 %shard_map.81 = (bf16[512,256]{1,0:T(8,128)(2,1)}, bf16[512,512]{1,0:T(8,128)(2,1)S(1)}, bf16[288,512]{1,0:T(8,128)(2,1)S(1)}, bf16[288,512]{1,0:T(8,128)(2,1)}) custom-call(s32[2]{0:T(128)S(1)} %pad_add_fusion.spot, bf16[8,256,256]{2,1,0:T(8,128)(2,1)S(1)} %all-to-all-done.whole, bf16[576,256]{1,0:T(8,128)(2,1)S(1)} %collective-permute-done.low, ...), custom_call_target="tpu_custom_call" | custom-call | tf_op jit(solution)/shard_map/pallas_call | solution.py:454
  79.2 3.9 %collective-permute-start.2 = (bf16[288,512]{1,0:T(8,128)(2,1)}, bf16[288,512]{1,0:T(8,128)(2,1)S(1)}, u32[]{:S(2)}, u32[]{:S(2)}) collective-permute-start(bf16[288,512]{1,0:T(8,128)(2,1)} %get-tuple-element.39), channel_id=1, source_target_pairs={{0,8},{8,16},{16,24},{24,32},{32,40},{40,48},{48,56},{56,64},{64,7... | collective-permute-start | bytes 884744 | tf_op jit(solution)/shard_map/ppermute | solution.py:404
  83.0 5.3 %collective-permute-start.3 = (bf16[288,512]{1,0:T(8,128)(2,1)S(1)}, bf16[288,512]{1,0:T(8,128)(2,1)S(1)}, u32[]{:S(2)}, u32[]{:S(2)}) collective-permute-start(bf16[288,512]{1,0:T(8,128)(2,1)S(1)} %get-tuple-element.40), channel_id=1, source_target_pairs={{0,504},{8,0},{16,8},{24,16},{32,24},{40,32},{48,40},{56,48},{64,5... | collective-permute-start | bytes 884744 | tf_op jit(solution)/shard_map/ppermute | solution.py:404
  88.3 0.0 all-to-all-done.3.near
  88.3 0.8 shard_map.83
  89.2 3.5 %all-to-all-start.4 = ((bf16[16,8,512]{2,1,0:T(8,128)(2,1)}), bf16[16,8,512]{2,1,0:T(8,128)(2,1)S(1)}, u32[]{:S(2)}, u32[]{:S(2)}) async-start(bf16[16,8,512]{2,1,0:T(8,128)(2,1)} %shard_map.83), calls=%async_computation.4 | async-start | bytes 262144 | tf_op jit(solution)/shard_map/all_to_all | solution.py:407
  92.7 0.0 collective-permute-done.2.from_prev
  92.7 4.0 %collective-permute-done.3.from_next = bf16[288,512]{1,0:T(8,128)(2,1)S(1)} collective-permute-done((bf16[288,512]{1,0:T(8,128)(2,1)S(1)}, bf16[288,512]{1,0:T(8,128)(2,1)S(1)}, u32[]{:S(2)}, u32[]{:S(2)}) %collective-permute-start.3) | collective-permute-done | bytes 294944 | tf_op jit(solution)/shard_map/ppermute | solution.py:404
  96.7 1.1 %shard_map.82.total = f32[512,512]{1,0:T(8,128)S(1)} custom-call(s32[2]{0:T(128)S(1)} %pad_add_fusion.spot, bf16[512,512]{1,0:T(8,128)(2,1)S(1)} %get-tuple-element.38.centre, bf16[288,512]{1,0:T(8,128)(2,1)S(1)} %collective-permute-done.2.from_prev, bf16[288,512]{1,0:T(8,128)(2,1)S(1)} %collective-permute-done.3.from_next, ...), custom_call_target="tpu_custom_call" | custom-call | flops 5000000000 | tf_op jit(solution)/shard_map/pallas_call | solution.py:464
  97.8 10.4 %all-to-all-done.4.far = bf16[16,8,512]{2,1,0:T(8,128)(2,1)S(1)} async-done(((bf16[16,8,512]{2,1,0:T(8,128)(2,1)}), bf16[16,8,512]{2,1,0:T(8,128)(2,1)S(1)}, u32[]{:S(2)}, u32[]{:S(2)}) %all-to-all-start.4) | async-done | bytes 131104 | tf_op jit(solution)/shard_map/all_to_all | solution.py:407
  108.2 1.1 shard_map.84
Async XLA Ops:
  2.6 23.8 %all-to-all-start = ((bf16[8,256,256]{2,1,0:T(8,128)(2,1)}), bf16[8,256,256]{2,1,0:T(8,128)(2,1)S(1)}, u32[]{:S(2)}, u32[]{:S(2)}) async-start(bf16[8,256,256]{2,1,0:T(8,128)(2,1)} %shard_map.75), calls=%async_computation | async-start | bytes 2097152 | tf_op jit(solution)/shard_map/all_to_all | solution.py:409
  28.2 31.0 %all-to-all-start.1 = ((bf16[16,8,512]{2,1,0:T(8,128)(2,1)}), bf16[16,8,512]{2,1,0:T(8,128)(2,1)S(1)}, u32[]{:S(2)}, u32[]{:S(2)}) async-start(bf16[16,8,512]{2,1,0:T(8,128)(2,1)} %get-tuple-element.30), calls=%async_computation.1 | async-start | bytes 262144 | tf_op jit(solution)/shard_map/all_to_all | solution.py:407
  41.5 22.2 %collective-permute-start = (bf16[576,256]{1,0:T(8,128)(2,1)S(1)}, bf16[576,256]{1,0:T(8,128)(2,1)S(1)}, u32[]{:S(2)}, u32[]{:S(2)}) collective-permute-start(bf16[576,256]{1,0:T(8,128)(2,1)S(1)} %get-tuple-element.25), channel_id=1, source_target_pairs={{0,8},{8,16},{16,24},{24,32},{32,40},{40,48},{48,56},{56,64},{64,7... | collective-permute-start | bytes 884744 | tf_op jit(solution)/shard_map/ppermute | solution.py:404
  44.4 19.3 %collective-permute-start.1 = (bf16[576,256]{1,0:T(8,128)(2,1)S(1)}, bf16[576,256]{1,0:T(8,128)(2,1)S(1)}, u32[]{:S(2)}, u32[]{:S(2)}) collective-permute-start(bf16[576,256]{1,0:T(8,128)(2,1)S(1)} %get-tuple-element.26), channel_id=1, source_target_pairs={{0,504},{8,0},{16,8},{24,16},{32,24},{40,32},{48,40},{56,48},{64,5... | collective-permute-start | bytes 884744 | tf_op jit(solution)/shard_map/ppermute | solution.py:404
  60.1 9.8 %all-to-all-start.2 = ((bf16[4,48,512]{2,1,0:T(8,128)(2,1)}), bf16[4,48,512]{2,1,0:T(8,128)(2,1)S(1)}, u32[]{:S(2)}, u32[]{:S(2)}) async-start(bf16[4,48,512]{2,1,0:T(8,128)(2,1)} %shard_map.78), calls=%async_computation.2 | async-start | bytes 393216 | tf_op jit(solution)/shard_map/all_to_all | solution.py:407
  72.3 16.0 %all-to-all-start.3 = ((bf16[4,48,512]{2,1,0:T(8,128)(2,1)}), bf16[4,48,512]{2,1,0:T(8,128)(2,1)S(1)}, u32[]{:S(2)}, u32[]{:S(2)}) async-start(bf16[4,48,512]{2,1,0:T(8,128)(2,1)} %get-tuple-element.41), calls=%async_computation.3 | async-start | bytes 393216 | tf_op jit(solution)/shard_map/all_to_all | solution.py:407
  79.2 13.5 %collective-permute-start.2 = (bf16[288,512]{1,0:T(8,128)(2,1)}, bf16[288,512]{1,0:T(8,128)(2,1)S(1)}, u32[]{:S(2)}, u32[]{:S(2)}) collective-permute-start(bf16[288,512]{1,0:T(8,128)(2,1)} %get-tuple-element.39), channel_id=1, source_target_pairs={{0,8},{8,16},{16,24},{24,32},{32,40},{40,48},{48,56},{56,64},{64,7... | collective-permute-start | bytes 884744 | tf_op jit(solution)/shard_map/ppermute | solution.py:404
  83.0 13.7 %collective-permute-start.3 = (bf16[288,512]{1,0:T(8,128)(2,1)S(1)}, bf16[288,512]{1,0:T(8,128)(2,1)S(1)}, u32[]{:S(2)}, u32[]{:S(2)}) collective-permute-start(bf16[288,512]{1,0:T(8,128)(2,1)S(1)} %get-tuple-element.40), channel_id=1, source_target_pairs={{0,504},{8,0},{16,8},{24,16},{32,24},{40,32},{48,40},{56,48},{64,5... | collective-permute-start | bytes 884744 | tf_op jit(solution)/shard_map/ppermute | solution.py:404
  89.2 19.0 %all-to-all-start.4 = ((bf16[16,8,512]{2,1,0:T(8,128)(2,1)}), bf16[16,8,512]{2,1,0:T(8,128)(2,1)S(1)}, u32[]{:S(2)}, u32[]{:S(2)}) async-start(bf16[16,8,512]{2,1,0:T(8,128)(2,1)} %shard_map.83), calls=%async_computation.4 | async-start | bytes 262144 | tf_op jit(solution)/shard_map/all_to_all | solution.py:407

commit v6 on v5

--- a/solution.py
+++ b/solution.py
@@ -1,3 +1,4 @@
+import functools
 import math
 
 import jax
@@ -132,36 +133,27 @@
     )(*sources)
 
 
-def pool_kernel(spot, whole, pooled, far_send, to_next, to_prev):
+def layout_kernel(spot, means, own, gather, scatter, weight):
+    far_at, near_at = spot[0] >> NEAR_BITS, spot[0] & (NEAR_PEERS - 1)
+    row, token = grid(FAR, TOKENS)
+    valid, source = far_slot((row >> 3) ^ far_at, row & 7)
+    result = jnp.zeros((FAR, TOKENS), F32)
+    for level in range(2, LEVELS):
+        shift = 4 + level
+        hit = valid & (source == START[level] + (token >> shift))
+        result = jnp.where(hit, 1.0 / (1 << shift), result)
+    means[:FAR, :] = result.astype(BF16)
     row, token = grid(OWN, TOKENS)
-    weight = jnp.zeros((OWN, TOKENS), F32)
+    result = jnp.zeros((OWN, TOKENS), F32)
     for level in range(LEVELS):
         shift = 4 + level
-        hit = row == START[level] + lax.shift_right_logical(token, shift)
-        weight = jnp.where(hit, 1.0 / (1 << shift), weight)
-    weight = weight.astype(BF16)
-    row, column = grid(FAR, OWN)
-    valid, source = far_slot((row >> 3) ^ (spot[0] >> NEAR_BITS), row & 7)
-    spread = ones(valid & (column == source))
-    for part in range(2):
-        rows = whole[:, part * SHARE : (part + 1) * SHARE, :].reshape(TOKENS, SPAN)
-        means = dot(weight, rows, NN).astype(BF16)
-        columns = slice(part * SPAN, (part + 1) * SPAN)
-        pooled[:, columns] = means
-        place = slice(TOKENS + part * COUNT[0], TOKENS + (part + 1) * COUNT[0])
-        to_next[place, :] = means[: COUNT[0]]
-        to_prev[place, :] = means[: COUNT[0]]
-        far_send[:, :, columns] = dot(spread, means, NN).astype(BF16).reshape(FAR_PEERS, FAR_ROWS, SPAN)
-    to_prev[:TOKENS, :] = whole[: SHARES // 2, : 2 * SHARE, :].reshape(TOKENS, SPAN)
-    to_next[:TOKENS, :] = whole[SHARES // 2 :, : 2 * SHARE, :].reshape(TOKENS, SPAN)
-
-
-def own_kernel(spot, pooled, own, gather, scatter, weight):
-    far_at, near_at = spot[0] >> NEAR_BITS, spot[0] & (NEAR_PEERS - 1)
+        hit = row == START[level] + (token >> shift)
+        result = jnp.where(hit, 1.0 / (1 << shift), result)
+    means[FAR:, :] = result.astype(BF16)
     index, column = grid(NEAR, OWN)
     slot, inside = near_place(index)
     valid, source = near_slot(slot ^ near_at, inside)
-    own[...] = dot(ones(valid & (column == source)), pooled[...], NN)
+    own[...] = ones(valid & (column == source))
     index, column = grid(NEAR, FAR)
     slot, inside = near_place(index)
     valid, offset, place = held_slot(inside)
@@ -180,9 +172,29 @@
     weight[...] = result.astype(BF16)
 
 
+def pool_kernel(means, whole, pooled, far_send):
+    for part in range(2):
+        rows = whole[:, part_rows(part), :].reshape(TOKENS, SPAN)
+        result = dot(means[...], rows, NN).astype(BF16)
+        columns = slice(part * SPAN, (part + 1) * SPAN)
+        far_send[:, :, columns] = result[:FAR].reshape(FAR_PEERS, FAR_ROWS, SPAN)
+        pooled[:, columns] = result[FAR:]
+
+
+def rim_kernel(whole, pooled, spread, to_next, to_prev, own):
+    for part in range(2):
+        place = slice(TOKENS + part * COUNT[0], TOKENS + (part + 1) * COUNT[0])
+        means = pooled[: COUNT[0], part * SPAN : (part + 1) * SPAN]
+        to_next[place, :] = means
+        to_prev[place, :] = means
+    to_prev[:TOKENS, :] = whole[: SHARES // 2, : 2 * SHARE, :].reshape(TOKENS, SPAN)
+    to_next[:TOKENS, :] = whole[SHARES // 2 :, : 2 * SHARE, :].reshape(TOKENS, SPAN)
+    own[...] = dot(spread[...], pooled[...], NN).astype(BF16)
+
+
 def near_kernel(own, gather, far, near_send):
     held = dot(gather[...], far[...].reshape(FAR, 2 * SPAN), NN)
-    near_send[...] = (own[...] + held).astype(BF16).reshape(NEAR_PEERS, NEAR_ROWS, 2 * SPAN)
+    near_send[...] = (own[...].astype(F32) + held).astype(BF16).reshape(NEAR_PEERS, NEAR_ROWS, 2 * SPAN)
 
 
 def far_send_kernel(scatter, near, far_send):
@@ -231,28 +243,24 @@
     return jnp.concatenate([near[: 2 * LEAF], near[2 * LEAF :] + bias], axis=0)
 
 
-def near_forward_kernel(spot, whole, low, high, mixed, stats, keys, values):
+def near_forward_kernel(spot, whole, low, high, stats, keys):
     for head, columns in enumerate(COLUMNS):
         ext(whole, low, high, 0, columns, keys.at[head])
-        ext(whole, low, high, 1, columns, values.at[head])
-    value_t = [jnp.transpose(values[head]) for head in range(2)]
     scores = [
         near_scores(spot, keys.at[head], load(whole, 2, block, COLUMNS[head]), block)
         for head, block in UNITS
     ]
-    for unit, (head, block) in enumerate(UNITS):
+    for unit in range(len(UNITS)):
         top = jnp.max(scores[unit], axis=0, keepdims=True)
         near = jnp.exp2(scores[unit] - top)
         stats[unit : unit + 1, :] = top
         stats[4 + unit : 5 + unit, :] = jnp.sum(near, axis=0, keepdims=True)
-        window = slice(block * LEAF, block * LEAF + 3 * LEAF)
-        mixed[unit] = dot(value_t[head][:, window], near.astype(BF16), NN)
 
 
 def far_kernel(
-    spot, whole, low, high, near_rows, mixed, near_stats,
-    attended, far_query, stats, near_send, zero_back,
-    coarse,
+    spot, whole, low, high, near_rows, near_stats,
+    mixed_low, far_query, stats, near_send, zero_back,
+    coarse, keys, values,
 ):
     factor = HEAD_DIM ** (-0.5)
     binary = factor * math.log2(math.e)
@@ -272,6 +280,10 @@
     for offset in (2, 3):
         start = first + (offset - 2) * COUNT[1]
         coarse[start : start + COUNT[1], :] = near_rows[near_at ^ offset, HELD:, :]
+    for head, columns in enumerate(COLUMNS):
+        ext(whole, low, high, 0, columns, keys.at[head])
+        ext(whole, low, high, 1, columns, values.at[head])
+    near_value_t = [jnp.transpose(values[head]) for head in range(2)]
     key = [coarse[:, part_columns(0, head)] for head in range(2)]
     value = [coarse[:, part_columns(1, head)] for head in range(2)]
     key_t = [jnp.transpose(key[head]) for head in range(2)]
@@ -283,6 +295,10 @@
         for unit, (head, _) in enumerate(UNITS)
     ]
     slopes = [dot(value[head], grad[unit], NT) for unit, (head, _) in enumerate(UNITS)]
+    nears = [
+        near_scores(spot, keys.at[head], query[unit], block)
+        for unit, (head, block) in enumerate(UNITS)
+    ]
     probs, lows, outs = [], [], []
     for unit, (head, block) in enumerate(UNITS):
         near_top = near_stats[unit : unit + 1, :]
@@ -295,7 +311,11 @@
         stats[4 + unit : 5 + unit, :] = inverse
         probs.append(far * inverse)
         lows.append(probs[unit].astype(BF16))
-        outs.append(mixed[unit] * (shrink * inverse) + dot(value_t[head], lows[unit], NN))
+        near_low = (jnp.exp2(nears[unit] - top) * inverse).astype(BF16)
+        window = slice(block * LEAF, block * LEAF + 3 * LEAF)
+        outs.append(
+            dot(near_value_t[head][:, window], near_low, NN) + dot(value_t[head], lows[unit], NN)
+        )
     key_grads, value_grads = [], []
     for unit, (head, block) in enumerate(UNITS):
         grad_t = jnp.transpose(grad[unit].astype(F32))
@@ -303,8 +323,7 @@
         stats[8 + unit : 9 + unit, :] = delta
         score = (probs[unit] * (slopes[unit] - delta)).astype(BF16)
         far_query[unit] = dot(key_t[head], score, NN)
-        rows = slice(block * LEAF, (block + 1) * LEAF)
-        attended[rows, COLUMNS[head]] = jnp.transpose(outs[unit]).astype(BF16)
+        mixed_low[unit] = outs[unit].astype(BF16)
         key_grads.append(dot(score, query[unit], NN))
         value_grads.append(dot(lows[unit], grad[unit], NN))
     for head in range(2):
@@ -322,9 +341,44 @@
                 near_send[near_at ^ offset, HELD:, place] = far_grad[start : start + COUNT[1]]
 
 
+def rim_grad_kernel(block, spot, whole, rim, stats, level_zero, other, target, attended=None):
+    factor = HEAD_DIM ** (-0.5)
+    edge = 0 if block == 0 else spot[1] - 1
+    bias = jnp.where(spot[0] == edge, -1e30, 0.0).astype(F32)
+    half = SHARES // 2
+    keys, values = [
+        [
+            rim[:TOKENS, COLUMNS[head]]
+            .reshape(half, 2 * SHARE, HEAD_DIM)[:, part_rows(part)]
+            .reshape(LEAF, HEAD_DIM)
+            for head in range(2)
+        ]
+        for part in range(2)
+    ]
+    query = [load(whole, 2, block, COLUMNS[head]) for head in range(2)]
+    grad = [load(whole, 3, block, COLUMNS[head]) for head in range(2)]
+    near = [dot(keys[head], query[head], NT) for head in range(2)]
+    slope = [dot(values[head], grad[head], NT) for head in range(2)]
+    lows, scores = [], []
+    for head in range(2):
+        unit = 2 * head + block
+        probs = near[head] * (factor * math.log2(math.e)) + bias
+        probs = jnp.exp2(probs - stats[unit : unit + 1, :]) * stats[4 + unit : 5 + unit, :]
+        lows.append(probs.astype(BF16))
+        scores.append((probs * (slope[head] - stats[8 + unit : 9 + unit, :])).astype(BF16))
+    for head in range(2):
+        target[:LEAF, part_columns(0, head)] = (dot(scores[head], query[head], NN) * factor).astype(BF16)
+        target[:LEAF, part_columns(1, head)] = dot(lows[head], grad[head], NN).astype(BF16)
+    target[LEAF:, :] = level_zero[...]
+    if attended is not None:
+        for unit, (head, block) in enumerate(UNITS):
+            rows = slice(block * LEAF, (block + 1) * LEAF)
+            attended[rows, COLUMNS[head]] = jnp.transpose(other[unit])
+
+
 def backward_kernel(
-    spot, whole, low, high, stats, far_query, level_zero,
-    query_grad, centre, to_prev, to_next,
+    spot, whole, low, high, stats, far_query,
+    query_grad, centre,
     keys, values,
 ):
     factor = HEAD_DIM ** (-0.5)
@@ -350,44 +404,39 @@
         for part, lefts, rights, scale in ((0, scores, query, factor), (1, lows, grad, None)):
             place = part_columns(part, head)
             first, second = 2 * head, 2 * head + 1
-            early = dot(lefts[first], rights[first], NN)
-            late = dot(lefts[second], rights[second], NN)
+            early = dot(lefts[first][LEAF:], rights[first], NN)
+            late = dot(lefts[second][: 2 * LEAF], rights[second], NN)
             if scale is not None:
                 early, late = early * scale, late * scale
-            to_prev[:LEAF, place] = early[:LEAF].astype(BF16)
-            centre[:, place] = (early[LEAF:] + late[: 2 * LEAF]).astype(BF16)
-            to_next[:LEAF, place] = late[2 * LEAF :].astype(BF16)
-    to_prev[LEAF:, :] = level_zero[...]
-    to_next[LEAF:, :] = level_zero[...]
-
-
-def gather_kernel(
-    spot, centre, from_prev, from_next, near, total, level_zero
-):
-    even = (spot[0] & 1) == 0
-    for rim, flag in ((from_next, even), (from_prev, jnp.logical_not(even))):
-
-        @pl.when(flag)
-        def _():
-            level_zero[...] = rim[LEAF:, :]
-
+            centre[:, place] = (early + late).astype(BF16)
+
+
+def gather_kernel(spot, centre, from_prev, near, total, zero_weight):
     token, column = grid(TOKENS, COUNT[0])
-    own = jnp.where((token >> 4) == column, 1.0 / RATIO, 0.0).astype(BF16)
-    spread = centre[...].astype(F32) + dot(own, level_zero[...], NN)
+    odd = jnp.where((spot[0] & 1) == 1, 1.0 / RATIO, 0.0).astype(F32)
+    even = 1.0 / RATIO - odd
+    own = (token >> 4) == column
+    zero_weight[...] = jnp.where(own, even, 0.0).astype(BF16)
+    spread = dot(jnp.where(own, odd, 0.0).astype(BF16), from_prev[LEAF:, :], NN)
+    spread = spread + centre[...].astype(F32)
     token, column = grid(TOKENS, COUNT[1])
     own = jnp.where((token >> 5) == column, 1.0 / (2 * RATIO), 0.0).astype(BF16)
     near_at = spot[0] & (NEAR_PEERS - 1)
     for offset in (2, 3):
         spread = spread + dot(own, near[near_at ^ offset, HELD:, :], NN)
     total[:LEAF, :] = spread[:LEAF] + from_prev[:LEAF, :].astype(F32)
-    total[LEAF:, :] = spread[LEAF:] + from_next[:LEAF, :].astype(F32)
-
-
-def finish_kernel(total, weight, far, key_grad, value_grad):
+    total[LEAF:, :] = spread[LEAF:]
+
+
+def finish_kernel(total, weight, zero_weight, far, from_next, key_grad, value_grad):
     rows = far[...].reshape(FAR, 2 * SPAN)
-    result = (total[...] + dot(weight[...], rows, NN)).astype(BF16)
-    key_grad[...] = result[:, :SPAN]
-    value_grad[...] = result[:, SPAN:]
+    result = total[...] + dot(weight[...], rows, NN) + dot(zero_weight[...], from_next[LEAF:, :], NN)
+    low = result[:LEAF].astype(BF16)
+    high = (result[LEAF:] + from_next[:LEAF, :].astype(F32)).astype(BF16)
+    for block, part in ((0, low), (1, high)):
+        rows = slice(block * LEAF, (block + 1) * LEAF)
+        key_grad[rows, :] = part[:, :SPAN]
+        value_grad[rows, :] = part[:, SPAN:]
 
 
 FAR_GROUPS = [[far * NEAR_PEERS + near for far in range(FAR_PEERS)] for near in range(NEAR_PEERS)]
@@ -410,67 +459,77 @@
     near_slots = shape(NEAR_PEERS, NEAR_ROWS, 2 * SPAN)
     far_slots = shape(FAR_PEERS, FAR_ROWS, 2 * SPAN)
     rim = shape(TOKENS + 2 * COUNT[0], SPAN)
-    pooled, far_send, to_next, to_prev = call(
-        pool_kernel, (shape(OWN, 2 * SPAN), far_slots, rim, rim), specs=[SMEM, VMEM]
-    )(spot, whole)
-    low = ring(to_next, 1)
-    high = ring(to_prev, -1)
-    far = exchange(far_send, FAR_GROUPS)
-    own, gather, scatter, weight = call(
-        own_kernel,
+    means, spread, gather, scatter, weight = call(
+        layout_kernel,
         (
-            shape(NEAR, 2 * SPAN, kind=F32),
+            shape(FAR + OWN, TOKENS),
+            shape(NEAR, OWN),
             shape(NEAR, FAR),
             shape(FAR, NEAR),
             shape(TOKENS, FAR),
         ),
-        specs=[SMEM, VMEM],
+        specs=[SMEM],
         cost=None,
-    )(spot, pooled)
+    )(spot)
+    pooled, far_send = call(pool_kernel, (shape(OWN, 2 * SPAN), far_slots), count=2)(means, whole)
+    to_next, to_prev, own = call(rim_kernel, (rim, rim, shape(NEAR, 2 * SPAN)), count=3)(
+        whole, pooled, spread
+    )
+    low = ring(to_next, 1)
+    high = ring(to_prev, -1)
+    far = exchange(far_send, FAR_GROUPS)
     near = exchange(call(near_kernel, near_slots, count=3)(own, gather, far), NEAR_GROUPS)
     span = 2 * LEAF + TOKENS
     sides = [pltpu.VMEM((2, span, HEAD_DIM), BF16)] * 2
-    mixed, near_stats = call(
+    near_stats = call(
         near_forward_kernel,
-        (shape(4, HEAD_DIM, LEAF, kind=F32), shape(8, LEAF, kind=F32)),
-        sides,
+        shape(8, LEAF, kind=F32),
+        sides[:1],
         [SMEM] + [VMEM] * 3,
         cost=pl.CostEstimate(flops=5000000000, bytes_accessed=0, transcendentals=0),
     )(spot, whole, low, high)
-    attended, far_query, stats, near_send, zero_back = call(
+    mixed_low, far_query, stats, near_send, zero_back = call(
         far_kernel,
         (
-            shape(TOKENS, SPAN),
+            shape(4, HEAD_DIM, LEAF),
             shape(4, HEAD_DIM, LEAF, kind=F32),
             shape(16, LEAF, kind=F32),
             near_slots,
             shape(COUNT[0], 2 * SPAN),
         ),
-        [pltpu.VMEM((COARSE, 2 * SPAN), BF16)],
-        [SMEM] + [VMEM] * 6,
-    )(spot, whole, low, high, near, mixed, near_stats)
+        [pltpu.VMEM((COARSE, 2 * SPAN), BF16)] + sides,
+        [SMEM] + [VMEM] * 5,
+    )(spot, whole, low, high, near, near_stats)
     near = exchange(near_send, NEAR_GROUPS)
     rim_grad = shape(LEAF + COUNT[0], 2 * SPAN)
-    query_grad, centre, to_prev, to_next = call(
-        backward_kernel,
-        (shape(TOKENS, SPAN), shape(TOKENS, 2 * SPAN), rim_grad, rim_grad),
-        sides,
-        [SMEM] + [VMEM] * 6,
-        cost=None,
-    )(spot, whole, low, high, stats, far_query, zero_back)
-    from_next = ring(to_prev, -1)
+    to_next, attended = call(
+        functools.partial(rim_grad_kernel, 1),
+        (rim_grad, shape(TOKENS, SPAN)),
+        specs=[SMEM] + [VMEM] * 5,
+        cost=pl.CostEstimate(flops=5000000000, bytes_accessed=0, transcendentals=0),
+    )(spot, whole, high, stats, zero_back, mixed_low)
     from_prev = ring(to_next, 1)
     far = exchange(call(far_send_kernel, far_slots, count=2)(scatter, near), FAR_GROUPS)
-    total = call(
+    to_prev = call(
+        functools.partial(rim_grad_kernel, 0), rim_grad, specs=[SMEM] + [VMEM] * 5, cost=None
+    )(spot, whole, low, stats, zero_back, from_prev)
+    from_next = ring(to_prev, -1)
+    query_grad, centre = call(
+        backward_kernel,
+        (shape(TOKENS, SPAN), shape(TOKENS, 2 * SPAN)),
+        sides,
+        [SMEM] + [VMEM] * 5,
+        cost=pl.CostEstimate(flops=5000000000, bytes_accessed=0, transcendentals=0),
+    )(spot, whole, low, high, stats, far_query)
+    total, zero_weight = call(
         gather_kernel,
-        shape(TOKENS, 2 * SPAN, kind=F32),
-        [pltpu.VMEM((COUNT[0], 2 * SPAN), BF16)],
-        [SMEM] + [VMEM] * 4,
-        cost=pl.CostEstimate(flops=5000000000, bytes_accessed=0, transcendentals=0),
-    )(spot, centre, from_prev, from_next, near)
+        (shape(TOKENS, 2 * SPAN, kind=F32), shape(TOKENS, COUNT[0])),
+        specs=[SMEM] + [VMEM] * 3,
+        cost=None,
+    )(spot, centre, from_prev, near)
     key_grad, value_grad = call(
-        finish_kernel, (shape(TOKENS, SPAN), shape(TOKENS, SPAN)), count=3
-    )(total, weight, far)
+        finish_kernel, (shape(TOKENS, SPAN), shape(TOKENS, SPAN)), count=5
+    )(total, weight, zero_weight, far, from_next)
     return attended, query_grad, key_grad, value_grad
 
 

time: 110 us -> 105 us (0.955)
  the two profiles are of different devices: /device:TPU:8 before, /device:TPU:32 now
where the time goes in v6:
time: 105 us
  starting transfers between devices  46.3 us (44%)
  waiting for transfers between devices  38.8 us (37%)
  Pallas kernels  18.7 us (18%)
    all_to_all x4, starting transfers between devices, exchange(): return lax.all_to_all(block, 'context', 0, 0, axis_index_groups=groups)  27.9 us
    all_to_all x4, waiting for transfers between devices, exchange(): return lax.all_to_all(block, 'context', 0, 0, axis_index_groups=groups)  21.2 us
    all_to_all x1, waiting for transfers between devices, body(): whole = lax.all_to_all(pack(key, value, query, cotangent), 'head', 0, 0)  14.8 us
    ppermute x4, starting transfers between devices, ring(): return lax.ppermute(block, 'context', pairs)  13.9 us
    all_to_all x1, starting transfers between devices, body(): whole = lax.all_to_all(pack(key, value, query, cotangent), 'head', 0, 0)  4.48 us
    pallas_call x1, Pallas kernels, body(): call(backward_kernel, (shape(TOKENS, SPAN), shape(TOKENS, 2 * SPAN)), sid...  3.06 us
    pallas_call x1, Pallas kernels, body(): call(far_kernel, (shape(4, HEAD_DIM, LEAF), shape(4, HEAD_DIM, LEAF, kind...  3.06 us
    ppermute x4, waiting for transfers between devices, ring(): return lax.ppermute(block, 'context', pairs)  2.81 us
  transfers between devices with their start and end apart: 9, of which 7 were waited for; matrix products, arithmetic and copies ran while one was open for 0% of the time, Pallas kernels for 11%

profile of v6, /device:TPU:32, one launch (start us, length us, event | category | flops | bytes accessed | tf_op | source)
XLA Modules:
  0.0 104.7 jit_solution(2997310751702540866)
XLA Ops:
  0.6 2.0 %shard_map.75 = bf16[8,256,256]{2,1,0:T(8,128)(2,1)} custom-call(bf16[64,2048]{1,0:T(8,128)(2,1)} %key.1, bf16[64,2048]{1,0:T(8,128)(2,1)} %value.1, bf16[64,2048]{1,0:T(8,128)(2,1)} %query.1, bf16[64,2048]{1,0:T(8,128)(2,1)} %cotangent.1), custom_call_target="tpu_custom_call" | custom-call | tf_op jit(solution)/shard_map/pallas_call | solution.py:121
  2.7 4.5 %all-to-all-start = ((bf16[8,256,256]{2,1,0:T(8,128)(2,1)}), bf16[8,256,256]{2,1,0:T(8,128)(2,1)S(1)}, u32[]{:S(2)}, u32[]{:S(2)}) async-start(bf16[8,256,256]{2,1,0:T(8,128)(2,1)} %shard_map.75), calls=%async_computation | async-start | bytes 2097152 | tf_op jit(solution)/shard_map/all_to_all | solution.py:458
  7.1 0.1 pad_add_fusion.spot
  7.2 1.0 shard_map.76
  8.3 14.8 %all-to-all-done.whole = bf16[8,256,256]{2,1,0:T(8,128)(2,1)S(1)} async-done(((bf16[8,256,256]{2,1,0:T(8,128)(2,1)}), bf16[8,256,256]{2,1,0:T(8,128)(2,1)S(1)}, u32[]{:S(2)}, u32[]{:S(2)}) %all-to-all-start) | async-done | bytes 1048608 | tf_op jit(solution)/shard_map/all_to_all | solution.py:458
  23.1 0.9 shard_map.77
  24.0 16.8 %all-to-all-start.1 = ((bf16[16,8,512]{2,1,0:T(8,128)(2,1)}), bf16[16,8,512]{2,1,0:T(8,128)(2,1)S(1)}, u32[]{:S(2)}, u32[]{:S(2)}) async-start(bf16[16,8,512]{2,1,0:T(8,128)(2,1)} %get-tuple-element.34), calls=%async_computation.1 | async-start | bytes 262144 | tf_op jit(solution)/shard_map/all_to_all | solution.py:456
  40.8 0.2 shard_map.78
  41.0 2.9 %collective-permute-start = (bf16[576,256]{1,0:T(8,128)(2,1)S(1)}, bf16[576,256]{1,0:T(8,128)(2,1)S(1)}, u32[]{:S(2)}, u32[]{:S(2)}) collective-permute-start(bf16[576,256]{1,0:T(8,128)(2,1)S(1)} %get-tuple-element.30), channel_id=1, source_target_pairs={{0,504},{8,0},{16,8},{24,16},{32,24},{40,32},{48,40},{56,48},{64,5... | collective-permute-start | bytes 884744 | tf_op jit(solution)/shard_map/ppermute | solution.py:453
  43.9 2.9 %collective-permute-start.1 = (bf16[576,256]{1,0:T(8,128)(2,1)S(1)}, bf16[576,256]{1,0:T(8,128)(2,1)S(1)}, u32[]{:S(2)}, u32[]{:S(2)}) collective-permute-start(bf16[576,256]{1,0:T(8,128)(2,1)S(1)} %get-tuple-element.31), channel_id=1, source_target_pairs={{0,8},{8,16},{16,24},{24,32},{32,40},{40,48},{48,56},{56,64},{64,7... | collective-permute-start | bytes 884744 | tf_op jit(solution)/shard_map/ppermute | solution.py:453
  46.9 12.6 %all-to-all-done.1.far = bf16[16,8,512]{2,1,0:T(8,128)(2,1)S(1)} async-done(((bf16[16,8,512]{2,1,0:T(8,128)(2,1)}), bf16[16,8,512]{2,1,0:T(8,128)(2,1)S(1)}, u32[]{:S(2)}, u32[]{:S(2)}) %all-to-all-start.1) | async-done | bytes 131104 | tf_op jit(solution)/shard_map/all_to_all | solution.py:456
  59.4 0.9 shard_map.79
  60.3 3.4 %all-to-all-start.2 = ((bf16[4,48,512]{2,1,0:T(8,128)(2,1)}), bf16[4,48,512]{2,1,0:T(8,128)(2,1)S(1)}, u32[]{:S(2)}, u32[]{:S(2)}) async-start(bf16[4,48,512]{2,1,0:T(8,128)(2,1)} %shard_map.79), calls=%async_computation.2 | async-start | bytes 393216 | tf_op jit(solution)/shard_map/all_to_all | solution.py:456
  63.7 0.0 collective-permute-done.high.rim
  63.7 0.0 collective-permute-done.1.low.rim
  63.7 1.6 %shard_map.80.near_stats = f32[8,256]{1,0:T(8,128)S(1)} custom-call(s32[2]{0:T(128)S(1)} %pad_add_fusion.spot, bf16[8,256,256]{2,1,0:T(8,128)(2,1)S(1)} %all-to-all-done.whole, bf16[576,256]{1,0:T(8,128)(2,1)S(1)} %collective-permute-done.1.low.rim, bf16[576,256]{1,0:T(8,128)(2,1)S(1)} %collective-permute-done.high.rim), custom_call_target="tpu_custom_call" | custom-call | flops 5000000000 | tf_op jit(solution)/shard_map/pallas_call | solution.py:484
  65.3 4.1 %all-to-all-done.2.near_rows = bf16[4,48,512]{2,1,0:T(8,128)(2,1)S(1)} async-done(((bf16[4,48,512]{2,1,0:T(8,128)(2,1)}), bf16[4,48,512]{2,1,0:T(8,128)(2,1)S(1)}, u32[]{:S(2)}, u32[]{:S(2)}) %all-to-all-start.2) | async-done | bytes 196640 | tf_op jit(solution)/shard_map/all_to_all | solution.py:456
  69.4 3.1 %shard_map.81 = (bf16[4,128,256]{2,1,0:T(8,128)(2,1)S(1)}, f32[4,128,256]{2,1,0:T(8,128)S(1)}, f32[16,256]{1,0:T(8,128)S(1)}, bf16[4,48,512]{2,1,0:T(8,128)(2,1)}, bf16[32,512]{1,0:T(8,128)(2,1)S(1)}) custom-call(s32[2]{0:T(128)S(1)} %pad_add_fusion.spot, bf16[8,256,256]{2,1,0:T(8,128)(2,1)S(1)} %all-to-all-done.whole, ...), custom_call_target="tpu_custom_call" | custom-call | tf_op jit(solution)/shard_map/pallas_call | solution.py:491
  72.4 4.3 %all-to-all-start.3 = ((bf16[4,48,512]{2,1,0:T(8,128)(2,1)}), bf16[4,48,512]{2,1,0:T(8,128)(2,1)S(1)}, u32[]{:S(2)}, u32[]{:S(2)}) async-start(bf16[4,48,512]{2,1,0:T(8,128)(2,1)} %get-tuple-element.43), calls=%async_computation.3 | async-start | bytes 393216 | tf_op jit(solution)/shard_map/all_to_all | solution.py:456
  76.7 1.7 %shard_map.82 = (bf16[288,512]{1,0:T(8,128)(2,1)S(1)}, bf16[512,256]{1,0:T(8,128)(2,1)}) custom-call(s32[2]{0:T(128)S(1)} %pad_add_fusion.spot, bf16[8,256,256]{2,1,0:T(8,128)(2,1)S(1)} %all-to-all-done.whole, bf16[576,256]{1,0:T(8,128)(2,1)S(1)} %collective-permute-done.high.rim, f32[16,256]{1,0:T(8,128)S(1)} %get-tuple-element.35.stats, ...), custom_call_target="tpu_custom_call" | custom-call | flops 5000000000 | tf_op jit(solution)/shard_map/pallas_call | solution.py:505
  78.4 3.3 %collective-permute-start.2 = (bf16[288,512]{1,0:T(8,128)(2,1)S(1)}, bf16[288,512]{1,0:T(8,128)(2,1)S(1)}, u32[]{:S(2)}, u32[]{:S(2)}) collective-permute-start(bf16[288,512]{1,0:T(8,128)(2,1)S(1)} %get-tuple-element.42), channel_id=1, source_target_pairs={{0,8},{8,16},{16,24},{24,32},{32,40},{40,48},{48,56},{56,64},{64,7... | collective-permute-start | bytes 884744 | tf_op jit(solution)/shard_map/ppermute | solution.py:453
  81.7 0.6 all-to-all-done.3.near
  82.4 0.8 shard_map.85
  83.2 3.6 %all-to-all-start.4 = ((bf16[16,8,512]{2,1,0:T(8,128)(2,1)}), bf16[16,8,512]{2,1,0:T(8,128)(2,1)S(1)}, u32[]{:S(2)}, u32[]{:S(2)}) async-start(bf16[16,8,512]{2,1,0:T(8,128)(2,1)} %shard_map.85), calls=%async_computation.4 | async-start | bytes 262144 | tf_op jit(solution)/shard_map/all_to_all | solution.py:456
  86.8 0.9 collective-permute-done.2.from_prev.other
  87.7 1.1 %shard_map.86 = bf16[288,512]{1,0:T(8,128)(2,1)S(1)} custom-call(s32[2]{0:T(128)S(1)} %pad_add_fusion.spot, bf16[8,256,256]{2,1,0:T(8,128)(2,1)S(1)} %all-to-all-done.whole, bf16[576,256]{1,0:T(8,128)(2,1)S(1)} %collective-permute-done.1.low.rim, f32[16,256]{1,0:T(8,128)S(1)} %get-tuple-element.35.stats, bf16[32,512]{1,0:T(8,128)(2,1)S(1)} %get-tuple-element.36.level_zero, ...), custom_call_target="tpu_custom_call" | custom-call | tf_op jit(solution)/shard_map/pallas_call | solution.py:513
  88.7 4.7 %collective-permute-start.3 = (bf16[288,512]{1,0:T(8,128)(2,1)S(1)}, bf16[288,512]{1,0:T(8,128)(2,1)S(1)}, u32[]{:S(2)}, u32[]{:S(2)}) collective-permute-start(bf16[288,512]{1,0:T(8,128)(2,1)S(1)} %shard_map.86), channel_id=1, source_target_pairs={{0,504},{8,0},{16,8},{24,16},{32,24},{40,32},{48,40},{56,48},{64,5... | collective-permute-start | bytes 884744 | tf_op jit(solution)/shard_map/ppermute | solution.py:453
  93.5 3.1 %shard_map.83 = (bf16[512,256]{1,0:T(8,128)(2,1)}, bf16[512,512]{1,0:T(8,128)(2,1)S(1)}) custom-call(s32[2]{0:T(128)S(1)} %pad_add_fusion.spot, bf16[8,256,256]{2,1,0:T(8,128)(2,1)S(1)} %all-to-all-done.whole, bf16[576,256]{1,0:T(8,128)(2,1)S(1)} %collective-permute-done.1.low.rim, bf16[576,256]{1,0:T(8,128)(2,1)S(1)} %collective-permute-done.high.rim, ...), custom_call_target="tpu_custom_call" | custom-call | flops 5000000000 | tf_op jit(solution)/shard_map/pallas_call | solution.py:517
  96.6 1.1 %shard_map.84 = (f32[512,512]{1,0:T(8,128)S(1)}, bf16[512,32]{1,0:T(8,128)(2,1)S(1)}) custom-call(s32[2]{0:T(128)S(1)} %pad_add_fusion.spot, bf16[512,512]{1,0:T(8,128)(2,1)S(1)} %get-tuple-element.41.centre, bf16[288,512]{1,0:T(8,128)(2,1)S(1)} %collective-permute-done.2.from_prev.other, bf16[4,48,512]{2,1,0:T(8,128)(2,1)S(1)} %all-to-all-done.3.near), custom_call_target="tpu_custom_call" | custom-call | tf_op jit(solution)/shard_map/pallas_call | solution.py:524
  97.7 1.9 %collective-permute-done.3.from_next = bf16[288,512]{1,0:T(8,128)(2,1)S(1)} collective-permute-done((bf16[288,512]{1,0:T(8,128)(2,1)S(1)}, bf16[288,512]{1,0:T(8,128)(2,1)S(1)}, u32[]{:S(2)}, u32[]{:S(2)}) %collective-permute-start.3) | collective-permute-done | bytes 294944 | tf_op jit(solution)/shard_map/ppermute | solution.py:453
  99.5 3.9 %all-to-all-done.4.far = bf16[16,8,512]{2,1,0:T(8,128)(2,1)S(1)} async-done(((bf16[16,8,512]{2,1,0:T(8,128)(2,1)}), bf16[16,8,512]{2,1,0:T(8,128)(2,1)S(1)}, u32[]{:S(2)}, u32[]{:S(2)}) %all-to-all-start.4) | async-done | bytes 131104 | tf_op jit(solution)/shard_map/all_to_all | solution.py:456
  103.4 1.2 %shard_map.87 = (bf16[512,256]{1,0:T(8,128)(2,1)}, bf16[512,256]{1,0:T(8,128)(2,1)}) custom-call(f32[512,512]{1,0:T(8,128)S(1)} %get-tuple-element.44.total, bf16[512,128]{1,0:T(8,128)(2,1)S(1)} %get-tuple-element.45.weight, bf16[512,32]{1,0:T(8,128)(2,1)S(1)} %get-tuple-element.46.zero_weight, bf16[16,8,512]{2,1,0:T(8,128)(2,1)S(1)} %all-to-all-done.4.far, ...), custom_call_target="tpu_custom_call" | custom-call | tf_op jit(solution)/shard_map/pallas_call | solution.py:530
Async XLA Ops:
  2.7 20.4 %all-to-all-start = ((bf16[8,256,256]{2,1,0:T(8,128)(2,1)}), bf16[8,256,256]{2,1,0:T(8,128)(2,1)S(1)}, u32[]{:S(2)}, u32[]{:S(2)}) async-start(bf16[8,256,256]{2,1,0:T(8,128)(2,1)} %shard_map.75), calls=%async_computation | async-start | bytes 2097152 | tf_op jit(solution)/shard_map/all_to_all | solution.py:458
  24.0 35.4 %all-to-all-start.1 = ((bf16[16,8,512]{2,1,0:T(8,128)(2,1)}), bf16[16,8,512]{2,1,0:T(8,128)(2,1)S(1)}, u32[]{:S(2)}, u32[]{:S(2)}) async-start(bf16[16,8,512]{2,1,0:T(8,128)(2,1)} %get-tuple-element.34), calls=%async_computation.1 | async-start | bytes 262144 | tf_op jit(solution)/shard_map/all_to_all | solution.py:456
  41.0 22.7 %collective-permute-start = (bf16[576,256]{1,0:T(8,128)(2,1)S(1)}, bf16[576,256]{1,0:T(8,128)(2,1)S(1)}, u32[]{:S(2)}, u32[]{:S(2)}) collective-permute-start(bf16[576,256]{1,0:T(8,128)(2,1)S(1)} %get-tuple-element.30), channel_id=1, source_target_pairs={{0,504},{8,0},{16,8},{24,16},{32,24},{40,32},{48,40},{56,48},{64,5... | collective-permute-start | bytes 884744 | tf_op jit(solution)/shard_map/ppermute | solution.py:453
  43.9 19.8 %collective-permute-start.1 = (bf16[576,256]{1,0:T(8,128)(2,1)S(1)}, bf16[576,256]{1,0:T(8,128)(2,1)S(1)}, u32[]{:S(2)}, u32[]{:S(2)}) collective-permute-start(bf16[576,256]{1,0:T(8,128)(2,1)S(1)} %get-tuple-element.31), channel_id=1, source_target_pairs={{0,8},{8,16},{16,24},{24,32},{32,40},{40,48},{48,56},{56,64},{64,7... | collective-permute-start | bytes 884744 | tf_op jit(solution)/shard_map/ppermute | solution.py:453
  60.3 9.1 %all-to-all-start.2 = ((bf16[4,48,512]{2,1,0:T(8,128)(2,1)}), bf16[4,48,512]{2,1,0:T(8,128)(2,1)S(1)}, u32[]{:S(2)}, u32[]{:S(2)}) async-start(bf16[4,48,512]{2,1,0:T(8,128)(2,1)} %shard_map.79), calls=%async_computation.2 | async-start | bytes 393216 | tf_op jit(solution)/shard_map/all_to_all | solution.py:456
  72.4 10.0 %all-to-all-start.3 = ((bf16[4,48,512]{2,1,0:T(8,128)(2,1)}), bf16[4,48,512]{2,1,0:T(8,128)(2,1)S(1)}, u32[]{:S(2)}, u32[]{:S(2)}) async-start(bf16[4,48,512]{2,1,0:T(8,128)(2,1)} %get-tuple-element.43), calls=%async_computation.3 | async-start | bytes 393216 | tf_op jit(solution)/shard_map/all_to_all | solution.py:456
  78.4 9.3 %collective-permute-start.2 = (bf16[288,512]{1,0:T(8,128)(2,1)S(1)}, bf16[288,512]{1,0:T(8,128)(2,1)S(1)}, u32[]{:S(2)}, u32[]{:S(2)}) collective-permute-start(bf16[288,512]{1,0:T(8,128)(2,1)S(1)} %get-tuple-element.42), channel_id=1, source_target_pairs={{0,8},{8,16},{16,24},{24,32},{32,40},{40,48},{48,56},{56,64},{64,7... | collective-permute-start | bytes 884744 | tf_op jit(solution)/shard_map/ppermute | solution.py:453
  83.2 20.2 %all-to-all-start.4 = ((bf16[16,8,512]{2,1,0:T(8,128)(2,1)}), bf16[16,8,512]{2,1,0:T(8,128)(2,1)S(1)}, u32[]{:S(2)}, u32[]{:S(2)}) async-start(bf16[16,8,512]{2,1,0:T(8,128)(2,1)} %shard_map.85), calls=%async_computation.4 | async-start | bytes 262144 | tf_op jit(solution)/shard_map/all_to_all | solution.py:456
  88.7 10.8 %collective-permute-start.3 = (bf16[288,512]{1,0:T(8,128)(2,1)S(1)}, bf16[288,512]{1,0:T(8,128)(2,1)S(1)}, u32[]{:S(2)}, u32[]{:S(2)}) collective-permute-start(bf16[288,512]{1,0:T(8,128)(2,1)S(1)} %shard_map.86), channel_id=1, source_target_pairs={{0,504},{8,0},{16,8},{24,16},{32,24},{40,32},{48,40},{56,48},{64,5... | collective-permute-start | bytes 884744 | tf_op jit(solution)/shard_map/ppermute | solution.py:453

commit v7 on v6

--- a/solution.py
+++ b/solution.py
@@ -181,14 +181,14 @@
         pooled[:, columns] = result[FAR:]
 
 
-def rim_kernel(whole, pooled, spread, to_next, to_prev, own):
+def rim_kernel(spot, whole, pooled, spread, to_pair, to_other, own):
+    half = SHARES // 2
+    upper = (1 - (spot[0] & 1)) * half
+    to_pair[:TOKENS, :] = whole[pl.ds(upper, half), : 2 * SHARE, :].reshape(TOKENS, SPAN)
+    to_other[...] = whole[pl.ds(half - upper, half), : 2 * SHARE, :].reshape(TOKENS, SPAN)
     for part in range(2):
         place = slice(TOKENS + part * COUNT[0], TOKENS + (part + 1) * COUNT[0])
-        means = pooled[: COUNT[0], part * SPAN : (part + 1) * SPAN]
-        to_next[place, :] = means
-        to_prev[place, :] = means
-    to_prev[:TOKENS, :] = whole[: SHARES // 2, : 2 * SHARE, :].reshape(TOKENS, SPAN)
-    to_next[:TOKENS, :] = whole[SHARES // 2 :, : 2 * SHARE, :].reshape(TOKENS, SPAN)
+        to_pair[place, :] = pooled[: COUNT[0], part * SPAN : (part + 1) * SPAN]
     own[...] = dot(spread[...], pooled[...], NN).astype(BF16)
 
 
@@ -222,14 +222,22 @@
     return whole[block * half : (block + 1) * half, part_rows(part), columns].reshape(LEAF, HEAD_DIM)
 
 
-def ext(whole, low, high, part, columns, store):
+def rim_rows(rim, part, columns):
     half = SHARES // 2
-    for place, rim in ((0, low), (LEAF + TOKENS, high)):
-        store[place : place + LEAF, :] = (
-            rim[:TOKENS, columns]
-            .reshape(half, 2 * SHARE, HEAD_DIM)[:, part_rows(part)]
-            .reshape(LEAF, HEAD_DIM)
-        )
+    return (
+        rim[:TOKENS, columns]
+        .reshape(half, 2 * SHARE, HEAD_DIM)[:, part_rows(part)]
+        .reshape(LEAF, HEAD_DIM)
+    )
+
+
+def ext(spot, whole, pair, other, part, columns, store):
+    odd = spot[0] & 1
+    far_end = LEAF + TOKENS
+    place = pl.multiple_of((1 - odd) * far_end, LEAF)
+    store[pl.ds(place, LEAF), :] = rim_rows(pair, part, columns)
+    place = pl.multiple_of(odd * far_end, LEAF)
+    store[pl.ds(place, LEAF), :] = rim_rows(other, part, columns)
     store[LEAF : LEAF + TOKENS, :] = whole[:, part_rows(part), columns].reshape(TOKENS, HEAD_DIM)
 
 
@@ -243,9 +251,9 @@
     return jnp.concatenate([near[: 2 * LEAF], near[2 * LEAF :] + bias], axis=0)
 
 
-def near_forward_kernel(spot, whole, low, high, stats, keys):
+def near_forward_kernel(spot, whole, pair, other, stats, keys):
     for head, columns in enumerate(COLUMNS):
-        ext(whole, low, high, 0, columns, keys.at[head])
+        ext(spot, whole, pair, other, 0, columns, keys.at[head])
     scores = [
         near_scores(spot, keys.at[head], load(whole, 2, block, COLUMNS[head]), block)
         for head, block in UNITS
@@ -258,21 +266,15 @@
 
 
 def far_kernel(
-    spot, whole, low, high, near_rows, near_stats,
+    spot, whole, pair, other, near_rows, near_stats,
     mixed_low, far_query, stats, near_send, zero_back,
     coarse, keys, values,
 ):
     factor = HEAD_DIM ** (-0.5)
     binary = factor * math.log2(math.e)
-    even = (spot[0] & 1) == 0
-    for rim, flag in ((high, even), (low, jnp.logical_not(even))):
-
-        @pl.when(flag)
-        def _():
-            for part in range(2):
-                summary = slice(TOKENS + part * COUNT[0], TOKENS + (part + 1) * COUNT[0])
-                coarse[COARSE - COUNT[0] :, part * SPAN : (part + 1) * SPAN] = rim[summary, :]
-
+    for part in range(2):
+        summary = slice(TOKENS + part * COUNT[0], TOKENS + (part + 1) * COUNT[0])
+        coarse[COARSE - COUNT[0] :, part * SPAN : (part + 1) * SPAN] = pair[summary, :]
     near_at = spot[0] & (NEAR_PEERS - 1)
     for slot in range(NEAR_PEERS):
         coarse[slot * HELD : (slot + 1) * HELD, :] = near_rows[slot, :HELD, :]
@@ -281,8 +283,8 @@
         start = first + (offset - 2) * COUNT[1]
         coarse[start : start + COUNT[1], :] = near_rows[near_at ^ offset, HELD:, :]
     for head, columns in enumerate(COLUMNS):
-        ext(whole, low, high, 0, columns, keys.at[head])
-        ext(whole, low, high, 1, columns, values.at[head])
+        ext(spot, whole, pair, other, 0, columns, keys.at[head])
+        ext(spot, whole, pair, other, 1, columns, values.at[head])
     near_value_t = [jnp.transpose(values[head]) for head in range(2)]
     key = [coarse[:, part_columns(0, head)] for head in range(2)]
     value = [coarse[:, part_columns(1, head)] for head in range(2)]
@@ -341,50 +343,61 @@
                 near_send[near_at ^ offset, HELD:, place] = far_grad[start : start + COUNT[1]]
 
 
-def rim_grad_kernel(block, spot, whole, rim, stats, level_zero, other, target, attended=None):
+def rim_grads(spot, whole, rim, stats, block, bias):
     factor = HEAD_DIM ** (-0.5)
-    edge = 0 if block == 0 else spot[1] - 1
-    bias = jnp.where(spot[0] == edge, -1e30, 0.0).astype(F32)
     half = SHARES // 2
-    keys, values = [
+    rows = pl.ds(block * half, half)
+    query, grad = [
         [
-            rim[:TOKENS, COLUMNS[head]]
-            .reshape(half, 2 * SHARE, HEAD_DIM)[:, part_rows(part)]
-            .reshape(LEAF, HEAD_DIM)
+            whole[rows, part_rows(part), COLUMNS[head]].reshape(LEAF, HEAD_DIM)
             for head in range(2)
         ]
-        for part in range(2)
+        for part in (2, 3)
     ]
-    query = [load(whole, 2, block, COLUMNS[head]) for head in range(2)]
-    grad = [load(whole, 3, block, COLUMNS[head]) for head in range(2)]
-    near = [dot(keys[head], query[head], NT) for head in range(2)]
-    slope = [dot(values[head], grad[head], NT) for head in range(2)]
+    near = [dot(rim_rows(rim, 0, COLUMNS[head]), query[head], NT) for head in range(2)]
+    slope = [dot(rim_rows(rim, 1, COLUMNS[head]), grad[head], NT) for head in range(2)]
     lows, scores = [], []
     for head in range(2):
         unit = 2 * head + block
         probs = near[head] * (factor * math.log2(math.e)) + bias
-        probs = jnp.exp2(probs - stats[unit : unit + 1, :]) * stats[4 + unit : 5 + unit, :]
+        probs = jnp.exp2(probs - stats[pl.ds(unit, 1), :]) * stats[pl.ds(4 + unit, 1), :]
         lows.append(probs.astype(BF16))
-        scores.append((probs * (slope[head] - stats[8 + unit : 9 + unit, :])).astype(BF16))
-    for head in range(2):
-        target[:LEAF, part_columns(0, head)] = (dot(scores[head], query[head], NN) * factor).astype(BF16)
-        target[:LEAF, part_columns(1, head)] = dot(lows[head], grad[head], NN).astype(BF16)
-    target[LEAF:, :] = level_zero[...]
-    if attended is not None:
-        for unit, (head, block) in enumerate(UNITS):
-            rows = slice(block * LEAF, (block + 1) * LEAF)
-            attended[rows, COLUMNS[head]] = jnp.transpose(other[unit])
+        scores.append((probs * (slope[head] - stats[pl.ds(8 + unit, 1), :])).astype(BF16))
+    return [
+        (
+            part_columns(part, head),
+            ((dot(scores[head], query[head], NN) * factor) if part == 0 else dot(lows[head], grad[head], NN)).astype(BF16),
+        )
+        for head in range(2)
+        for part in range(2)
+    ]
+
+
+def pair_grad_kernel(spot, whole, pair, stats, level_zero, mixed_low, to_pair, attended):
+    for place, result in rim_grads(spot, whole, pair, stats, 1 - (spot[0] & 1), 0.0):
+        to_pair[:LEAF, place] = result
+    to_pair[LEAF:, :] = level_zero[...]
+    for unit, (head, block) in enumerate(UNITS):
+        rows = slice(block * LEAF, (block + 1) * LEAF)
+        attended[rows, COLUMNS[head]] = jnp.transpose(mixed_low[unit])
+
+
+def other_grad_kernel(spot, whole, other, stats, _after, to_other):
+    edge = (spot[0] == 0) | (spot[0] == spot[1] - 1)
+    bias = jnp.where(edge, -1e30, 0.0).astype(F32)
+    for place, result in rim_grads(spot, whole, other, stats, spot[0] & 1, bias):
+        to_other[:, place] = result
 
 
 def backward_kernel(
-    spot, whole, low, high, stats, far_query,
+    spot, whole, pair, other, stats, far_query,
     query_grad, centre,
     keys, values,
 ):
     factor = HEAD_DIM ** (-0.5)
     for head, columns in enumerate(COLUMNS):
-        ext(whole, low, high, 0, columns, keys.at[head])
-        ext(whole, low, high, 1, columns, values.at[head])
+        ext(spot, whole, pair, other, 0, columns, keys.at[head])
+        ext(spot, whole, pair, other, 1, columns, values.at[head])
     key_t = [jnp.transpose(keys[head]) for head in range(2)]
     query = [load(whole, 2, block, COLUMNS[head]) for head, block in UNITS]
     grad = [load(whole, 3, block, COLUMNS[head]) for head, block in UNITS]
@@ -411,32 +424,30 @@
             centre[:, place] = (early + late).astype(BF16)
 
 
-def gather_kernel(spot, centre, from_prev, near, total, zero_weight):
+def gather_kernel(spot, centre, from_pair, near, total):
     token, column = grid(TOKENS, COUNT[0])
-    odd = jnp.where((spot[0] & 1) == 1, 1.0 / RATIO, 0.0).astype(F32)
-    even = 1.0 / RATIO - odd
-    own = (token >> 4) == column
-    zero_weight[...] = jnp.where(own, even, 0.0).astype(BF16)
-    spread = dot(jnp.where(own, odd, 0.0).astype(BF16), from_prev[LEAF:, :], NN)
-    spread = spread + centre[...].astype(F32)
+    own = jnp.where((token >> 4) == column, 1.0 / RATIO, 0.0).astype(BF16)
+    spread = centre[...].astype(F32) + dot(own, from_pair[LEAF:, :], NN)
     token, column = grid(TOKENS, COUNT[1])
     own = jnp.where((token >> 5) == column, 1.0 / (2 * RATIO), 0.0).astype(BF16)
     near_at = spot[0] & (NEAR_PEERS - 1)
     for offset in (2, 3):
         spread = spread + dot(own, near[near_at ^ offset, HELD:, :], NN)
-    total[:LEAF, :] = spread[:LEAF] + from_prev[:LEAF, :].astype(F32)
-    total[LEAF:, :] = spread[LEAF:]
-
-
-def finish_kernel(total, weight, zero_weight, far, from_next, key_grad, value_grad):
+    total[...] = spread
+    rows = pl.ds(pl.multiple_of((1 - (spot[0] & 1)) * LEAF, LEAF), LEAF)
+    total[rows, :] += from_pair[:LEAF, :].astype(F32)
+
+
+def finish_kernel(spot, total, weight, far, from_other, key_grad, value_grad):
     rows = far[...].reshape(FAR, 2 * SPAN)
-    result = total[...] + dot(weight[...], rows, NN) + dot(zero_weight[...], from_next[LEAF:, :], NN)
-    low = result[:LEAF].astype(BF16)
-    high = (result[LEAF:] + from_next[:LEAF, :].astype(F32)).astype(BF16)
-    for block, part in ((0, low), (1, high)):
-        rows = slice(block * LEAF, (block + 1) * LEAF)
-        key_grad[rows, :] = part[:, :SPAN]
-        value_grad[rows, :] = part[:, SPAN:]
+    odd = spot[0] & 1
+    near = pl.ds(pl.multiple_of(odd * LEAF, LEAF), LEAF)
+    rest = pl.ds(pl.multiple_of((1 - odd) * LEAF, LEAF), LEAF)
+    first = total[near, :] + dot(weight[near, :], rows, NN) + from_other[...].astype(F32)
+    second = total[rest, :] + dot(weight[rest, :], rows, NN)
+    for place, result in ((near, first.astype(BF16)), (rest, second.astype(BF16))):
+        key_grad[place, :] = result[:, :SPAN]
+        value_grad[place, :] = result[:, SPAN:]
 
 
 FAR_GROUPS = [[far * NEAR_PEERS + near for far in range(FAR_PEERS)] for near in range(NEAR_PEERS)]
@@ -448,8 +459,11 @@
     position = lax.axis_index("context")
     spot = jnp.stack([position, jnp.int32(devices)])
 
-    def ring(block, step):
-        pairs = [(source, (source + step) % devices) for source in range(devices)]
+    def swap(block, odd_step):
+        pairs = [
+            (source, (source + (odd_step if source % 2 else -odd_step)) % devices)
+            for source in range(devices)
+        ]
         return lax.ppermute(block, "context", pairs)
 
     def exchange(block, groups):
@@ -472,11 +486,13 @@
         cost=None,
     )(spot)
     pooled, far_send = call(pool_kernel, (shape(OWN, 2 * SPAN), far_slots), count=2)(means, whole)
-    to_next, to_prev, own = call(rim_kernel, (rim, rim, shape(NEAR, 2 * SPAN)), count=3)(
-        whole, pooled, spread
-    )
-    low = ring(to_next, 1)
-    high = ring(to_prev, -1)
+    to_pair, to_other, own = call(
+        rim_kernel,
+        (rim, shape(TOKENS, SPAN), shape(NEAR, 2 * SPAN)),
+        specs=[SMEM] + [VMEM] * 3,
+    )(spot, whole, pooled, spread)
+    pair = swap(to_pair, -1)
+    other = swap(to_other, 1)
     far = exchange(far_send, FAR_GROUPS)
     near = exchange(call(near_kernel, near_slots, count=3)(own, gather, far), NEAR_GROUPS)
     span = 2 * LEAF + TOKENS
@@ -487,7 +503,7 @@
         sides[:1],
         [SMEM] + [VMEM] * 3,
         cost=pl.CostEstimate(flops=5000000000, bytes_accessed=0, transcendentals=0),
-    )(spot, whole, low, high)
+    )(spot, whole, pair, other)
     mixed_low, far_query, stats, near_send, zero_back = call(
         far_kernel,
         (
@@ -499,37 +515,34 @@
         ),
         [pltpu.VMEM((COARSE, 2 * SPAN), BF16)] + sides,
         [SMEM] + [VMEM] * 5,
-    )(spot, whole, low, high, near, near_stats)
+    )(spot, whole, pair, other, near, near_stats)
     near = exchange(near_send, NEAR_GROUPS)
     rim_grad = shape(LEAF + COUNT[0], 2 * SPAN)
-    to_next, attended = call(
-        functools.partial(rim_grad_kernel, 1),
+    to_pair, attended = call(
+        pair_grad_kernel,
         (rim_grad, shape(TOKENS, SPAN)),
         specs=[SMEM] + [VMEM] * 5,
         cost=pl.CostEstimate(flops=5000000000, bytes_accessed=0, transcendentals=0),
-    )(spot, whole, high, stats, zero_back, mixed_low)
-    from_prev = ring(to_next, 1)
+    )(spot, whole, pair, stats, zero_back, mixed_low)
+    from_pair = swap(to_pair, -1)
     far = exchange(call(far_send_kernel, far_slots, count=2)(scatter, near), FAR_GROUPS)
-    to_prev = call(
-        functools.partial(rim_grad_kernel, 0), rim_grad, specs=[SMEM] + [VMEM] * 5, cost=None
-    )(spot, whole, low, stats, zero_back, from_prev)
-    from_next = ring(to_prev, -1)
+    to_other = call(
+        other_grad_kernel, shape(LEAF, 2 * SPAN), specs=[SMEM] + [VMEM] * 4, cost=None
+    )(spot, whole, other, stats, from_pair)
+    from_other = swap(to_other, 1)
     query_grad, centre = call(
         backward_kernel,
         (shape(TOKENS, SPAN), shape(TOKENS, 2 * SPAN)),
         sides,
         [SMEM] + [VMEM] * 5,
         cost=pl.CostEstimate(flops=5000000000, bytes_accessed=0, transcendentals=0),
-    )(spot, whole, low, high, stats, far_query)
-    total, zero_weight = call(
-        gather_kernel,
-        (shape(TOKENS, 2 * SPAN, kind=F32), shape(TOKENS, COUNT[0])),
-        specs=[SMEM] + [VMEM] * 3,
-        cost=None,
-    )(spot, centre, from_prev, near)
+    )(spot, whole, pair, other, stats, far_query)
+    total = call(
+        gather_kernel, shape(TOKENS, 2 * SPAN, kind=F32), specs=[SMEM] + [VMEM] * 3, cost=None
+    )(spot, centre, from_pair, near)
     key_grad, value_grad = call(
-        finish_kernel, (shape(TOKENS, SPAN), shape(TOKENS, SPAN)), count=5
-    )(total, weight, zero_weight, far, from_next)
+        finish_kernel, (shape(TOKENS, SPAN), shape(TOKENS, SPAN)), specs=[SMEM] + [VMEM] * 4
+    )(spot, total, weight, far, from_other)
     return attended, query_grad, key_grad, value_grad
 
 

time: 105 us -> 108 us (1.029)
  the two profiles are of different devices: /device:TPU:32 before, /device:TPU:1 now
where the time goes in v7:
time: 108 us; the launch traced here: 107 us
  starting transfers between devices  59 us (55%)
  waiting for transfers between devices  27.6 us (26%)
  Pallas kernels  19.7 us (18%)
    all_to_all x4, starting transfers between devices, exchange(): return lax.all_to_all(block, 'context', 0, 0, axis_index_groups=groups)  25.8 us
    ppermute x4, starting transfers between devices, swap(): return lax.ppermute(block, 'context', pairs)  22.8 us
    all_to_all x1, waiting for transfers between devices, body(): whole = lax.all_to_all(pack(key, value, query, cotangent), 'head', 0, 0)  14 us
    all_to_all x1, starting transfers between devices, body(): whole = lax.all_to_all(pack(key, value, query, cotangent), 'head', 0, 0)  10.3 us
    all_to_all x4, waiting for transfers between devices, exchange(): return lax.all_to_all(block, 'context', 0, 0, axis_index_groups=groups)  8.07 us
    ppermute x4, waiting for transfers between devices, swap(): return lax.ppermute(block, 'context', pairs)  5.57 us
    pallas_call x1, Pallas kernels, body(): call(far_kernel, (shape(4, HEAD_DIM, LEAF), shape(4, HEAD_DIM, LEAF, kind...  3.11 us
    pallas_call x1, Pallas kernels, body(): call(backward_kernel, (shape(TOKENS, SPAN), shape(TOKENS, 2 * SPAN)), sid...  3.06 us
  transfers between devices with their start and end apart: 9, of which 6 were waited for; matrix products, arithmetic and copies ran while one was open for 0% of the time, Pallas kernels for 11%

profile of v7, /device:TPU:1, one launch (start us, length us, event | category | flops | bytes accessed | tf_op | source)
XLA Modules:
  0.0 107.1 jit_solution(8616857864223286640)
XLA Ops:
  0.6 2.0 %shard_map.75 = bf16[8,256,256]{2,1,0:T(8,128)(2,1)} custom-call(bf16[64,2048]{1,0:T(8,128)(2,1)} %key.1, bf16[64,2048]{1,0:T(8,128)(2,1)} %value.1, bf16[64,2048]{1,0:T(8,128)(2,1)} %query.1, bf16[64,2048]{1,0:T(8,128)(2,1)} %cotangent.1), custom_call_target="tpu_custom_call" | custom-call | tf_op jit(solution)/shard_map/pallas_call | solution.py:121
  2.7 10.3 %all-to-all-start = ((bf16[8,256,256]{2,1,0:T(8,128)(2,1)}), bf16[8,256,256]{2,1,0:T(8,128)(2,1)S(1)}, u32[]{:S(2)}, u32[]{:S(2)}) async-start(bf16[8,256,256]{2,1,0:T(8,128)(2,1)} %shard_map.75), calls=%async_computation | async-start | bytes 2097152 | tf_op jit(solution)/shard_map/all_to_all | solution.py:472
  13.0 0.1 pad_add_fusion.spot
  13.1 1.0 shard_map.76
  14.1 14.0 %all-to-all-done.whole = bf16[8,256,256]{2,1,0:T(8,128)(2,1)S(1)} async-done(((bf16[8,256,256]{2,1,0:T(8,128)(2,1)}), bf16[8,256,256]{2,1,0:T(8,128)(2,1)S(1)}, u32[]{:S(2)}, u32[]{:S(2)}) %all-to-all-start) | async-done | bytes 1048608 | tf_op jit(solution)/shard_map/all_to_all | solution.py:472
  28.1 0.9 shard_map.77
  29.0 13.0 %all-to-all-start.1 = ((bf16[16,8,512]{2,1,0:T(8,128)(2,1)}), bf16[16,8,512]{2,1,0:T(8,128)(2,1)S(1)}, u32[]{:S(2)}, u32[]{:S(2)}) async-start(bf16[16,8,512]{2,1,0:T(8,128)(2,1)} %get-tuple-element.32), calls=%async_computation.1 | async-start | bytes 262144 | tf_op jit(solution)/shard_map/all_to_all | solution.py:470
  42.0 0.8 shard_map.78
  42.8 2.6 %collective-permute-start = (bf16[576,256]{1,0:T(8,128)(2,1)S(1)}, bf16[576,256]{1,0:T(8,128)(2,1)S(1)}, u32[]{:S(2)}, u32[]{:S(2)}) collective-permute-start(bf16[576,256]{1,0:T(8,128)(2,1)S(1)} %get-tuple-element.28), channel_id=1, source_target_pairs={{0,8},{8,0},{16,24},{24,16},{32,40},{40,32},{48,56},{56,48},{64,72... | collective-permute-start | bytes 884744 | tf_op jit(solution)/shard_map/ppermute | solution.py:467
  45.5 8.0 %collective-permute-start.1 = (bf16[512,256]{1,0:T(8,128)(2,1)S(1)}, bf16[512,256]{1,0:T(8,128)(2,1)S(1)}, u32[]{:S(2)}, u32[]{:S(2)}) collective-permute-start(bf16[512,256]{1,0:T(8,128)(2,1)S(1)} %get-tuple-element.29), channel_id=1, source_target_pairs={{0,504},{8,16},{16,8},{24,32},{32,24},{40,48},{48,40},{56,64},{64,... | collective-permute-start | bytes 786440 | tf_op jit(solution)/shard_map/ppermute | solution.py:467
  53.4 4.5 %all-to-all-done.1.far = bf16[16,8,512]{2,1,0:T(8,128)(2,1)S(1)} async-done(((bf16[16,8,512]{2,1,0:T(8,128)(2,1)}), bf16[16,8,512]{2,1,0:T(8,128)(2,1)S(1)}, u32[]{:S(2)}, u32[]{:S(2)}) %all-to-all-start.1) | async-done | bytes 131104 | tf_op jit(solution)/shard_map/all_to_all | solution.py:470
  57.9 0.9 shard_map.79
  58.8 4.2 %all-to-all-start.2 = ((bf16[4,48,512]{2,1,0:T(8,128)(2,1)}), bf16[4,48,512]{2,1,0:T(8,128)(2,1)S(1)}, u32[]{:S(2)}, u32[]{:S(2)}) async-start(bf16[4,48,512]{2,1,0:T(8,128)(2,1)} %shard_map.79), calls=%async_computation.2 | async-start | bytes 393216 | tf_op jit(solution)/shard_map/all_to_all | solution.py:470
  63.0 0.0 collective-permute-done.1.other
  63.0 0.0 collective-permute-done.pair
  63.0 1.6 %shard_map.80.near_stats = f32[8,256]{1,0:T(8,128)S(1)} custom-call(s32[2]{0:T(128)S(1)} %pad_add_fusion.spot, bf16[8,256,256]{2,1,0:T(8,128)(2,1)S(1)} %all-to-all-done.whole, bf16[576,256]{1,0:T(8,128)(2,1)S(1)} %collective-permute-done.pair, bf16[512,256]{1,0:T(8,128)(2,1)S(1)} %collective-permute-done.1.other), custom_call_target="tpu_custom_call" | custom-call | flops 5000000000 | tf_op jit(solution)/shard_map/pallas_call | solution.py:500
  64.6 3.5 %all-to-all-done.2.near_rows = bf16[4,48,512]{2,1,0:T(8,128)(2,1)S(1)} async-done(((bf16[4,48,512]{2,1,0:T(8,128)(2,1)}), bf16[4,48,512]{2,1,0:T(8,128)(2,1)S(1)}, u32[]{:S(2)}, u32[]{:S(2)}) %all-to-all-start.2) | async-done | bytes 196640 | tf_op jit(solution)/shard_map/all_to_all | solution.py:470
  68.1 3.1 %shard_map.81 = (bf16[4,128,256]{2,1,0:T(8,128)(2,1)S(1)}, f32[4,128,256]{2,1,0:T(8,128)S(1)}, f32[16,256]{1,0:T(8,128)S(1)}, bf16[4,48,512]{2,1,0:T(8,128)(2,1)}, bf16[32,512]{1,0:T(8,128)(2,1)S(1)}) custom-call(s32[2]{0:T(128)S(1)} %pad_add_fusion.spot, bf16[8,256,256]{2,1,0:T(8,128)(2,1)S(1)} %all-to-all-done.whole, ...), custom_call_target="tpu_custom_call" | custom-call | tf_op jit(solution)/shard_map/pallas_call | solution.py:507
  71.2 3.4 %all-to-all-start.3 = ((bf16[4,48,512]{2,1,0:T(8,128)(2,1)}), bf16[4,48,512]{2,1,0:T(8,128)(2,1)S(1)}, u32[]{:S(2)}, u32[]{:S(2)}) async-start(bf16[4,48,512]{2,1,0:T(8,128)(2,1)} %get-tuple-element.41), calls=%async_computation.3 | async-start | bytes 393216 | tf_op jit(solution)/shard_map/all_to_all | solution.py:470
  74.6 1.7 %shard_map.82 = (bf16[288,512]{1,0:T(8,128)(2,1)S(1)}, bf16[512,256]{1,0:T(8,128)(2,1)}) custom-call(s32[2]{0:T(128)S(1)} %pad_add_fusion.spot, bf16[8,256,256]{2,1,0:T(8,128)(2,1)S(1)} %all-to-all-done.whole, bf16[576,256]{1,0:T(8,128)(2,1)S(1)} %collective-permute-done.pair, f32[16,256]{1,0:T(8,128)S(1)} %get-tuple-element.33.stats, ...), custom_call_target="tpu_custom_call" | custom-call | flops 5000000000 | tf_op jit(solution)/shard_map/pallas_call | solution.py:521
  76.3 3.3 %collective-permute-start.2 = (bf16[288,512]{1,0:T(8,128)(2,1)S(1)}, bf16[288,512]{1,0:T(8,128)(2,1)S(1)}, u32[]{:S(2)}, u32[]{:S(2)}) collective-permute-start(bf16[288,512]{1,0:T(8,128)(2,1)S(1)} %get-tuple-element.40), channel_id=1, source_target_pairs={{0,8},{8,0},{16,24},{24,16},{32,40},{40,32},{48,56},{56,48},{64,72... | collective-permute-start | bytes 884744 | tf_op jit(solution)/shard_map/ppermute | solution.py:467
  79.6 0.1 all-to-all-done.3.near
  79.7 0.8 shard_map.85
  80.5 5.2 %all-to-all-start.4 = ((bf16[16,8,512]{2,1,0:T(8,128)(2,1)}), bf16[16,8,512]{2,1,0:T(8,128)(2,1)S(1)}, u32[]{:S(2)}, u32[]{:S(2)}) async-start(bf16[16,8,512]{2,1,0:T(8,128)(2,1)} %shard_map.85), calls=%async_computation.4 | async-start | bytes 262144 | tf_op jit(solution)/shard_map/all_to_all | solution.py:470
  85.8 0.5 collective-permute-done.2.from_pair._after
  86.3 1.1 shard_map.86
  87.3 8.9 %collective-permute-start.3 = (bf16[256,512]{1,0:T(8,128)(2,1)S(1)}, bf16[256,512]{1,0:T(8,128)(2,1)S(1)}, u32[]{:S(2)}, u32[]{:S(2)}) collective-permute-start(bf16[256,512]{1,0:T(8,128)(2,1)S(1)} %shard_map.86), channel_id=1, source_target_pairs={{0,504},{8,16},{16,8},{24,32},{32,24},{40,48},{48,40},{56,64},{64,... | collective-permute-start | bytes 786440 | tf_op jit(solution)/shard_map/ppermute | solution.py:467
  96.2 3.1 %shard_map.83 = (bf16[512,256]{1,0:T(8,128)(2,1)}, bf16[512,512]{1,0:T(8,128)(2,1)S(1)}) custom-call(s32[2]{0:T(128)S(1)} %pad_add_fusion.spot, bf16[8,256,256]{2,1,0:T(8,128)(2,1)S(1)} %all-to-all-done.whole, bf16[576,256]{1,0:T(8,128)(2,1)S(1)} %collective-permute-done.pair, bf16[512,256]{1,0:T(8,128)(2,1)S(1)} %collective-permute-done.1.other, ...), custom_call_target="tpu_custom_call" | custom-call | flops 5000000000 | tf_op jit(solution)/shard_map/pallas_call | solution.py:533
  99.3 1.2 %shard_map.84.total = f32[512,512]{1,0:T(8,128)S(1)} custom-call(s32[2]{0:T(128)S(1)} %pad_add_fusion.spot, bf16[512,512]{1,0:T(8,128)(2,1)S(1)} %get-tuple-element.39.centre, bf16[288,512]{1,0:T(8,128)(2,1)S(1)} %collective-permute-done.2.from_pair._after, bf16[4,48,512]{2,1,0:T(8,128)(2,1)S(1)} %all-to-all-done.3.near), custom_call_target="tpu_custom_call" | custom-call | tf_op jit(solution)/shard_map/pallas_call | solution.py:540
  100.5 5.0 %collective-permute-done.3.from_other = bf16[256,512]{1,0:T(8,128)(2,1)S(1)} collective-permute-done((bf16[256,512]{1,0:T(8,128)(2,1)S(1)}, bf16[256,512]{1,0:T(8,128)(2,1)S(1)}, u32[]{:S(2)}, u32[]{:S(2)}) %collective-permute-start.3) | collective-permute-done | bytes 262176 | tf_op jit(solution)/shard_map/ppermute | solution.py:467
  105.5 0.0 all-to-all-done.4.far
  105.5 1.6 %shard_map.87 = (bf16[512,256]{1,0:T(8,128)(2,1)}, bf16[512,256]{1,0:T(8,128)(2,1)}) custom-call(s32[2]{0:T(128)S(1)} %pad_add_fusion.spot, f32[512,512]{1,0:T(8,128)S(1)} %shard_map.84.total, bf16[512,128]{1,0:T(8,128)(2,1)S(1)} %get-tuple-element.42.weight, bf16[16,8,512]{2,1,0:T(8,128)(2,1)S(1)} %all-to-all-done.4.far, ...), custom_call_target="tpu_custom_call" | custom-call | tf_op jit(solution)/shard_map/pallas_call | solution.py:543
Async XLA Ops:
  2.7 25.5 %all-to-all-start = ((bf16[8,256,256]{2,1,0:T(8,128)(2,1)}), bf16[8,256,256]{2,1,0:T(8,128)(2,1)S(1)}, u32[]{:S(2)}, u32[]{:S(2)}) async-start(bf16[8,256,256]{2,1,0:T(8,128)(2,1)} %shard_map.75), calls=%async_computation | async-start | bytes 2097152 | tf_op jit(solution)/shard_map/all_to_all | solution.py:472
  29.0 28.9 %all-to-all-start.1 = ((bf16[16,8,512]{2,1,0:T(8,128)(2,1)}), bf16[16,8,512]{2,1,0:T(8,128)(2,1)S(1)}, u32[]{:S(2)}, u32[]{:S(2)}) async-start(bf16[16,8,512]{2,1,0:T(8,128)(2,1)} %get-tuple-element.32), calls=%async_computation.1 | async-start | bytes 262144 | tf_op jit(solution)/shard_map/all_to_all | solution.py:470
  42.8 20.2 %collective-permute-start = (bf16[576,256]{1,0:T(8,128)(2,1)S(1)}, bf16[576,256]{1,0:T(8,128)(2,1)S(1)}, u32[]{:S(2)}, u32[]{:S(2)}) collective-permute-start(bf16[576,256]{1,0:T(8,128)(2,1)S(1)} %get-tuple-element.28), channel_id=1, source_target_pairs={{0,8},{8,0},{16,24},{24,16},{32,40},{40,32},{48,56},{56,48},{64,72... | collective-permute-start | bytes 884744 | tf_op jit(solution)/shard_map/ppermute | solution.py:467
  45.5 17.6 %collective-permute-start.1 = (bf16[512,256]{1,0:T(8,128)(2,1)S(1)}, bf16[512,256]{1,0:T(8,128)(2,1)S(1)}, u32[]{:S(2)}, u32[]{:S(2)}) collective-permute-start(bf16[512,256]{1,0:T(8,128)(2,1)S(1)} %get-tuple-element.29), channel_id=1, source_target_pairs={{0,504},{8,16},{16,8},{24,32},{32,24},{40,48},{48,40},{56,64},{64,... | collective-permute-start | bytes 786440 | tf_op jit(solution)/shard_map/ppermute | solution.py:467
  58.8 9.3 %all-to-all-start.2 = ((bf16[4,48,512]{2,1,0:T(8,128)(2,1)}), bf16[4,48,512]{2,1,0:T(8,128)(2,1)S(1)}, u32[]{:S(2)}, u32[]{:S(2)}) async-start(bf16[4,48,512]{2,1,0:T(8,128)(2,1)} %shard_map.79), calls=%async_computation.2 | async-start | bytes 393216 | tf_op jit(solution)/shard_map/all_to_all | solution.py:470
  71.2 8.4 %all-to-all-start.3 = ((bf16[4,48,512]{2,1,0:T(8,128)(2,1)}), bf16[4,48,512]{2,1,0:T(8,128)(2,1)S(1)}, u32[]{:S(2)}, u32[]{:S(2)}) async-start(bf16[4,48,512]{2,1,0:T(8,128)(2,1)} %get-tuple-element.41), calls=%async_computation.3 | async-start | bytes 393216 | tf_op jit(solution)/shard_map/all_to_all | solution.py:470
  76.3 10.0 %collective-permute-start.2 = (bf16[288,512]{1,0:T(8,128)(2,1)S(1)}, bf16[288,512]{1,0:T(8,128)(2,1)S(1)}, u32[]{:S(2)}, u32[]{:S(2)}) collective-permute-start(bf16[288,512]{1,0:T(8,128)(2,1)S(1)} %get-tuple-element.40), channel_id=1, source_target_pairs={{0,8},{8,0},{16,24},{24,16},{32,40},{40,32},{48,56},{56,48},{64,72... | collective-permute-start | bytes 884744 | tf_op jit(solution)/shard_map/ppermute | solution.py:467
  80.5 25.0 %all-to-all-start.4 = ((bf16[16,8,512]{2,1,0:T(8,128)(2,1)}), bf16[16,8,512]{2,1,0:T(8,128)(2,1)S(1)}, u32[]{:S(2)}, u32[]{:S(2)}) async-start(bf16[16,8,512]{2,1,0:T(8,128)(2,1)} %shard_map.85), calls=%async_computation.4 | async-start | bytes 262144 | tf_op jit(solution)/shard_map/all_to_all | solution.py:470
  87.3 18.2 %collective-permute-start.3 = (bf16[256,512]{1,0:T(8,128)(2,1)S(1)}, bf16[256,512]{1,0:T(8,128)(2,1)S(1)}, u32[]{:S(2)}, u32[]{:S(2)}) collective-permute-start(bf16[256,512]{1,0:T(8,128)(2,1)S(1)} %shard_map.86), channel_id=1, source_target_pairs={{0,504},{8,16},{16,8},{24,32},{32,24},{40,48},{48,40},{56,64},{64,... | collective-permute-start | bytes 786440 | tf_op jit(solution)/shard_map/ppermute | solution.py:467

commit v8 on v6

--- a/solution.py
+++ b/solution.py
@@ -411,28 +411,28 @@
             centre[:, place] = (early + late).astype(BF16)
 
 
-def gather_kernel(spot, centre, from_prev, near, total, zero_weight):
+def gather_kernel(spot, centre, from_next, near, total, zero_weight):
     token, column = grid(TOKENS, COUNT[0])
     odd = jnp.where((spot[0] & 1) == 1, 1.0 / RATIO, 0.0).astype(F32)
     even = 1.0 / RATIO - odd
     own = (token >> 4) == column
-    zero_weight[...] = jnp.where(own, even, 0.0).astype(BF16)
-    spread = dot(jnp.where(own, odd, 0.0).astype(BF16), from_prev[LEAF:, :], NN)
+    zero_weight[...] = jnp.where(own, odd, 0.0).astype(BF16)
+    spread = dot(jnp.where(own, even, 0.0).astype(BF16), from_next[LEAF:, :], NN)
     spread = spread + centre[...].astype(F32)
     token, column = grid(TOKENS, COUNT[1])
     own = jnp.where((token >> 5) == column, 1.0 / (2 * RATIO), 0.0).astype(BF16)
     near_at = spot[0] & (NEAR_PEERS - 1)
     for offset in (2, 3):
         spread = spread + dot(own, near[near_at ^ offset, HELD:, :], NN)
-    total[:LEAF, :] = spread[:LEAF] + from_prev[:LEAF, :].astype(F32)
-    total[LEAF:, :] = spread[LEAF:]
-
-
-def finish_kernel(total, weight, zero_weight, far, from_next, key_grad, value_grad):
+    total[:LEAF, :] = spread[:LEAF]
+    total[LEAF:, :] = spread[LEAF:] + from_next[:LEAF, :].astype(F32)
+
+
+def finish_kernel(total, weight, zero_weight, far, from_prev, key_grad, value_grad):
     rows = far[...].reshape(FAR, 2 * SPAN)
-    result = total[...] + dot(weight[...], rows, NN) + dot(zero_weight[...], from_next[LEAF:, :], NN)
-    low = result[:LEAF].astype(BF16)
-    high = (result[LEAF:] + from_next[:LEAF, :].astype(F32)).astype(BF16)
+    result = total[...] + dot(weight[...], rows, NN) + dot(zero_weight[...], from_prev[LEAF:, :], NN)
+    low = (result[:LEAF] + from_prev[:LEAF, :].astype(F32)).astype(BF16)
+    high = result[LEAF:].astype(BF16)
     for block, part in ((0, low), (1, high)):
         rows = slice(block * LEAF, (block + 1) * LEAF)
         key_grad[rows, :] = part[:, :SPAN]
@@ -502,18 +502,18 @@
     )(spot, whole, low, high, near, near_stats)
     near = exchange(near_send, NEAR_GROUPS)
     rim_grad = shape(LEAF + COUNT[0], 2 * SPAN)
-    to_next, attended = call(
-        functools.partial(rim_grad_kernel, 1),
+    to_prev, attended = call(
+        functools.partial(rim_grad_kernel, 0),
         (rim_grad, shape(TOKENS, SPAN)),
         specs=[SMEM] + [VMEM] * 5,
         cost=pl.CostEstimate(flops=5000000000, bytes_accessed=0, transcendentals=0),
-    )(spot, whole, high, stats, zero_back, mixed_low)
+    )(spot, whole, low, stats, zero_back, mixed_low)
+    from_next = ring(to_prev, -1)
+    far = exchange(call(far_send_kernel, far_slots, count=2)(scatter, near), FAR_GROUPS)
+    to_next = call(
+        functools.partial(rim_grad_kernel, 1), rim_grad, specs=[SMEM] + [VMEM] * 5, cost=None
+    )(spot, whole, high, stats, zero_back, from_next)
     from_prev = ring(to_next, 1)
-    far = exchange(call(far_send_kernel, far_slots, count=2)(scatter, near), FAR_GROUPS)
-    to_prev = call(
-        functools.partial(rim_grad_kernel, 0), rim_grad, specs=[SMEM] + [VMEM] * 5, cost=None
-    )(spot, whole, low, stats, zero_back, from_prev)
-    from_next = ring(to_prev, -1)
     query_grad, centre = call(
         backward_kernel,
         (shape(TOKENS, SPAN), shape(TOKENS, 2 * SPAN)),
@@ -526,10 +526,10 @@
         (shape(TOKENS, 2 * SPAN, kind=F32), shape(TOKENS, COUNT[0])),
         specs=[SMEM] + [VMEM] * 3,
         cost=None,
-    )(spot, centre, from_prev, near)
+    )(spot, centre, from_next, near)
     key_grad, value_grad = call(
         finish_kernel, (shape(TOKENS, SPAN), shape(TOKENS, SPAN)), count=5
-    )(total, weight, zero_weight, far, from_next)
+    )(total, weight, zero_weight, far, from_prev)
     return attended, query_grad, key_grad, value_grad
 
 

time: 105 us -> 107 us (1.019)
  the two profiles are of different devices: /device:TPU:32 before, /device:TPU:1 now
where the time goes in v8:
time: 107 us
  starting transfers between devices  53.8 us (50%)
  waiting for transfers between devices  33.4 us (31%)
  Pallas kernels  18.7 us (17%)
    all_to_all x4, starting transfers between devices, exchange(): return lax.all_to_all(block, 'context', 0, 0, axis_index_groups=groups)  27.7 us
    ppermute x4, starting transfers between devices, ring(): return lax.ppermute(block, 'context', pairs)  15.7 us
    all_to_all x1, waiting for transfers between devices, body(): whole = lax.all_to_all(pack(key, value, query, cotangent), 'head', 0, 0)  14 us
    all_to_all x1, starting transfers between devices, body(): whole = lax.all_to_all(pack(key, value, query, cotangent), 'head', 0, 0)  10.3 us
    ppermute x4, waiting for transfers between devices, ring(): return lax.ppermute(block, 'context', pairs)  10 us
    all_to_all x4, waiting for transfers between devices, exchange(): return lax.all_to_all(block, 'context', 0, 0, axis_index_groups=groups)  9.39 us
    pallas_call x1, Pallas kernels, body(): call(far_kernel, (shape(4, HEAD_DIM, LEAF), shape(4, HEAD_DIM, LEAF, kind...  3.07 us
    pallas_call x1, Pallas kernels, body(): call(backward_kernel, (shape(TOKENS, SPAN), shape(TOKENS, 2 * SPAN)), sid...  3.06 us
  transfers between devices with their start and end apart: 9, of which 5 were waited for; matrix products, arithmetic and copies ran while one was open for 0% of the time, Pallas kernels for 11%

profile of v8, /device:TPU:1, one launch (start us, length us, event | category | flops | bytes accessed | tf_op | source)
XLA Modules:
  0.0 106.7 jit_solution(1085026996019681001)
XLA Ops:
  0.6 2.0 %shard_map.75 = bf16[8,256,256]{2,1,0:T(8,128)(2,1)} custom-call(bf16[64,2048]{1,0:T(8,128)(2,1)} %key.1, bf16[64,2048]{1,0:T(8,128)(2,1)} %value.1, bf16[64,2048]{1,0:T(8,128)(2,1)} %query.1, bf16[64,2048]{1,0:T(8,128)(2,1)} %cotangent.1), custom_call_target="tpu_custom_call" | custom-call | tf_op jit(solution)/shard_map/pallas_call | solution.py:121
  2.7 10.3 %all-to-all-start = ((bf16[8,256,256]{2,1,0:T(8,128)(2,1)}), bf16[8,256,256]{2,1,0:T(8,128)(2,1)S(1)}, u32[]{:S(2)}, u32[]{:S(2)}) async-start(bf16[8,256,256]{2,1,0:T(8,128)(2,1)} %shard_map.75), calls=%async_computation | async-start | bytes 2097152 | tf_op jit(solution)/shard_map/all_to_all | solution.py:458
  13.0 0.1 pad_add_fusion.spot
  13.1 1.0 shard_map.76
  14.1 14.0 %all-to-all-done.whole = bf16[8,256,256]{2,1,0:T(8,128)(2,1)S(1)} async-done(((bf16[8,256,256]{2,1,0:T(8,128)(2,1)}), bf16[8,256,256]{2,1,0:T(8,128)(2,1)S(1)}, u32[]{:S(2)}, u32[]{:S(2)}) %all-to-all-start) | async-done | bytes 1048608 | tf_op jit(solution)/shard_map/all_to_all | solution.py:458
  28.1 0.9 shard_map.77
  29.0 13.0 %all-to-all-start.1 = ((bf16[16,8,512]{2,1,0:T(8,128)(2,1)}), bf16[16,8,512]{2,1,0:T(8,128)(2,1)S(1)}, u32[]{:S(2)}, u32[]{:S(2)}) async-start(bf16[16,8,512]{2,1,0:T(8,128)(2,1)} %get-tuple-element.34), calls=%async_computation.1 | async-start | bytes 262144 | tf_op jit(solution)/shard_map/all_to_all | solution.py:456
  42.0 0.2 shard_map.78
  42.3 2.6 %collective-permute-start = (bf16[576,256]{1,0:T(8,128)(2,1)S(1)}, bf16[576,256]{1,0:T(8,128)(2,1)S(1)}, u32[]{:S(2)}, u32[]{:S(2)}) collective-permute-start(bf16[576,256]{1,0:T(8,128)(2,1)S(1)} %get-tuple-element.30), channel_id=1, source_target_pairs={{0,8},{8,16},{16,24},{24,32},{32,40},{40,48},{48,56},{56,64},{64,7... | collective-permute-start | bytes 884744 | tf_op jit(solution)/shard_map/ppermute | solution.py:453
  44.9 7.2 %collective-permute-start.1 = (bf16[576,256]{1,0:T(8,128)(2,1)S(1)}, bf16[576,256]{1,0:T(8,128)(2,1)S(1)}, u32[]{:S(2)}, u32[]{:S(2)}) collective-permute-start(bf16[576,256]{1,0:T(8,128)(2,1)S(1)} %get-tuple-element.31), channel_id=1, source_target_pairs={{0,504},{8,0},{16,8},{24,16},{32,24},{40,32},{48,40},{56,48},{64,5... | collective-permute-start | bytes 884744 | tf_op jit(solution)/shard_map/ppermute | solution.py:453
  52.2 5.8 %all-to-all-done.1.far = bf16[16,8,512]{2,1,0:T(8,128)(2,1)S(1)} async-done(((bf16[16,8,512]{2,1,0:T(8,128)(2,1)}), bf16[16,8,512]{2,1,0:T(8,128)(2,1)S(1)}, u32[]{:S(2)}, u32[]{:S(2)}) %all-to-all-start.1) | async-done | bytes 131104 | tf_op jit(solution)/shard_map/all_to_all | solution.py:456
  57.9 0.9 shard_map.79
  58.8 4.1 %all-to-all-start.2 = ((bf16[4,48,512]{2,1,0:T(8,128)(2,1)}), bf16[4,48,512]{2,1,0:T(8,128)(2,1)S(1)}, u32[]{:S(2)}, u32[]{:S(2)}) async-start(bf16[4,48,512]{2,1,0:T(8,128)(2,1)} %shard_map.79), calls=%async_computation.2 | async-start | bytes 393216 | tf_op jit(solution)/shard_map/all_to_all | solution.py:456
  62.9 0.0 collective-permute-done.low.rim
  62.9 0.0 collective-permute-done.1.high.rim
  62.9 1.6 %shard_map.80.near_stats = f32[8,256]{1,0:T(8,128)S(1)} custom-call(s32[2]{0:T(128)S(1)} %pad_add_fusion.spot, bf16[8,256,256]{2,1,0:T(8,128)(2,1)S(1)} %all-to-all-done.whole, bf16[576,256]{1,0:T(8,128)(2,1)S(1)} %collective-permute-done.low.rim, bf16[576,256]{1,0:T(8,128)(2,1)S(1)} %collective-permute-done.1.high.rim), custom_call_target="tpu_custom_call" | custom-call | flops 5000000000 | tf_op jit(solution)/shard_map/pallas_call | solution.py:484
  64.5 3.5 %all-to-all-done.2.near_rows = bf16[4,48,512]{2,1,0:T(8,128)(2,1)S(1)} async-done(((bf16[4,48,512]{2,1,0:T(8,128)(2,1)}), bf16[4,48,512]{2,1,0:T(8,128)(2,1)S(1)}, u32[]{:S(2)}, u32[]{:S(2)}) %all-to-all-start.2) | async-done | bytes 196640 | tf_op jit(solution)/shard_map/all_to_all | solution.py:456
  68.0 3.1 %shard_map.81 = (bf16[4,128,256]{2,1,0:T(8,128)(2,1)S(1)}, f32[4,128,256]{2,1,0:T(8,128)S(1)}, f32[16,256]{1,0:T(8,128)S(1)}, bf16[4,48,512]{2,1,0:T(8,128)(2,1)}, bf16[32,512]{1,0:T(8,128)(2,1)S(1)}) custom-call(s32[2]{0:T(128)S(1)} %pad_add_fusion.spot, bf16[8,256,256]{2,1,0:T(8,128)(2,1)S(1)} %all-to-all-done.whole, ...), custom_call_target="tpu_custom_call" | custom-call | tf_op jit(solution)/shard_map/pallas_call | solution.py:491
  71.1 3.4 %all-to-all-start.3 = ((bf16[4,48,512]{2,1,0:T(8,128)(2,1)}), bf16[4,48,512]{2,1,0:T(8,128)(2,1)S(1)}, u32[]{:S(2)}, u32[]{:S(2)}) async-start(bf16[4,48,512]{2,1,0:T(8,128)(2,1)} %get-tuple-element.43), calls=%async_computation.3 | async-start | bytes 393216 | tf_op jit(solution)/shard_map/all_to_all | solution.py:456
  74.5 1.7 %shard_map.82 = (bf16[288,512]{1,0:T(8,128)(2,1)S(1)}, bf16[512,256]{1,0:T(8,128)(2,1)}) custom-call(s32[2]{0:T(128)S(1)} %pad_add_fusion.spot, bf16[8,256,256]{2,1,0:T(8,128)(2,1)S(1)} %all-to-all-done.whole, bf16[576,256]{1,0:T(8,128)(2,1)S(1)} %collective-permute-done.low.rim, f32[16,256]{1,0:T(8,128)S(1)} %get-tuple-element.35.stats, ...), custom_call_target="tpu_custom_call" | custom-call | flops 5000000000 | tf_op jit(solution)/shard_map/pallas_call | solution.py:505
  76.1 3.2 %collective-permute-start.2 = (bf16[288,512]{1,0:T(8,128)(2,1)S(1)}, bf16[288,512]{1,0:T(8,128)(2,1)S(1)}, u32[]{:S(2)}, u32[]{:S(2)}) collective-permute-start(bf16[288,512]{1,0:T(8,128)(2,1)S(1)} %get-tuple-element.42), channel_id=1, source_target_pairs={{0,504},{8,0},{16,8},{24,16},{32,24},{40,32},{48,40},{56,48},{64,5... | collective-permute-start | bytes 884744 | tf_op jit(solution)/shard_map/ppermute | solution.py:453
  79.4 0.1 all-to-all-done.3.near
  79.5 0.8 shard_map.85
  80.4 7.3 %all-to-all-start.4 = ((bf16[16,8,512]{2,1,0:T(8,128)(2,1)}), bf16[16,8,512]{2,1,0:T(8,128)(2,1)S(1)}, u32[]{:S(2)}, u32[]{:S(2)}) async-start(bf16[16,8,512]{2,1,0:T(8,128)(2,1)} %shard_map.85), calls=%async_computation.4 | async-start | bytes 262144 | tf_op jit(solution)/shard_map/all_to_all | solution.py:456
  87.6 0.0 collective-permute-done.2.from_next.other
  87.6 1.1 shard_map.86
  88.7 2.5 %collective-permute-start.3 = (bf16[288,512]{1,0:T(8,128)(2,1)S(1)}, bf16[288,512]{1,0:T(8,128)(2,1)S(1)}, u32[]{:S(2)}, u32[]{:S(2)}) collective-permute-start(bf16[288,512]{1,0:T(8,128)(2,1)S(1)} %shard_map.86), channel_id=1, source_target_pairs={{0,8},{8,16},{16,24},{24,32},{32,40},{40,48},{48,56},{56,64},{64,7... | collective-permute-start | bytes 884744 | tf_op jit(solution)/shard_map/ppermute | solution.py:453
  91.3 3.1 %shard_map.83 = (bf16[512,256]{1,0:T(8,128)(2,1)}, bf16[512,512]{1,0:T(8,128)(2,1)S(1)}) custom-call(s32[2]{0:T(128)S(1)} %pad_add_fusion.spot, bf16[8,256,256]{2,1,0:T(8,128)(2,1)S(1)} %all-to-all-done.whole, bf16[576,256]{1,0:T(8,128)(2,1)S(1)} %collective-permute-done.low.rim, bf16[576,256]{1,0:T(8,128)(2,1)S(1)} %collective-permute-done.1.high.rim, ...), custom_call_target="tpu_custom_call" | custom-call | flops 5000000000 | tf_op jit(solution)/shard_map/pallas_call | solution.py:517
  94.3 1.1 %shard_map.84 = (f32[512,512]{1,0:T(8,128)S(1)}, bf16[512,32]{1,0:T(8,128)(2,1)S(1)}) custom-call(s32[2]{0:T(128)S(1)} %pad_add_fusion.spot, bf16[512,512]{1,0:T(8,128)(2,1)S(1)} %get-tuple-element.41.centre, bf16[288,512]{1,0:T(8,128)(2,1)S(1)} %collective-permute-done.2.from_next.other, bf16[4,48,512]{2,1,0:T(8,128)(2,1)S(1)} %all-to-all-done.3.near), custom_call_target="tpu_custom_call" | custom-call | tf_op jit(solution)/shard_map/pallas_call | solution.py:524
  95.4 10.0 %collective-permute-done.3.from_prev = bf16[288,512]{1,0:T(8,128)(2,1)S(1)} collective-permute-done((bf16[288,512]{1,0:T(8,128)(2,1)S(1)}, bf16[288,512]{1,0:T(8,128)(2,1)S(1)}, u32[]{:S(2)}, u32[]{:S(2)}) %collective-permute-start.3) | collective-permute-done | bytes 294944 | tf_op jit(solution)/shard_map/ppermute | solution.py:453
  105.4 0.0 all-to-all-done.4.far
  105.5 1.2 %shard_map.87 = (bf16[512,256]{1,0:T(8,128)(2,1)}, bf16[512,256]{1,0:T(8,128)(2,1)}) custom-call(f32[512,512]{1,0:T(8,128)S(1)} %get-tuple-element.44.total, bf16[512,128]{1,0:T(8,128)(2,1)S(1)} %get-tuple-element.45.weight, bf16[512,32]{1,0:T(8,128)(2,1)S(1)} %get-tuple-element.46.zero_weight, bf16[16,8,512]{2,1,0:T(8,128)(2,1)S(1)} %all-to-all-done.4.far, ...), custom_call_target="tpu_custom_call" | custom-call | tf_op jit(solution)/shard_map/pallas_call | solution.py:530
Async XLA Ops:
  2.7 25.5 %all-to-all-start = ((bf16[8,256,256]{2,1,0:T(8,128)(2,1)}), bf16[8,256,256]{2,1,0:T(8,128)(2,1)S(1)}, u32[]{:S(2)}, u32[]{:S(2)}) async-start(bf16[8,256,256]{2,1,0:T(8,128)(2,1)} %shard_map.75), calls=%async_computation | async-start | bytes 2097152 | tf_op jit(solution)/shard_map/all_to_all | solution.py:458
  29.0 28.9 %all-to-all-start.1 = ((bf16[16,8,512]{2,1,0:T(8,128)(2,1)}), bf16[16,8,512]{2,1,0:T(8,128)(2,1)S(1)}, u32[]{:S(2)}, u32[]{:S(2)}) async-start(bf16[16,8,512]{2,1,0:T(8,128)(2,1)} %get-tuple-element.34), calls=%async_computation.1 | async-start | bytes 262144 | tf_op jit(solution)/shard_map/all_to_all | solution.py:456
  42.3 20.6 %collective-permute-start = (bf16[576,256]{1,0:T(8,128)(2,1)S(1)}, bf16[576,256]{1,0:T(8,128)(2,1)S(1)}, u32[]{:S(2)}, u32[]{:S(2)}) collective-permute-start(bf16[576,256]{1,0:T(8,128)(2,1)S(1)} %get-tuple-element.30), channel_id=1, source_target_pairs={{0,8},{8,16},{16,24},{24,32},{32,40},{40,48},{48,56},{56,64},{64,7... | collective-permute-start | bytes 884744 | tf_op jit(solution)/shard_map/ppermute | solution.py:453
  44.9 18.0 %collective-permute-start.1 = (bf16[576,256]{1,0:T(8,128)(2,1)S(1)}, bf16[576,256]{1,0:T(8,128)(2,1)S(1)}, u32[]{:S(2)}, u32[]{:S(2)}) collective-permute-start(bf16[576,256]{1,0:T(8,128)(2,1)S(1)} %get-tuple-element.31), channel_id=1, source_target_pairs={{0,504},{8,0},{16,8},{24,16},{32,24},{40,32},{48,40},{56,48},{64,5... | collective-permute-start | bytes 884744 | tf_op jit(solution)/shard_map/ppermute | solution.py:453
  58.8 9.2 %all-to-all-start.2 = ((bf16[4,48,512]{2,1,0:T(8,128)(2,1)}), bf16[4,48,512]{2,1,0:T(8,128)(2,1)S(1)}, u32[]{:S(2)}, u32[]{:S(2)}) async-start(bf16[4,48,512]{2,1,0:T(8,128)(2,1)} %shard_map.79), calls=%async_computation.2 | async-start | bytes 393216 | tf_op jit(solution)/shard_map/all_to_all | solution.py:456
  71.1 8.4 %all-to-all-start.3 = ((bf16[4,48,512]{2,1,0:T(8,128)(2,1)}), bf16[4,48,512]{2,1,0:T(8,128)(2,1)S(1)}, u32[]{:S(2)}, u32[]{:S(2)}) async-start(bf16[4,48,512]{2,1,0:T(8,128)(2,1)} %get-tuple-element.43), calls=%async_computation.3 | async-start | bytes 393216 | tf_op jit(solution)/shard_map/all_to_all | solution.py:456
  76.1 11.5 %collective-permute-start.2 = (bf16[288,512]{1,0:T(8,128)(2,1)S(1)}, bf16[288,512]{1,0:T(8,128)(2,1)S(1)}, u32[]{:S(2)}, u32[]{:S(2)}) collective-permute-start(bf16[288,512]{1,0:T(8,128)(2,1)S(1)} %get-tuple-element.42), channel_id=1, source_target_pairs={{0,504},{8,0},{16,8},{24,16},{32,24},{40,32},{48,40},{56,48},{64,5... | collective-permute-start | bytes 884744 | tf_op jit(solution)/shard_map/ppermute | solution.py:453
  80.4 25.1 %all-to-all-start.4 = ((bf16[16,8,512]{2,1,0:T(8,128)(2,1)}), bf16[16,8,512]{2,1,0:T(8,128)(2,1)S(1)}, u32[]{:S(2)}, u32[]{:S(2)}) async-start(bf16[16,8,512]{2,1,0:T(8,128)(2,1)} %shard_map.85), calls=%async_computation.4 | async-start | bytes 262144 | tf_op jit(solution)/shard_map/all_to_all | solution.py:456
  88.7 16.8 %collective-permute-start.3 = (bf16[288,512]{1,0:T(8,128)(2,1)S(1)}, bf16[288,512]{1,0:T(8,128)(2,1)S(1)}, u32[]{:S(2)}, u32[]{:S(2)}) collective-permute-start(bf16[288,512]{1,0:T(8,128)(2,1)S(1)} %shard_map.86), channel_id=1, source_target_pairs={{0,8},{8,16},{16,24},{24,32},{32,40},{40,48},{48,56},{56,64},{64,7... | collective-permute-start | bytes 884744 | tf_op jit(solution)/shard_map/ppermute | solution.py:453
